TPU v7x, 128 devices: a whole 4x4x4 slice. The times are simulated.
128 devices in a mesh: tm: 32 (over y_lo, z, x), feat: 4 (over y_hi, core).
Axes of the slice: x: 4, y: 4 (y_hi: 2, y_lo: 2; y = y_hi * 2 + y_lo), z: 4, core: 2. Of those that a mesh axis runs over, the one named last changes fastest.
Arguments:
- coords: float32 [2048, 3, 8, 256], P('tm'), may hold values from -12 to 12, as said below
- set_a: int32 [128], replicated, may hold values from 0 to 255
- set_b: int32 [128], replicated, may hold values from 0 to 255
Outputs:
- c00: float32 [16384, 16384], P('feat', 'tm')
- c0t: float32 [16384, 16384], P('feat', 'tm')
Inputs may be any that keep to these rules, and one draw needn't show every extreme that they name: `coords`: positions of a folding protein.
All inputs are finite; a program needn't handle non-finite values.
Results may differ from a plain program's by a relative error of at most 0.0003.
Values may be sent and summed in bfloat16 or wider, within the bound.
No kernel may reach another device: no remote copies, remote signals or barrier semaphores. Data moves between devices by JAX's collectives and lax.ppermute only.
A program may use at most 128 MiB of HBM per device.

v0:
```python
import jax
import jax.numpy as jnp
from jax import lax
from jax.sharding import PartitionSpec as P

LAG = 64


contact_radius = 1.2
contact_width = 0.25


def from_behind(array, axis, by):
    length = lax.axis_size(axis)
    pairs = [(i, i + by) for i in range(length) if 0 <= i + by < length]
    return lax.ppermute(array, axis, pairs)


def contact_features(positions, index_a, index_b):
    part_a = jnp.take(positions, index_a, axis=3)
    part_b = jnp.take(positions, index_b, axis=3)
    frame_rows = positions.shape[0]
    summed = jnp.zeros((frame_rows, part_a.shape[3], part_b.shape[3]), jnp.float32)
    for first_atom in range(part_a.shape[2]):
        square = jnp.zeros(
            (frame_rows, part_b.shape[2], part_a.shape[3], part_b.shape[3]), jnp.float32
        )
        for component in range(3):
            difference = (
                part_a[:, component, first_atom, :][:, None, :, None]
                - part_b[:, component, :, :][:, :, None, :]
            )
            square = square + difference * difference
        summed = summed + jnp.sum(
            jax.nn.sigmoid((contact_radius - jnp.sqrt(square)) / contact_width), axis=1
        )
    summed = summed / float(part_a.shape[2])
    return summed.reshape(frame_rows, part_a.shape[3] * part_b.shape[3])


def contract_frames(left, right):
    return lax.dot_general(
        left, right, (((0,), (0,)), ((), ())), preferred_element_type=jnp.float32
    )


def pair_sums(frames_block, pairs):
    early = frames_block[:pairs].astype(jnp.float32)
    later = frames_block[LAG:].astype(jnp.float32)
    padding = jnp.zeros((LAG, frames_block.shape[1]), jnp.bfloat16)
    plus = jnp.concatenate([(early + later).astype(jnp.bfloat16), padding], axis=0)
    minus = jnp.concatenate([(early - later).astype(jnp.bfloat16), padding], axis=0)
    return (plus, minus)


def per_device(coords, set_a, set_b):
    feat_count = lax.axis_size("feat")
    feat_index = lax.axis_index("feat")
    rows_a = set_a.shape[0] // feat_count
    index_a = lax.dynamic_slice_in_dim(set_a, feat_index * rows_a, rows_a)
    lifted = contact_features(coords, index_a, set_b)
    frame_rows = coords.shape[0]
    time_count = lax.axis_size("tm")
    time_index = lax.axis_index("tm")
    frames_all = frame_rows * time_count
    pairs = frames_all - LAG
    frame_ids = time_index * frame_rows + jnp.arange(frame_rows, dtype=jnp.int32)
    weight = (frame_ids < pairs).astype(jnp.float32) + (frame_ids >= LAG).astype(jnp.float32)
    local_sums = jnp.dot(weight, lifted, precision=lax.Precision.HIGHEST)
    means = lax.psum(local_sums, "tm") / (2.0 * pairs)
    centered = (lifted - means[None, :]).astype(jnp.bfloat16)
    centered = lax.optimization_barrier(centered)
    every_feature = lax.all_gather(centered, "feat", axis=1, tiled=True)
    column_block = lax.all_to_all(every_feature, "tm", split_axis=1, concat_axis=0, tiled=True)
    plus_cols, minus_cols = pair_sums(column_block, pairs)
    following = from_behind(centered, "tm", -1)
    later = jnp.concatenate([centered[LAG:], following], axis=0).astype(jnp.float32)
    early = centered.astype(jnp.float32)
    valid = (frame_ids < pairs)[:, None]
    plus_rows = jnp.where(valid, early + later, 0.0).astype(jnp.bfloat16)
    minus_rows = jnp.where(valid, early - later, 0.0).astype(jnp.bfloat16)
    sum_plus = contract_frames(lax.all_gather(plus_rows, "tm", axis=0, tiled=True), plus_cols)
    sum_minus = contract_frames(lax.all_gather(minus_rows, "tm", axis=0, tiled=True), minus_cols)
    c00 = (sum_plus + sum_minus) / (4.0 * pairs)
    c0t = (sum_plus - sum_minus) / (4.0 * pairs)
    return (c00, c0t)


def solution(mesh):
    placed = (P("tm", None, None, None), P(), P())
    return jax.shard_map(
        per_device,
        mesh=mesh,
        in_specs=placed,
        out_specs=(P("feat", "tm"), P("feat", "tm")),
        check_vma=False,
    )
```

profile of v0, /device:TPU:0, one launch (start us, length us, event | category | flops | bytes accessed | tf_op | source)
XLA Modules:
  0.0 697.9 jit_solution(5199489083653316100)
XLA Ops:
  7.2 0.7 compare_and_fusion.1
  8.0 2.3 copy.95
  10.3 0.6 gather_fusion
  10.9 0.1 select_bitcast_fusion.1
  11.0 0.3 fusion.34
  11.4 1.2 compare_select_fusion
  12.5 1.1 compare_and_fusion
  13.7 0.7 copy.105
  14.4 0.7 copy.107
  15.2 0.7 copy.109
  16.0 0.7 copy.111
  16.7 0.7 copy.112
  17.3 0.7 copy.113
  18.1 0.7 copy.115
  18.9 0.7 copy.117
  19.7 0.7 copy.104
  20.3 0.7 pad_clamp_fusion
  21.0 1.9 gather_fusion.1
  22.9 1.6 select_bitcast_fusion
  24.5 0.1 slice_bitcast_fusion.2
  24.6 0.2 copy.100
  24.9 0.2 copy.102
  25.1 0.2 copy.98
  25.3 0.1 copy.118
  25.6 0.1 copy.121
  25.7 0.1 copy.122
  25.8 0.1 copy.123
  25.8 0.1 copy.101
  25.9 0.1 copy.96
  26.0 0.1 copy.99
  26.2 19.8 %fusion.7 = (f32[64,32,128]{2,1,0:T(8,128)S(1)}, f32[64,32,128]{2,1,0:T(8,128)S(1)}, f32[64,32,128]{2,1,0:T(8,128)S(1)}) fusion(f32[64,8,128]{2,1,0:T(8,128)S(1)} %copy.102, f32[64,32]{1,0:T(8,128)S(1)} %copy.101, f32[64,8,128]{2,1,0:T(8,128)S(1)} %copy.100, f32[64,32]{1,0:T(8,128)S(1)} %copy.99, f32[64,8,128]{2,1,0:T(8,128)S(1)} %copy.98, ...), kind=kLoop, calls=%fused_computation.19 | loop fusion | flops 87293952 | bytes 4005888 | tf_op jit(solution)/shard_map/reduce_sum | solution.py:34
  46.0 31.7 %fusion.6 = (f32[64,32,128]{2,1,0:T(8,128)S(1)}, f32[64,32,128]{2,1,0:T(8,128)S(1)}, f32[64,32,128]{2,1,0:T(8,128)S(1)}, f32[64,32,128]{2,1,0:T(8,128)S(1)}, f32[64,32,128]{2,1,0:T(8,128)S(1)}) fusion(f32[64,32]{1,0:T(8,128)S(1)} %copy-done, f32[64,32]{1,0:T(8,128)S(1)} %copy-done.8, f32[64,32]{1,0:T(8,128)S(1)} %copy.103, f32[64,8,128]{2,1,0:T(8,128)S(1)} %copy.102, ...), kind=kLoop, calls=%fused_computation.17 | loop fusion | flops 145489920 | bytes 6152192 | tf_op jit(solution)/shard_map/reduce_sum | solution.py:34
  77.8 1.0 add_multiply_fusion.1
  78.8 1.2 fusion.18
  80.0 159.4 %psum.7 = f32[4096]{0:T(1024)S(1)} all-reduce(f32[4096]{0:T(1024)S(1)} %bitcast.61), channel_id=1, replica_groups=mesh['tm'=32,'feat'=4] {'tm'}, use_global_device_ids=true, to_apply=%region_8.9 | all-reduce | flops 4096 | bytes 32768 | tf_op jit(solution)/shard_map/psum | solution.py:70
  239.3 1.4 fusion.20
  240.8 1.3 collective-permute-start
  242.1 10.0 %collective-permute-done = bf16[64,4096]{1,0:T(8,128)(2,1)S(1)} collective-permute-done((bf16[64,4096]{1,0:T(8,128)(2,1)}, bf16[64,4096]{1,0:T(8,128)(2,1)S(1)}, u32[]{:S(2)}, u32[]{:S(2)}) %collective-permute-start) | collective-permute-done | bytes 524320 | tf_op jit(solution)/shard_map/ppermute | solution.py:16
  252.1 2.3 fusion.17
  254.5 0.7 all-gather.4.cloned.1.call-update
  255.2 8.5 %all-gather.6.cloned.1.call-done = bf16[64,16384]{1,0:T(8,128)(2,1)} async-done(((bf16[64,4096]{1,0:T(8,128)(2,1)}), bf16[64,16384]{1,0:T(8,128)(2,1)}) %all-gather.6.cloned.1.call-update) | async-done | bytes 2097168 | tf_op jit(solution)/shard_map/all_gather | solution.py:73
  263.7 1.9 copy.133
  265.5 56.4 %all_to_all.16 = bf16[64,32,512]{2,0,1:T(8,128)(2,1)S(1)} all-to-all(bf16[64,32,512]{2,0,1:T(8,128)(2,1)S(1)} %bitcast.57), channel_id=1, replica_groups=mesh['tm'=32,'feat'=4] {'tm'}, dimensions={1} | all-to-all | bytes 4194304 | tf_op jit(solution)/shard_map/all_to_all | solution.py:74
  321.9 2.4 fusion.9
  324.3 153.6 %all-gather.8.cloned.1.call-done = bf16[2048,4096]{1,0:T(8,128)(2,1)} async-done(((bf16[64,4096]{1,0:T(8,128)(2,1)}), bf16[2048,4096]{1,0:T(8,128)(2,1)}) %all-gather.8.cloned.1.call-update) | async-done | bytes 16777232 | tf_op jit(solution)/shard_map/all_gather | solution.py:83
  477.9 15.1 %fusion.10 = f32[4096,512]{1,0:T(8,128)} fusion(bf16[2048,4096]{1,0:T(8,128)(2,1)} %all-gather.8.cloned.1.call-done, bf16[1984,512]{1,0:T(8,128)(2,1)} %bitcast.60), kind=kOutput, calls=%fused_computation.25 | convolution fusion | flops 8589934592 | bytes 27197440 | tf_op jit(solution)/shard_map/dot_general | solution.py:42
  493.0 177.1 %all-gather.4.cloned.1.call-done = bf16[2048,4096]{1,0:T(8,128)(2,1)} async-done(((bf16[64,4096]{1,0:T(8,128)(2,1)}), bf16[2048,4096]{1,0:T(8,128)(2,1)}) %all-gather.4.cloned.1.call-update) | async-done | bytes 16777232 | tf_op jit(solution)/shard_map/all_gather | solution.py:82
  670.1 21.3 %subtract_multiply_fusion = (f32[4096,512]{1,0:T(8,128)}, f32[4096,512]{1,0:T(8,128)}) fusion(f32[4096,512]{1,0:T(8,128)} %fusion.10, bf16[2048,4096]{1,0:T(8,128)(2,1)} %all-gather.4.cloned.1.call-done, bf16[1984,512]{1,0:T(8,128)(2,1)S(1)} %bitcast.59), kind=kOutput, calls=%fused_computation.2 | convolution fusion | flops 8598323200 | bytes 43974656 | tf_op jit(solution)/shard_map/dot_general | solution.py:42
  (35 shorter events, 0.9 us)
Async XLA Ops:
  7.2 256.5 %all-gather.6.cloned.1.call-start = ((), (), s32[]{:S(2)}) async-start(), calls=%async_computation.2 | async-start | bytes 2621440 | tf_op jit(solution)/shard_map/all_gather | solution.py:73
  26.1 19.9 %copy-start = (f32[64,32]{1,0:T(8,128)S(1)}, f32[64,32]{1,0:T(8,128)}, u32[]{:S(2)}) copy-start(f32[64,32]{1,0:T(8,128)} %copy.105) | copy-start | bytes 24580
  26.1 19.9 %copy-start.1 = (f32[64,32]{1,0:T(8,128)S(1)}, f32[64,32]{1,0:T(8,128)}, u32[]{:S(2)}) copy-start(f32[64,32]{1,0:T(8,128)} %copy.107) | copy-start | bytes 24580
  26.1 19.9 %copy-start.2 = (f32[64,32]{1,0:T(8,128)S(1)}, f32[64,32]{1,0:T(8,128)}, u32[]{:S(2)}) copy-start(f32[64,32]{1,0:T(8,128)} %copy.109) | copy-start | bytes 24580
  26.1 19.9 %copy-start.3 = (f32[64,32]{1,0:T(8,128)S(1)}, f32[64,32]{1,0:T(8,128)}, u32[]{:S(2)}) copy-start(f32[64,32]{1,0:T(8,128)} %copy.111) | copy-start | bytes 24580
  26.1 19.9 %copy-start.4 = (f32[64,32]{1,0:T(8,128)S(1)}, f32[64,32]{1,0:T(8,128)}, u32[]{:S(2)}) copy-start(f32[64,32]{1,0:T(8,128)} %copy.112) | copy-start | bytes 24580
  26.1 19.9 %copy-start.5 = (f32[64,32]{1,0:T(8,128)S(1)}, f32[64,32]{1,0:T(8,128)}, u32[]{:S(2)}) copy-start(f32[64,32]{1,0:T(8,128)} %copy.113) | copy-start | bytes 24580
  26.2 19.9 %copy-start.6 = (f32[64,32]{1,0:T(8,128)S(1)}, f32[64,32]{1,0:T(8,128)}, u32[]{:S(2)}) copy-start(f32[64,32]{1,0:T(8,128)} %copy.115) | copy-start | bytes 24580
  26.2 19.9 %copy-start.7 = (f32[64,32]{1,0:T(8,128)S(1)}, f32[64,32]{1,0:T(8,128)}, u32[]{:S(2)}) copy-start(f32[64,32]{1,0:T(8,128)} %copy.117) | copy-start | bytes 24580
  26.2 19.9 %copy-start.8 = (f32[64,32]{1,0:T(8,128)S(1)}, f32[64,32]{1,0:T(8,128)}, u32[]{:S(2)}) copy-start(f32[64,32]{1,0:T(8,128)} %copy.104) | copy-start | bytes 24580
  240.7 237.1 %all-gather.8.cloned.1.call-start = ((), (), s32[]{:S(2)}) async-start(), calls=%async_computation.3 | async-start | bytes 17301504 | tf_op jit(solution)/shard_map/all_gather | solution.py:83
  240.8 11.3 %collective-permute-start = (bf16[64,4096]{1,0:T(8,128)(2,1)}, bf16[64,4096]{1,0:T(8,128)(2,1)S(1)}, u32[]{:S(2)}, u32[]{:S(2)}) collective-permute-start(bf16[64,4096]{1,0:T(8,128)(2,1)} %fusion.20), channel_id=1, source_target_pairs={{4,0},{8,4},{12,8},{16,12},{20,16},{24,20},{28,24},{32,28},{36,32}... | collective-permute-start | bytes 1572872 | tf_op jit(solution)/shard_map/ppermute | solution.py:16
  254.4 415.6 %all-gather.4.cloned.1.call-start = ((), (), s32[]{:S(2)}) async-start(), calls=%async_computation.1 | async-start | bytes 17301504 | tf_op jit(solution)/shard_map/all_gather | solution.py:82
Sparse Core Ops, SparseCore 0:
  240.9 22.7 all-gather.5
  265.3 212.4 all-gather.7
  479.5 190.5 all-gather.3
where the time goes:
time: 698 us
  waiting for transfers between devices  350 us (50%)
  blocking collectives  216 us (31%)
  other arithmetic  64 us (9%)
  matrix products  37.5 us (5%)
  local copies, waits for them, and re-layouts  15.3 us (2%)
  between operations  14 us (2%)
    all_gather x1, waiting for transfers between devices, per_device(): lax.all_gather(plus_rows, 'tm', axis=0, tiled=True)  177 us
    psum x1, blocking collectives, per_device(): means = lax.psum(local_sums, 'tm') / (2.0 * pairs)  159 us
    all_gather x1, waiting for transfers between devices, per_device(): lax.all_gather(minus_rows, 'tm', axis=0, tiled=True)  154 us
    all_to_all x1, blocking collectives, per_device(): lax.all_to_all(every_feature, 'tm', split_axis=1, concat_axis=0, tiled=True)  56.4 us
    reduce_sum x2, other arithmetic, contact_features(): jnp.sum(jax.nn.sigmoid((contact_radius - jnp.sqrt(square)) / contact_widt...  51.5 us
    dot_general x2, matrix products, contract_frames(): lax.dot_general(left, right, (((0,), (0,)), ((), ())), preferred_element_...  36.4 us
  transfers between devices with their start and end apart: 4, of which 4 were waited for; matrix products, arithmetic and copies ran while one was open for 3% of the time, Pallas kernels for 0%

commit v1 on v0

v1 whole, which is shorter than its diff:
```python
import jax
import jax.numpy as jnp
from jax import lax
from jax.experimental import pallas as pl
from jax.experimental.pallas import tpu as pltpu
from jax.sharding import Mesh, PartitionSpec as P

LAG = 64
contact_radius = 1.2
contact_width = 0.25
CHUNKS = 2
TILE = 256
MIB = 1 << 20


def feature_kernel(count, first, index_ref, coords_ref, lifted_ref, sums_ref, part_a, part_b):
    frames = coords_ref.shape[1]
    atoms = coords_ref.shape[0] // 3
    index_a = jnp.broadcast_to(index_ref[0:1, :], (8, 128))
    index_b = jnp.broadcast_to(index_ref[1:2, :], (8, 128))

    def lanes(array, index):
        return jnp.take_along_axis(array, index, axis=1, mode="promise_in_bounds")

    def chosen(low, high, index):
        return jnp.where(index < 128, lanes(low, index & 127), lanes(high, index & 127))

    scale = 0.5 / contact_width
    shift = contact_radius * scale

    @pl.loop(0, frames // 8)
    def _(octet):
        rows = pl.ds(pl.multiple_of(octet * 8, 8), 8)
        for piece in range(3 * atoms):
            both = coords_ref[piece, rows, :] * scale
            low, high = both[:, :128], both[:, 128:]
            part_a[piece] = chosen(low, high, index_a)
            part_b[piece] = chosen(low, high, index_b)

        @pl.loop(0, count)
        def _(residue):
            at = jnp.full((8, 128), first + residue, jnp.int32)
            total = None
            for p in range(atoms):
                ax, ay, az = [lanes(part_a[c * atoms + p], at) for c in range(3)]
                for q in range(atoms):
                    dx = ax - part_b[q]
                    dy = ay - part_b[atoms + q]
                    dz = az - part_b[2 * atoms + q]
                    square = jnp.maximum(dx * dx + dy * dy + dz * dz, 1e-30)
                    value = jnp.tanh(shift - square * lax.rsqrt(square))
                    total = value if total is None else total + value
            features = (total + float(atoms * atoms)) * (0.5 / atoms)
            lifted_ref[rows, pl.ds(pl.multiple_of(residue * 128, 128), 128)] = features

    sums_ref[...] = jnp.sum(lifted_ref[...], axis=0, keepdims=True) * index_ref[2:3, 0:1].astype(jnp.float32)


def contact_features(count, first, indices, coords):
    pieces, frames, residues = coords.shape
    width = count * 128
    pairs = frames * width * (pieces // 3) ** 2
    return pl.pallas_call(
        lambda *refs: feature_kernel(count, first, *refs),
        out_shape=(
            jax.ShapeDtypeStruct((frames, width), jnp.float32),
            jax.ShapeDtypeStruct((1, width), jnp.float32),
        ),
        in_specs=[pl.BlockSpec(memory_space=pltpu.VMEM)] * 2,
        out_specs=[pl.BlockSpec(memory_space=pltpu.VMEM)] * 2,
        scratch_shapes=[pltpu.VMEM((pieces, 8, 128), jnp.float32)] * 2,
        compiler_params=pltpu.CompilerParams(vmem_limit_bytes=24 * MIB),
        cost_estimate=pl.CostEstimate(flops=pairs * 12, bytes_accessed=4 * MIB, transcendentals=2 * pairs),
    )(indices, coords)


def column_kernel(map_ref, cols_ref, out_ref):
    blocks, frames, width = cols_ref.shape

    @pl.loop(0, blocks)
    def _(block):
        here = cols_ref[map_ref[block]].astype(jnp.float32)
        before = cols_ref[map_ref[jnp.maximum(block - 1, 0)]].astype(jnp.float32)
        after = cols_ref[map_ref[jnp.minimum(block + 1, blocks - 1)]].astype(jnp.float32)
        inner = jnp.logical_and(block > 0, block < blocks - 1)
        out_ref[block, :, :width] = jnp.where(inner, 2.0 * here, here).astype(jnp.bfloat16)
        lagged = jnp.where(block > 0, before, 0.0) + jnp.where(block < blocks - 1, after, 0.0)
        out_ref[block, :, width:] = lagged.astype(jnp.bfloat16)


def lagged_columns(block_map, cols):
    blocks, frames, width = cols.shape
    return pl.pallas_call(
        column_kernel,
        out_shape=jax.ShapeDtypeStruct((blocks, frames, 2 * width), jnp.bfloat16),
        in_specs=[pl.BlockSpec(memory_space=pltpu.SMEM), pl.BlockSpec(memory_space=pltpu.VMEM)],
        out_specs=pl.BlockSpec(memory_space=pltpu.VMEM),
        compiler_params=pltpu.CompilerParams(vmem_limit_bytes=24 * MIB),
        cost_estimate=pl.CostEstimate(flops=8 * cols.size, bytes_accessed=6 * cols.size, transcendentals=0),
    )(block_map, cols)


def product_kernel(sizes, factor, aliased, map_ref, *refs):
    pieces = refs[: len(sizes)]
    columns_ref = refs[len(sizes)]
    c00_ref, c0t_ref, gathered = refs[len(sizes) + 1 + aliased :]
    frames = columns_ref.shape[1]
    width = c00_ref.shape[1]
    place = 0
    for size, piece in zip(sizes, pieces):
        for shard in range(size):
            start = pl.multiple_of(map_ref[place] * frames, frames)
            gathered[pl.ds(start, frames), :] = piece[shard]
            place += 1
    columns = columns_ref[...].reshape(gathered.shape[0], 2 * width)
    sums = lax.dot_general(
        gathered[...], columns, (((0,), (0,)), ((), ())), preferred_element_type=jnp.float32
    )
    c00_ref[...] = sums[:, :width] * factor
    c0t_ref[...] = sums[:, width:] * factor


def products(block_map, pieces, columns, row_start, rows, factor, previous):
    blocks, frames, double = columns.shape
    width = double // 2
    features = pieces[0].shape[2]
    sizes = [piece.shape[0] for piece in pieces]
    first = row_start // TILE
    out = jax.ShapeDtypeStruct((rows, width), jnp.float32)
    count = len(sizes)
    passed = () if previous is None else previous
    in_specs = [pl.BlockSpec(memory_space=pltpu.SMEM)]
    in_specs += [pl.BlockSpec((size, frames, TILE), lambda i: (0, 0, i)) for size in sizes]
    in_specs += [pl.BlockSpec((blocks, frames, double), lambda i: (0, 0, 0))]
    in_specs += [pl.BlockSpec(memory_space=pl.ANY)] * len(passed)
    return pl.pallas_call(
        lambda *refs: product_kernel(sizes, factor, len(passed), *refs),
        grid=(features // TILE,),
        out_shape=(out, out),
        in_specs=in_specs,
        out_specs=[pl.BlockSpec((TILE, width), lambda i: (first + i, 0))] * 2,
        scratch_shapes=[pltpu.VMEM((blocks * frames, TILE), jnp.bfloat16)],
        input_output_aliases={count + 2 + n: n for n in range(len(passed))},
        compiler_params=pltpu.CompilerParams(vmem_limit_bytes=40 * MIB),
        cost_estimate=pl.CostEstimate(
            flops=2 * features * blocks * frames * double,
            bytes_accessed=features * blocks * frames * 2 + features * double * 4 + columns.size * 2,
            transcendentals=0,
        ),
    )(block_map, *pieces, columns, *passed)


def moved(array, axis, by):
    length = lax.axis_size(axis)
    return lax.ppermute(array, axis, [(i, (i + by) % length) for i in range(length)])


def summed(array):
    for axis, flip in (("x", 1), ("x", 2), ("z", 1), ("z", 2), ("yl", 1)):
        length = lax.axis_size(axis)
        array = array + lax.ppermute(array, axis, [(i, i ^ flip) for i in range(length)])
    return array


def around(block, axis):
    half = block.shape[0] // 2
    behind = moved(block, axis, 1)
    ahead = moved(block, axis, -1)
    far_first = moved(behind[:half], axis, 1)
    far_last = moved(ahead[half:], axis, -1)
    return (block, behind, ahead, far_first, far_last)


def gathered_rows(block, first, second):
    plane = jnp.concatenate(around(block, first), axis=0)
    return around(plane, second)


def row_order(first, second, outer_is_z, place):
    partner = [place["yl"], 1 - place["yl"]]
    line = []
    for offset in (0, -1, 1):
        line += [((place[first] + offset) % 4, y) for y in partner]
    line += [((place[first] + 2) % 4, y) for y in partner]
    whole = []
    half = len(line) // 2
    for offset in (0, -1, 1):
        whole += [((place[second] + offset) % 4, one, y) for one, y in line]
    whole += [((place[second] + 2) % 4, one, y) for one, y in line]
    order = []
    for two, one, y in whole:
        z, x = (two, one) if outer_is_z else (one, two)
        order.append(y * 16 + z * 4 + x)
    return jnp.stack(order).astype(jnp.int32)


def own_columns(centered, place):
    frames, features = centered.shape
    width = features // 8
    by_owner = jnp.transpose(centered.reshape(frames, 2, 4, width), (2, 1, 0, 3))
    along_x = [lax.dynamic_index_in_dim(by_owner, place["x"], 0, keepdims=False)]
    for by in (1, 2, 3):
        piece = lax.dynamic_index_in_dim(by_owner, (place["x"] + by) % 4, 0, keepdims=False)
        along_x.append(moved(piece, "x", by))
    along_x = jnp.stack(along_x)
    along_z = [lax.dynamic_index_in_dim(along_x, place["z"] % 2, 1, keepdims=False)]
    for by in (1, 2, 3):
        piece = lax.dynamic_index_in_dim(along_x, (place["z"] + by) % 2, 1, keepdims=False)
        pairs = []
        for z in range(4):
            target = (z + by) % 4
            core = target // 2
            pairs.append((z * 2 + core, target * 2 + core))
        along_z.append(lax.ppermute(piece, ("z", "c"), pairs))
    along_z = jnp.stack(along_z)

    def along_y(moves):
        pairs = []
        for z in range(4):
            for source, target in moves:
                flat = lambda y: (((y % 2) * 4 + z) * 2 + y // 2) * 2 + z // 2
                pairs.append((flat(source), flat(target)))
        return lax.ppermute(along_z, ("yl", "z", "yh", "c"), pairs)

    one = along_y([(0, 2), (1, 0), (2, 3), (3, 1)])
    two = along_y([(1, 2), (2, 1)])
    two = jnp.where(place["yl"] == place["yh"], along_z, two)
    both = jnp.stack([one, two])
    pairs = [(z * 2 + z // 2, z * 2 + 1 - z // 2) for z in range(4)]
    passed = lax.ppermute(both, ("z", "c"), pairs)
    both = jnp.where(place["z"] // 2 == place["c"], both, passed)
    order = []
    for block in range(32):
        y, z, x = block // 16, (block // 4) % 4, block % 4
        group = jnp.where(y == 1 - place["yh"], 0, 1)
        order.append(group * 16 + ((place["z"] - z) % 4) * 4 + (place["x"] - x) % 4)
    return both.reshape(32, frames, width), jnp.stack(order).astype(jnp.int32)


def per_device(coords, set_a, set_b):
    place = {axis: lax.axis_index(axis) for axis in ("yl", "z", "x", "yh", "c")}
    frames, _, atoms, residues = coords.shape
    feat_index = place["yh"] * 2 + place["c"]
    time_index = place["yl"] * 16 + place["z"] * 4 + place["x"]
    rows_a = set_a.shape[0] // 4
    pairs = frames * 32 - LAG
    edge = jnp.logical_or(time_index == 0, time_index == 31)
    index_a = lax.dynamic_slice_in_dim(set_a, feat_index * rows_a, rows_a)
    index_a = jnp.concatenate([index_a, jnp.zeros((128 - rows_a,), jnp.int32)])
    weight = jnp.broadcast_to(jnp.where(edge, 1, 2).astype(jnp.int32), (128,))
    indices = jnp.stack([index_a, set_b, weight, *([weight] * 5)])
    atoms_first = jnp.transpose(coords, (1, 2, 0, 3)).reshape(3 * atoms, frames, residues)

    count = rows_a // CHUNKS
    features = count * 128
    chunks = []
    for chunk in range(CHUNKS):
        lifted, sums = contact_features(count, chunk * count, indices, atoms_first)
        means = summed(sums) / (2.0 * pairs)
        chunks.append((lifted - means).astype(jnp.bfloat16))

    cols, col_order = own_columns(jnp.concatenate(chunks, axis=1), place)
    columns = lagged_columns(col_order, cols)

    rows = rows_a * 128
    results = None
    half = features // 2
    for chunk in range(CHUNKS):
        partner = moved(chunks[chunk], "yl", 1)
        block = jnp.stack([chunks[chunk], partner])
        for part, (first, second) in enumerate((("x", "z"), ("z", "x"))):
            pieces = gathered_rows(block[:, :, part * half : (part + 1) * half], first, second)
            order = row_order(first, second, second == "z", place)
            start = chunk * features + part * half
            results = products(order, pieces, columns, start, rows, 1.0 / (2.0 * pairs), results)
    return results


def solution(mesh):
    fine = Mesh(mesh.devices.reshape(2, 4, 4, 2, 2), ("yl", "z", "x", "yh", "c"))
    time_axes, feat_axes = ("yl", "z", "x"), ("yh", "c")
    return jax.shard_map(
        per_device,
        mesh=fine,
        in_specs=(P(time_axes, None, None, None), P(), P()),
        out_specs=(P(feat_axes, time_axes), P(feat_axes, time_axes)),
        check_vma=False,
    )
```

time: 698 us -> 258 us (0.37)
  waiting for transfers between devices: 350 us -> 41.3 us
  blocking collectives: 216 us -> 0 us
  starting transfers between devices: 1.41 us -> 91.8 us
  Pallas kernels: 0 us -> 89.6 us
  other arithmetic: 64 us -> 5.24 us
  matrix products: 37.5 us -> 0 us
  local copies, waits for them, and re-layouts: 15.3 us -> 28.2 us
  between operations: 14 us -> 1.24 us
    all_gather x3 -> x0, waiting for transfers between devices: 339 us -> none  [the longest x1 177 us: per_device(): lax.all_gather(plus_rows, 'tm', axis=0, tiled=True)]
    psum x1 -> x0, blocking collectives: 159 us -> none  [per_device(): means = lax.psum(local_sums, 'tm') / (2.0 * pairs)]
    ppermute x1 -> x53, starting transfers between devices: 1.29 us -> 91.8 us  [the longest x37 55.3 us: moved(): lax.ppermute(array, axis, [(i, (i + by) % length) for i in range(length)])]
    pallas_call x0 -> x7, Pallas kernels: none -> 89.6 us  [the longest x2 57.3 us: contact_features(): pl.pallas_call(lambda *refs: feature_kernel(count, first, *refs), out_sha...]
    all_to_all x1 -> x0, blocking collectives: 56.4 us -> none  [per_device(): lax.all_to_all(every_feature, 'tm', split_axis=1, concat_axis=0, tiled=True)]
    reduce_sum x2 -> x0, other arithmetic: 51.5 us -> none  [contact_features(): jnp.sum(jax.nn.sigmoid((contact_radius - jnp.sqrt(square)) / contact_widt...]
    dot_general x3 -> x0, matrix products: 37.5 us -> none  [the longest x2 36.4 us: contract_frames(): lax.dot_general(left, right, (((0,), (0,)), ((), ())), preferred_element_...]
    ppermute x1 -> x53, waiting for transfers between devices: 9.97 us -> 41.3 us  [the longest x37 33.4 us: moved(): lax.ppermute(array, axis, [(i, (i + by) % length) for i in range(length)])]
  transfers between devices with their start and end apart: 4 -> 53, of which waited for: 4 -> 13; matrix products, arithmetic and copies ran while one was open for 3% -> 11% of each run, Pallas kernels for 0% -> 21%
where the time goes in v1:
time: 258 us; the launch traced here: 257 us
  starting transfers between devices  91.8 us (36%)
  Pallas kernels  89.6 us (35%)
  waiting for transfers between devices  41.3 us (16%)
  local copies, waits for them, and re-layouts  28.2 us (11%)
  other arithmetic  5.24 us (2%)
    pallas_call x2, Pallas kernels, contact_features(): pl.pallas_call(lambda *refs: feature_kernel(count, first, *refs), out_sha...  57.3 us
    ppermute x37, starting transfers between devices, moved(): lax.ppermute(array, axis, [(i, (i + by) % length) for i in range(length)])  55.3 us
    ppermute x37, waiting for transfers between devices, moved(): lax.ppermute(array, axis, [(i, (i + by) % length) for i in range(length)])  33.4 us
    pallas_call x4, Pallas kernels, products(): pl.pallas_call(lambda *refs: product_kernel(sizes, factor, len(passed), *...  30.3 us
    ppermute x10, starting transfers between devices, summed(): lax.ppermute(array, axis, [(i, i ^ flip) for i in range(length)])  21.1 us
    unnamed x44, local copies, waits for them, and re-layouts  11.9 us
    ppermute x2, starting transfers between devices, along_y(): return lax.ppermute(along_z, ('yl', 'z', 'yh', 'c'), pairs)  7.62 us
    slice x8, local copies, waits for them, and re-layouts, around(): far_last = moved(ahead[half:], axis, -1)  5.93 us
  transfers between devices with their start and end apart: 53, of which 13 were waited for; matrix products, arithmetic and copies ran while one was open for 11% of the time, Pallas kernels for 21%

profile of v1, /device:TPU:0, one launch (start us, length us, event | category | flops | bytes accessed | tf_op | source)
XLA Modules:
  0.0 257.4 jit_solution(15822986716319044183)
XLA Ops:
  1.4 1.9 copy.15
  3.4 28.7 %shard_map.50 = (f32[64,2048]{1,0:T(8,128)S(1)}, f32[1,2048]{1,0:T(1,128)S(1)}) custom-call(s32[8,128]{1,0:T(8,128)S(1)} %stack.398.refs_0_, f32[24,64,256]{2,1,0:T(8,128)S(1)} %bitcast.112), custom_call_target="tpu_custom_call" | custom-call | flops 100663296 | bytes 4194304 | tf_op jit(solution)/shard_map/pallas_call | solution.py:63
  32.1 1.6 collective-permute-start
  33.7 28.6 %shard_map.51 = (f32[64,2048]{1,0:T(8,128)S(1)}, f32[1,2048]{1,0:T(1,128)S(1)}) custom-call(s32[8,128]{1,0:T(8,128)S(1)} %stack.398.refs_0_, f32[24,64,256]{2,1,0:T(8,128)S(1)} %bitcast.113), custom_call_target="tpu_custom_call" | custom-call | flops 100663296 | bytes 4194304 | tf_op jit(solution)/shard_map/pallas_call | solution.py:63
  62.9 3.2 %collective-permute-start.1 = (f32[1,2048]{1,0:T(1,128)S(1)}, f32[1,2048]{1,0:T(1,128)S(1)}, u32[]{:S(2)}, u32[]{:S(2)}) collective-permute-start(f32[1,2048]{1,0:T(1,128)S(1)} %add.1023), channel_id=1, source_target_pairs={{0,8},{4,12},{8,0},{12,4},{1,9},{5,13},{9,1},{13,5},{2,10},{6,14},... | collective-permute-start | bytes 24584 | tf_op jit(solution)/shard_map/ppermute | solution.py:161
  66.1 2.8 %collective-permute-start.15 = (f32[1,2048]{1,0:T(1,128)S(1)}, f32[1,2048]{1,0:T(1,128)S(1)}, u32[]{:S(2)}, u32[]{:S(2)}) collective-permute-start(f32[1,2048]{1,0:T(1,128)S(1)} %add.1072), channel_id=1, source_target_pairs={{0,8},{4,12},{8,0},{12,4},{1,9},{5,13},{9,1},{13,5},{2,10},{6,14},... | collective-permute-start | bytes 24584 | tf_op jit(solution)/shard_map/ppermute | solution.py:161
  68.9 2.0 collective-permute-start.2
  71.3 2.0 collective-permute-start.16
  73.4 3.7 %collective-permute-start.3 = (f32[1,2048]{1,0:T(1,128)S(1)}, f32[1,2048]{1,0:T(1,128)S(1)}, u32[]{:S(2)}, u32[]{:S(2)}) collective-permute-start(f32[1,2048]{1,0:T(1,128)S(1)} %add.1025), channel_id=1, source_target_pairs={{0,32},{16,48},{32,0},{48,16},{1,33},{17,49},{33,1},{49,17},{2,34}... | collective-permute-start | bytes 24584 | tf_op jit(solution)/shard_map/ppermute | solution.py:161
  77.0 2.0 collective-permute-start.17
  79.1 1.7 collective-permute-start.4
  82.3 1.7 collective-permute-start.18
  84.0 2.1 collective-permute-done.18
  88.4 3.0 %collective-permute-start.20 = (bf16[2,64,512]{2,1,0:T(8,128)(2,1)S(1)}, bf16[2,64,512]{2,1,0:T(8,128)(2,1)S(1)}, u32[]{:S(2)}, u32[]{:S(2)}) collective-permute-start(bf16[2,64,512]{2,1,0:T(8,128)(2,1)S(1)} %bitcast.129), channel_id=1, source_target_pairs={{0,8},{4,12},{8,0},{12,4},{1,9},{5,13},{9,1},{13,5},{2,10},{6,14},... | collective-permute-start | bytes 393224 | tf_op jit(solution)/shard_map/ppermute | solution.py:155
  91.5 1.9 collective-permute-start.21
  93.4 1.6 collective-permute-start.36
  96.7 2.5 collective-permute-start.22
  104.3 1.7 collective-permute-start.46
  106.0 3.8 %collective-permute-done.22 = bf16[4,64,512]{2,1,0:T(8,128)(2,1)S(1)} collective-permute-done((bf16[4,64,512]{2,1,0:T(8,128)(2,1)S(1)}, bf16[4,64,512]{2,1,0:T(8,128)(2,1)S(1)}, u32[]{:S(2)}, u32[]{:S(2)}) %collective-permute-start.22) | collective-permute-done | bytes 262176 | tf_op jit(solution)/shard_map/ppermute | solution.py:214
  110.8 3.2 %collective-permute-start.38 = (bf16[2,64,1024]{2,1,0:T(8,128)(2,1)}, bf16[2,64,1024]{2,1,0:T(8,128)(2,1)}, u32[]{:S(2)}, u32[]{:S(2)}) collective-permute-start(bf16[2,64,1024]{2,1,0:T(8,128)(2,1)} %get-tuple-element.31), channel_id=1, source_target_pairs={{0,48},{16,0},{32,16},{48,32},{1,49},{17,1},{33,17},{49,33},{2,50}... | collective-permute-start | bytes 786440 | tf_op jit(solution)/shard_map/ppermute | solution.py:155
  114.0 3.4 %collective-permute-start.28 = (bf16[2,64,1024]{2,1,0:T(8,128)(2,1)}, bf16[2,64,1024]{2,1,0:T(8,128)(2,1)S(1)}, u32[]{:S(2)}, u32[]{:S(2)}) collective-permute-start(bf16[2,64,1024]{2,1,0:T(8,128)(2,1)} %get-tuple-element.27), channel_id=1, source_target_pairs={{0,4},{4,8},{8,12},{12,0},{1,5},{5,9},{9,13},{13,1},{2,6},{6,10},{... | collective-permute-start | bytes 786440 | tf_op jit(solution)/shard_map/ppermute | solution.py:155
  120.7 1.7 constant_dynamic-update-slice_fusion.18
  122.3 3.2 %collective-permute-start.7 = (bf16[2,64,1024]{2,1,0:T(8,128)(2,1)}, bf16[2,64,1024]{2,1,0:T(8,128)(2,1)S(1)}, u32[]{:S(2)}, u32[]{:S(2)}) collective-permute-start(bf16[2,64,1024]{2,1,0:T(8,128)(2,1)} %get-tuple-element.33), channel_id=1, source_target_pairs={{0,48},{16,0},{32,16},{48,32},{1,49},{17,1},{33,17},{49,33},{2,50}... | collective-permute-start | bytes 786440 | tf_op jit(solution)/shard_map/ppermute | solution.py:155
  125.6 6.9 %collective-permute-start.25 = (bf16[4,4,64,512]{3,2,1,0:T(8,128)(2,1)}, bf16[4,4,64,512]{3,2,1,0:T(8,128)(2,1)S(1)}, u32[]{:S(2)}, u32[]{:S(2)}) collective-permute-start(bf16[4,4,64,512]{3,2,1,0:T(8,128)(2,1)} %pad_maximum_fusion.1), channel_id=1, source_target_pairs={{0,2},{64,0},{2,66},{66,64},{16,18},{80,16},{18,82},{82,80},{33,35... | collective-permute-start | bytes 3145736 | tf_op jit(solution)/shard_map/ppermute | solution.py:223
  132.5 1.7 constant_dynamic-update-slice_fusion.17
  136.3 1.7 constant_dynamic-update-slice_fusion.13
  138.9 2.2 collective-permute-start.48
  141.1 1.7 constant_dynamic-update-slice_fusion.12
  145.6 3.3 %collective-permute-start.40 = (bf16[1,64,1024]{2,1,0:T(8,128)(2,1)S(1)}, bf16[1,64,1024]{2,1,0:T(8,128)(2,1)S(1)}, u32[]{:S(2)}, u32[]{:S(2)}) collective-permute-start(bf16[1,64,1024]{2,1,0:T(8,128)(2,1)S(1)} %slice.93), channel_id=1, source_target_pairs={{0,48},{16,0},{32,16},{48,32},{1,49},{17,1},{33,17},{49,33},{2,50}... | collective-permute-start | bytes 393224 | tf_op jit(solution)/shard_map/ppermute | solution.py:155
  150.2 3.0 %collective-permute-done.39 = bf16[1,64,1024]{2,1,0:T(8,128)(2,1)S(1)} collective-permute-done((bf16[1,64,1024]{2,1,0:T(8,128)(2,1)S(1)}, bf16[1,64,1024]{2,1,0:T(8,128)(2,1)S(1)}, u32[]{:S(2)}, u32[]{:S(2)}) %collective-permute-start.39) | collective-permute-done | bytes 131104 | tf_op jit(solution)/shard_map/ppermute | solution.py:155
  155.5 1.7 collective-permute-done.30
  157.2 3.2 %collective-permute-start.50 = (bf16[8,64,1024]{2,1,0:T(8,128)(2,1)}, bf16[8,64,1024]{2,1,0:T(8,128)(2,1)S(1)}, u32[]{:S(2)}, u32[]{:S(2)}) collective-permute-start(bf16[8,64,1024]{2,1,0:T(8,128)(2,1)} %constant_dynamic-update-slice_fusion.15.refs_1_), channel_id=1, source_target_pairs={{0,48},{16,0},{32,16},{48,32},{1,49},{17,1},{33,17},{49,33},{2,50}... | collective-permute-start | bytes 3145736 | tf_op jit(solution)/shard_map/ppermute | solution.py:155
  162.1 2.2 collective-permute-start.42
  165.8 8.6 %collective-permute-done.9 = bf16[1,64,1024]{2,1,0:T(8,128)(2,1)S(1)} collective-permute-done((bf16[1,64,1024]{2,1,0:T(8,128)(2,1)S(1)}, bf16[1,64,1024]{2,1,0:T(8,128)(2,1)S(1)}, u32[]{:S(2)}, u32[]{:S(2)}) %collective-permute-start.9) | collective-permute-done | bytes 131104 | tf_op jit(solution)/shard_map/ppermute | solution.py:155
  174.4 2.6 %collective-permute-start.27 = (bf16[2,4,4,64,512]{4,3,2,1,0:T(8,128)(2,1)}, bf16[2,4,4,64,512]{4,3,2,1,0:T(8,128)(2,1)}, u32[]{:S(2)}, u32[]{:S(2)}) collective-permute-start(bf16[2,4,4,64,512]{4,3,2,1,0:T(8,128)(2,1)} %pad_maximum_fusion), channel_id=1, source_target_pairs={{0,1},{16,17},{33,32},{49,48},{2,3},{18,19},{35,34},{51,50},{4,5},... | collective-permute-start | bytes 6291464 | tf_op jit(solution)/shard_map/ppermute | solution.py:230
  179.8 2.6 collective-permute-start.33
  183.7 3.2 %collective-permute-start.11 = (bf16[8,64,1024]{2,1,0:T(8,128)(2,1)}, bf16[8,64,1024]{2,1,0:T(8,128)(2,1)}, u32[]{:S(2)}, u32[]{:S(2)}) collective-permute-start(bf16[8,64,1024]{2,1,0:T(8,128)(2,1)} %constant_dynamic-update-slice_fusion.refs_1_), channel_id=1, source_target_pairs={{0,12},{4,0},{8,4},{12,8},{1,13},{5,1},{9,5},{13,9},{2,14},{6,2},{... | collective-permute-start | bytes 3145736 | tf_op jit(solution)/shard_map/ppermute | solution.py:155
  189.6 15.9 %collective-permute-done.32.refs_2_ = bf16[8,64,1024]{2,1,0:T(8,128)(2,1)S(1)} collective-permute-done((bf16[8,64,1024]{2,1,0:T(8,128)(2,1)S(1)}, bf16[8,64,1024]{2,1,0:T(8,128)(2,1)S(1)}, u32[]{:S(2)}, u32[]{:S(2)}) %collective-permute-start.32) | collective-permute-done | bytes 1048608 | tf_op jit(solution)/shard_map/ppermute | solution.py:155
  205.6 3.5 %collective-permute-start.52 = (bf16[4,64,1024]{2,1,0:T(8,128)(2,1)}, bf16[4,64,1024]{2,1,0:T(8,128)(2,1)}, u32[]{:S(2)}, u32[]{:S(2)}) collective-permute-start(bf16[4,64,1024]{2,1,0:T(8,128)(2,1)} %slice.99), channel_id=1, source_target_pairs={{0,48},{16,0},{32,16},{48,32},{1,49},{17,1},{33,17},{49,33},{2,50}... | collective-permute-start | bytes 1572872 | tf_op jit(solution)/shard_map/ppermute | solution.py:155
  212.0 3.3 %collective-permute-start.44 = (bf16[4,64,1024]{2,1,0:T(8,128)(2,1)S(1)}, bf16[4,64,1024]{2,1,0:T(8,128)(2,1)S(1)}, u32[]{:S(2)}, u32[]{:S(2)}) collective-permute-start(bf16[4,64,1024]{2,1,0:T(8,128)(2,1)S(1)} %slice.95), channel_id=1, source_target_pairs={{0,12},{4,0},{8,4},{12,8},{1,13},{5,1},{9,5},{13,9},{2,14},{6,2},{... | collective-permute-start | bytes 1572872 | tf_op jit(solution)/shard_map/ppermute | solution.py:155
  216.8 2.0 shard_map.52.refs_6_
  218.8 2.9 %collective-permute-done.51.refs_4_ = bf16[4,64,1024]{2,1,0:T(8,128)(2,1)} collective-permute-done((bf16[4,64,1024]{2,1,0:T(8,128)(2,1)}, bf16[4,64,1024]{2,1,0:T(8,128)(2,1)}, u32[]{:S(2)}, u32[]{:S(2)}) %collective-permute-start.51) | collective-permute-done | bytes 524320 | tf_op jit(solution)/shard_map/ppermute | solution.py:155
  221.7 2.0 collective-permute-start.35
  223.7 7.5 %shard_map.53 = (f32[4096,512]{1,0:T(8,128)}, f32[4096,512]{1,0:T(8,128)}) custom-call(s32[32]{0:T(128)S(1)} %stack.447.refs_0_, bf16[8,64,1024]{2,1,0:T(8,128)(2,1)} %constant_dynamic-update-slice_fusion.15.refs_1_, bf16[8,64,1024]{2,1,0:T(8,128)(2,1)S(1)} %copy-done.6, bf16[8,64,1024]{2,1,0:T(8,128)(2,1)S(1)} %copy-done.8, ...), custom_call_target="tpu_custom_call" | custom-call | flops 4294967296 | bytes 12582912 | tf_op jit(solution)/shard_map/pallas_call | solution.py:136
  231.2 3.4 %collective-permute-start.13 = (bf16[4,64,1024]{2,1,0:T(8,128)(2,1)S(1)}, bf16[4,64,1024]{2,1,0:T(8,128)(2,1)S(1)}, u32[]{:S(2)}, u32[]{:S(2)}) collective-permute-start(bf16[4,64,1024]{2,1,0:T(8,128)(2,1)S(1)} %slice.85), channel_id=1, source_target_pairs={{0,12},{4,0},{8,4},{12,8},{1,13},{5,1},{9,5},{13,9},{2,14},{6,2},{... | collective-permute-start | bytes 1572872 | tf_op jit(solution)/shard_map/ppermute | solution.py:155
  234.6 7.6 %shard_map.54 = (f32[4096,512]{1,0:T(8,128)}, f32[4096,512]{1,0:T(8,128)}) custom-call(s32[32]{0:T(128)S(1)} %stack.395.refs_0_, bf16[8,64,1024]{2,1,0:T(8,128)(2,1)} %constant_dynamic-update-slice_fusion.10.refs_1_, bf16[8,64,1024]{2,1,0:T(8,128)(2,1)S(1)} %collective-permute-done.41.refs_2_, ...), custom_call_target="tpu_custom_call", output_to_operand_aliasing={{0}: (7, {}), {1}: (8, {})} | custom-call | flops 4294967296 | bytes 12582912 | tf_op jit(solution)/shard_map/pallas_call | solution.py:136
  242.2 7.7 %shard_map.55 = (f32[4096,512]{1,0:T(8,128)}, f32[4096,512]{1,0:T(8,128)}) custom-call(s32[32]{0:T(128)S(1)} %stack.447.refs_0_, bf16[8,64,1024]{2,1,0:T(8,128)(2,1)S(1)} %copy-done.4, bf16[8,64,1024]{2,1,0:T(8,128)(2,1)S(1)} %collective-permute-done.32.refs_2_, ...), custom_call_target="tpu_custom_call", output_to_operand_aliasing={{0}: (7, {}), {1}: (8, {})} | custom-call | flops 4294967296 | bytes 12582912 | tf_op jit(solution)/shard_map/pallas_call | solution.py:136
  249.9 7.6 %shard_map.56 = (f32[4096,512]{1,0:T(8,128)}, f32[4096,512]{1,0:T(8,128)}) custom-call(s32[32]{0:T(128)S(1)} %stack.395.refs_0_, bf16[8,64,1024]{2,1,0:T(8,128)(2,1)S(1)} %copy-done.1, bf16[8,64,1024]{2,1,0:T(8,128)(2,1)} %collective-permute-done.10.refs_2_, ...), custom_call_target="tpu_custom_call", output_to_operand_aliasing={{0}: (7, {}), {1}: (8, {})} | custom-call | flops 4294967296 | bytes 12582912 | tf_op jit(solution)/shard_map/pallas_call | solution.py:136
  (159 shorter events, 40.6 us)
Async XLA Ops:
  32.1 30.8 %collective-permute-start = (f32[1,2048]{1,0:T(1,128)S(1)}, f32[1,2048]{1,0:T(1,128)S(1)}, u32[]{:S(2)}, u32[]{:S(2)}) collective-permute-start(f32[1,2048]{1,0:T(1,128)S(1)} %get-tuple-element.13), channel_id=1, source_target_pairs={{0,4},{4,0},{8,12},{12,8},{1,5},{5,1},{9,13},{13,9},{2,6},{6,2},{1... | collective-permute-start | bytes 24584 | tf_op jit(solution)/shard_map/ppermute | solution.py:161
  62.9 6.0 %collective-permute-start.1 = (f32[1,2048]{1,0:T(1,128)S(1)}, f32[1,2048]{1,0:T(1,128)S(1)}, u32[]{:S(2)}, u32[]{:S(2)}) collective-permute-start(f32[1,2048]{1,0:T(1,128)S(1)} %add.1023), channel_id=1, source_target_pairs={{0,8},{4,12},{8,0},{12,4},{1,9},{5,13},{9,1},{13,5},{2,10},{6,14},... | collective-permute-start | bytes 24584 | tf_op jit(solution)/shard_map/ppermute | solution.py:161
  66.1 5.2 %collective-permute-start.15 = (f32[1,2048]{1,0:T(1,128)S(1)}, f32[1,2048]{1,0:T(1,128)S(1)}, u32[]{:S(2)}, u32[]{:S(2)}) collective-permute-start(f32[1,2048]{1,0:T(1,128)S(1)} %add.1072), channel_id=1, source_target_pairs={{0,8},{4,12},{8,0},{12,4},{1,9},{5,13},{9,1},{13,5},{2,10},{6,14},... | collective-permute-start | bytes 24584 | tf_op jit(solution)/shard_map/ppermute | solution.py:161
  71.3 5.7 %collective-permute-start.16 = (f32[1,2048]{1,0:T(1,128)S(1)}, f32[1,2048]{1,0:T(1,128)S(1)}, u32[]{:S(2)}, u32[]{:S(2)}) collective-permute-start(f32[1,2048]{1,0:T(1,128)S(1)} %add.1073), channel_id=1, source_target_pairs={{0,16},{16,0},{32,48},{48,32},{1,17},{17,1},{33,49},{49,33},{2,18}... | collective-permute-start | bytes 24584 | tf_op jit(solution)/shard_map/ppermute | solution.py:161
  73.4 5.7 %collective-permute-start.3 = (f32[1,2048]{1,0:T(1,128)S(1)}, f32[1,2048]{1,0:T(1,128)S(1)}, u32[]{:S(2)}, u32[]{:S(2)}) collective-permute-start(f32[1,2048]{1,0:T(1,128)S(1)} %add.1025), channel_id=1, source_target_pairs={{0,32},{16,48},{32,0},{48,16},{1,33},{17,49},{33,1},{49,17},{2,34}... | collective-permute-start | bytes 24584 | tf_op jit(solution)/shard_map/ppermute | solution.py:161
  77.0 5.2 %collective-permute-start.17 = (f32[1,2048]{1,0:T(1,128)S(1)}, f32[1,2048]{1,0:T(1,128)S(1)}, u32[]{:S(2)}, u32[]{:S(2)}) collective-permute-start(f32[1,2048]{1,0:T(1,128)S(1)} %add.1074), channel_id=1, source_target_pairs={{0,32},{16,48},{32,0},{48,16},{1,33},{17,49},{33,1},{49,17},{2,34}... | collective-permute-start | bytes 24584 | tf_op jit(solution)/shard_map/ppermute | solution.py:161
  87.7 7.7 %collective-permute-start.19 = (bf16[2,64,512]{2,1,0:T(8,128)(2,1)S(1)}, bf16[2,64,512]{2,1,0:T(8,128)(2,1)S(1)}, u32[]{:S(2)}, u32[]{:S(2)}) collective-permute-start(bf16[2,64,512]{2,1,0:T(8,128)(2,1)S(1)} %bitcast.128), channel_id=1, source_target_pairs={{0,4},{4,8},{8,12},{12,0},{1,5},{5,9},{9,13},{13,1},{2,6},{6,10},{... | collective-permute-start | bytes 393224 | tf_op jit(solution)/shard_map/ppermute | solution.py:155
  88.4 7.3 %collective-permute-start.20 = (bf16[2,64,512]{2,1,0:T(8,128)(2,1)S(1)}, bf16[2,64,512]{2,1,0:T(8,128)(2,1)S(1)}, u32[]{:S(2)}, u32[]{:S(2)}) collective-permute-start(bf16[2,64,512]{2,1,0:T(8,128)(2,1)S(1)} %bitcast.129), channel_id=1, source_target_pairs={{0,8},{4,12},{8,0},{12,4},{1,9},{5,13},{9,1},{13,5},{2,10},{6,14},... | collective-permute-start | bytes 393224 | tf_op jit(solution)/shard_map/ppermute | solution.py:155
  93.4 8.5 %collective-permute-start.36 = (bf16[64,2048]{1,0:T(8,128)(2,1)S(1)}, bf16[64,2048]{1,0:T(8,128)(2,1)S(1)}, u32[]{:S(2)}, u32[]{:S(2)}) collective-permute-start(bf16[64,2048]{1,0:T(8,128)(2,1)S(1)} %get-tuple-element.42), channel_id=1, source_target_pairs={{0,64},{64,0},{1,65},{65,1},{2,66},{66,2},{3,67},{67,3},{4,68},{68... | collective-permute-start | bytes 786440 | tf_op jit(solution)/shard_map/ppermute | solution.py:155
  94.9 9.4 %collective-permute-start.5 = (bf16[64,2048]{1,0:T(8,128)(2,1)S(1)}, bf16[64,2048]{1,0:T(8,128)(2,1)S(1)}, u32[]{:S(2)}, u32[]{:S(2)}) collective-permute-start(bf16[64,2048]{1,0:T(8,128)(2,1)S(1)} %get-tuple-element.43), channel_id=1, source_target_pairs={{0,64},{64,0},{1,65},{65,1},{2,66},{66,2},{3,67},{67,3},{4,68},{68... | collective-permute-start | bytes 786440 | tf_op jit(solution)/shard_map/ppermute | solution.py:155
  96.7 13.1 %collective-permute-start.22 = (bf16[4,64,512]{2,1,0:T(8,128)(2,1)S(1)}, bf16[4,64,512]{2,1,0:T(8,128)(2,1)S(1)}, u32[]{:S(2)}, u32[]{:S(2)}) collective-permute-start(bf16[4,64,512]{2,1,0:T(8,128)(2,1)S(1)} %get-tuple-element.37), channel_id=1, source_target_pairs={{0,16},{17,33},{33,49},{48,0},{2,18},{19,35},{35,51},{50,2},{4,20}... | collective-permute-start | bytes 786440 | tf_op jit(solution)/shard_map/ppermute | solution.py:214
  99.2 11.6 %collective-permute-start.23 = (bf16[4,64,512]{2,1,0:T(8,128)(2,1)S(1)}, bf16[4,64,512]{2,1,0:T(8,128)(2,1)S(1)}, u32[]{:S(2)}, u32[]{:S(2)}) collective-permute-start(bf16[4,64,512]{2,1,0:T(8,128)(2,1)S(1)} %get-tuple-element.36), channel_id=1, source_target_pairs={{1,33},{17,49},{32,0},{48,16},{3,35},{19,51},{34,2},{50,18},{5,37}... | collective-permute-start | bytes 786440 | tf_op jit(solution)/shard_map/ppermute | solution.py:214
  100.5 13.5 %collective-permute-start.24 = (bf16[4,64,512]{2,1,0:T(8,128)(2,1)S(1)}, bf16[4,64,512]{2,1,0:T(8,128)(2,1)S(1)}, u32[]{:S(2)}, u32[]{:S(2)}) collective-permute-start(bf16[4,64,512]{2,1,0:T(8,128)(2,1)S(1)} %get-tuple-element.35), channel_id=1, source_target_pairs={{1,49},{16,0},{32,16},{49,33},{3,51},{18,2},{34,18},{51,35},{5,53}... | collective-permute-start | bytes 786440 | tf_op jit(solution)/shard_map/ppermute | solution.py:214
  102.8 15.8 %collective-permute-start.45 = (bf16[2,64,1024]{2,1,0:T(8,128)(2,1)S(1)}, bf16[2,64,1024]{2,1,0:T(8,128)(2,1)}, u32[]{:S(2)}, u32[]{:S(2)}) collective-permute-start(bf16[2,64,1024]{2,1,0:T(8,128)(2,1)S(1)} %get-tuple-element.23), channel_id=1, source_target_pairs={{0,4},{4,8},{8,12},{12,0},{1,5},{5,9},{9,13},{13,1},{2,6},{6,10},{... | collective-permute-start | bytes 786440 | tf_op jit(solution)/shard_map/ppermute | solution.py:155
  104.3 14.9 %collective-permute-start.46 = (bf16[2,64,1024]{2,1,0:T(8,128)(2,1)S(1)}, bf16[2,64,1024]{2,1,0:T(8,128)(2,1)}, u32[]{:S(2)}, u32[]{:S(2)}) collective-permute-start(bf16[2,64,1024]{2,1,0:T(8,128)(2,1)S(1)} %get-tuple-element.23), channel_id=1, source_target_pairs={{0,12},{4,0},{8,4},{12,8},{1,13},{5,1},{9,5},{13,9},{2,14},{6,2},{... | collective-permute-start | bytes 786440 | tf_op jit(solution)/shard_map/ppermute | solution.py:155
  109.8 10.8 %collective-permute-start.37 = (bf16[2,64,1024]{2,1,0:T(8,128)(2,1)}, bf16[2,64,1024]{2,1,0:T(8,128)(2,1)}, u32[]{:S(2)}, u32[]{:S(2)}) collective-permute-start(bf16[2,64,1024]{2,1,0:T(8,128)(2,1)} %get-tuple-element.31), channel_id=1, source_target_pairs={{0,16},{16,32},{32,48},{48,0},{1,17},{17,33},{33,49},{49,1},{2,18}... | collective-permute-start | bytes 786440 | tf_op jit(solution)/shard_map/ppermute | solution.py:155
  110.8 11.6 %collective-permute-start.38 = (bf16[2,64,1024]{2,1,0:T(8,128)(2,1)}, bf16[2,64,1024]{2,1,0:T(8,128)(2,1)}, u32[]{:S(2)}, u32[]{:S(2)}) collective-permute-start(bf16[2,64,1024]{2,1,0:T(8,128)(2,1)} %get-tuple-element.31), channel_id=1, source_target_pairs={{0,48},{16,0},{32,16},{48,32},{1,49},{17,1},{33,17},{49,33},{2,50}... | collective-permute-start | bytes 786440 | tf_op jit(solution)/shard_map/ppermute | solution.py:155
  114.0 11.6 %collective-permute-start.28 = (bf16[2,64,1024]{2,1,0:T(8,128)(2,1)}, bf16[2,64,1024]{2,1,0:T(8,128)(2,1)S(1)}, u32[]{:S(2)}, u32[]{:S(2)}) collective-permute-start(bf16[2,64,1024]{2,1,0:T(8,128)(2,1)} %get-tuple-element.27), channel_id=1, source_target_pairs={{0,4},{4,8},{8,12},{12,0},{1,5},{5,9},{9,13},{13,1},{2,6},{6,10},{... | collective-permute-start | bytes 786440 | tf_op jit(solution)/shard_map/ppermute | solution.py:155
  118.5 38.7 %collective-permute-start.26 = (bf16[4,4,64,512]{3,2,1,0:T(8,128)(2,1)}, bf16[4,4,64,512]{3,2,1,0:T(8,128)(2,1)S(1)}, u32[]{:S(2)}, u32[]{:S(2)}) collective-permute-start(bf16[4,4,64,512]{3,2,1,0:T(8,128)(2,1)} %pad_maximum_fusion.1), channel_id=1, source_target_pairs={{64,2},{2,64},{80,18},{18,80},{97,35},{35,97},{113,51},{51,113},{6... | collective-permute-start | bytes 3145736 | tf_op jit(solution)/shard_map/ppermute | solution.py:223
  119.2 15.8 %collective-permute-start.29 = (bf16[2,64,1024]{2,1,0:T(8,128)(2,1)}, bf16[2,64,1024]{2,1,0:T(8,128)(2,1)}, u32[]{:S(2)}, u32[]{:S(2)}) collective-permute-start(bf16[2,64,1024]{2,1,0:T(8,128)(2,1)} %get-tuple-element.27), channel_id=1, source_target_pairs={{0,12},{4,0},{8,4},{12,8},{1,13},{5,1},{9,5},{13,9},{2,14},{6,2},{... | collective-permute-start | bytes 786440 | tf_op jit(solution)/shard_map/ppermute | solution.py:155
  120.7 18.2 %collective-permute-start.6 = (bf16[2,64,1024]{2,1,0:T(8,128)(2,1)}, bf16[2,64,1024]{2,1,0:T(8,128)(2,1)S(1)}, u32[]{:S(2)}, u32[]{:S(2)}) collective-permute-start(bf16[2,64,1024]{2,1,0:T(8,128)(2,1)} %get-tuple-element.33), channel_id=1, source_target_pairs={{0,16},{16,32},{32,48},{48,0},{1,17},{17,33},{33,49},{49,1},{2,18}... | collective-permute-start | bytes 786440 | tf_op jit(solution)/shard_map/ppermute | solution.py:155
  122.3 23.2 %collective-permute-start.7 = (bf16[2,64,1024]{2,1,0:T(8,128)(2,1)}, bf16[2,64,1024]{2,1,0:T(8,128)(2,1)S(1)}, u32[]{:S(2)}, u32[]{:S(2)}) collective-permute-start(bf16[2,64,1024]{2,1,0:T(8,128)(2,1)} %get-tuple-element.33), channel_id=1, source_target_pairs={{0,48},{16,0},{32,16},{48,32},{1,49},{17,1},{33,17},{49,33},{2,50}... | collective-permute-start | bytes 786440 | tf_op jit(solution)/shard_map/ppermute | solution.py:155
  125.6 36.6 %collective-permute-start.25 = (bf16[4,4,64,512]{3,2,1,0:T(8,128)(2,1)}, bf16[4,4,64,512]{3,2,1,0:T(8,128)(2,1)S(1)}, u32[]{:S(2)}, u32[]{:S(2)}) collective-permute-start(bf16[4,4,64,512]{3,2,1,0:T(8,128)(2,1)} %pad_maximum_fusion.1), channel_id=1, source_target_pairs={{0,2},{64,0},{2,66},{66,64},{16,18},{80,16},{18,82},{82,80},{33,35... | collective-permute-start | bytes 3145736 | tf_op jit(solution)/shard_map/ppermute | solution.py:223
  135.1 10.6 %collective-permute-start.47 = (bf16[1,64,1024]{2,1,0:T(8,128)(2,1)S(1)}, bf16[1,64,1024]{2,1,0:T(8,128)(2,1)S(1)}, u32[]{:S(2)}, u32[]{:S(2)}) collective-permute-start(bf16[1,64,1024]{2,1,0:T(8,128)(2,1)S(1)} %slice.96), channel_id=1, source_target_pairs={{0,4},{4,8},{8,12},{12,0},{1,5},{5,9},{9,13},{13,1},{2,6},{6,10},{... | collective-permute-start | bytes 393224 | tf_op jit(solution)/shard_map/ppermute | solution.py:155
  138.9 10.7 %collective-permute-start.48 = (bf16[1,64,1024]{2,1,0:T(8,128)(2,1)S(1)}, bf16[1,64,1024]{2,1,0:T(8,128)(2,1)S(1)}, u32[]{:S(2)}, u32[]{:S(2)}) collective-permute-start(bf16[1,64,1024]{2,1,0:T(8,128)(2,1)S(1)} %slice.97), channel_id=1, source_target_pairs={{0,12},{4,0},{8,4},{12,8},{1,13},{5,1},{9,5},{13,9},{2,14},{6,2},{... | collective-permute-start | bytes 393224 | tf_op jit(solution)/shard_map/ppermute | solution.py:155
  145.5 7.7 %collective-permute-start.39 = (bf16[1,64,1024]{2,1,0:T(8,128)(2,1)S(1)}, bf16[1,64,1024]{2,1,0:T(8,128)(2,1)S(1)}, u32[]{:S(2)}, u32[]{:S(2)}) collective-permute-start(bf16[1,64,1024]{2,1,0:T(8,128)(2,1)S(1)} %slice.92), channel_id=1, source_target_pairs={{0,16},{16,32},{32,48},{48,0},{1,17},{17,33},{33,49},{49,1},{2,18}... | collective-permute-start | bytes 393224 | tf_op jit(solution)/shard_map/ppermute | solution.py:155
  145.6 9.2 %collective-permute-start.40 = (bf16[1,64,1024]{2,1,0:T(8,128)(2,1)S(1)}, bf16[1,64,1024]{2,1,0:T(8,128)(2,1)S(1)}, u32[]{:S(2)}, u32[]{:S(2)}) collective-permute-start(bf16[1,64,1024]{2,1,0:T(8,128)(2,1)S(1)} %slice.93), channel_id=1, source_target_pairs={{0,48},{16,0},{32,16},{48,32},{1,49},{17,1},{33,17},{49,33},{2,50}... | collective-permute-start | bytes 393224 | tf_op jit(solution)/shard_map/ppermute | solution.py:155
  149.6 7.6 %collective-permute-start.30 = (bf16[1,64,1024]{2,1,0:T(8,128)(2,1)S(1)}, bf16[1,64,1024]{2,1,0:T(8,128)(2,1)S(1)}, u32[]{:S(2)}, u32[]{:S(2)}) collective-permute-start(bf16[1,64,1024]{2,1,0:T(8,128)(2,1)S(1)} %slice.86), channel_id=1, source_target_pairs={{0,4},{4,8},{8,12},{12,0},{1,5},{5,9},{9,13},{13,1},{2,6},{6,10},{... | collective-permute-start | bytes 393224 | tf_op jit(solution)/shard_map/ppermute | solution.py:155
  153.2 7.4 %collective-permute-start.31 = (bf16[1,64,1024]{2,1,0:T(8,128)(2,1)S(1)}, bf16[1,64,1024]{2,1,0:T(8,128)(2,1)S(1)}, u32[]{:S(2)}, u32[]{:S(2)}) collective-permute-start(bf16[1,64,1024]{2,1,0:T(8,128)(2,1)S(1)} %slice.87), channel_id=1, source_target_pairs={{0,12},{4,0},{8,4},{12,8},{1,13},{5,1},{9,5},{13,9},{2,14},{6,2},{... | collective-permute-start | bytes 393224 | tf_op jit(solution)/shard_map/ppermute | solution.py:155
  154.9 6.2 %collective-permute-start.8 = (bf16[1,64,1024]{2,1,0:T(8,128)(2,1)S(1)}, bf16[1,64,1024]{2,1,0:T(8,128)(2,1)S(1)}, u32[]{:S(2)}, u32[]{:S(2)}) collective-permute-start(bf16[1,64,1024]{2,1,0:T(8,128)(2,1)S(1)} %slice.82), channel_id=1, source_target_pairs={{0,16},{16,32},{32,48},{48,0},{1,17},{17,33},{33,49},{49,1},{2,18}... | collective-permute-start | bytes 393224 | tf_op jit(solution)/shard_map/ppermute | solution.py:155
  157.2 21.9 %collective-permute-start.49 = (bf16[8,64,1024]{2,1,0:T(8,128)(2,1)}, bf16[8,64,1024]{2,1,0:T(8,128)(2,1)S(1)}, u32[]{:S(2)}, u32[]{:S(2)}) collective-permute-start(bf16[8,64,1024]{2,1,0:T(8,128)(2,1)} %constant_dynamic-update-slice_fusion.15.refs_1_), channel_id=1, source_target_pairs={{0,16},{16,32},{32,48},{48,0},{1,17},{17,33},{33,49},{49,1},{2,18}... | collective-permute-start | bytes 3145736 | tf_op jit(solution)/shard_map/ppermute | solution.py:155
  157.2 22.6 %collective-permute-start.50 = (bf16[8,64,1024]{2,1,0:T(8,128)(2,1)}, bf16[8,64,1024]{2,1,0:T(8,128)(2,1)S(1)}, u32[]{:S(2)}, u32[]{:S(2)}) collective-permute-start(bf16[8,64,1024]{2,1,0:T(8,128)(2,1)} %constant_dynamic-update-slice_fusion.15.refs_1_), channel_id=1, source_target_pairs={{0,48},{16,0},{32,16},{48,32},{1,49},{17,1},{33,17},{49,33},{2,50}... | collective-permute-start | bytes 3145736 | tf_op jit(solution)/shard_map/ppermute | solution.py:155
  160.7 13.7 %collective-permute-start.9 = (bf16[1,64,1024]{2,1,0:T(8,128)(2,1)S(1)}, bf16[1,64,1024]{2,1,0:T(8,128)(2,1)S(1)}, u32[]{:S(2)}, u32[]{:S(2)}) collective-permute-start(bf16[1,64,1024]{2,1,0:T(8,128)(2,1)S(1)} %slice.83), channel_id=1, source_target_pairs={{0,48},{16,0},{32,16},{48,32},{1,49},{17,1},{33,17},{49,33},{2,50}... | collective-permute-start | bytes 393224 | tf_op jit(solution)/shard_map/ppermute | solution.py:155
  161.1 22.6 %collective-permute-start.41 = (bf16[8,64,1024]{2,1,0:T(8,128)(2,1)}, bf16[8,64,1024]{2,1,0:T(8,128)(2,1)S(1)}, u32[]{:S(2)}, u32[]{:S(2)}) collective-permute-start(bf16[8,64,1024]{2,1,0:T(8,128)(2,1)} %constant_dynamic-update-slice_fusion.10.refs_1_), channel_id=1, source_target_pairs={{0,4},{4,8},{8,12},{12,0},{1,5},{5,9},{9,13},{13,1},{2,6},{6,10},{... | collective-permute-start | bytes 3145736 | tf_op jit(solution)/shard_map/ppermute | solution.py:155
  162.1 21.6 %collective-permute-start.42 = (bf16[8,64,1024]{2,1,0:T(8,128)(2,1)}, bf16[8,64,1024]{2,1,0:T(8,128)(2,1)S(1)}, u32[]{:S(2)}, u32[]{:S(2)}) collective-permute-start(bf16[8,64,1024]{2,1,0:T(8,128)(2,1)} %constant_dynamic-update-slice_fusion.10.refs_1_), channel_id=1, source_target_pairs={{0,12},{4,0},{8,4},{12,8},{1,13},{5,1},{9,5},{13,9},{2,14},{6,2},{... | collective-permute-start | bytes 3145736 | tf_op jit(solution)/shard_map/ppermute | solution.py:155
  174.4 42.0 %collective-permute-start.27 = (bf16[2,4,4,64,512]{4,3,2,1,0:T(8,128)(2,1)}, bf16[2,4,4,64,512]{4,3,2,1,0:T(8,128)(2,1)}, u32[]{:S(2)}, u32[]{:S(2)}) collective-permute-start(bf16[2,4,4,64,512]{4,3,2,1,0:T(8,128)(2,1)} %pad_maximum_fusion), channel_id=1, source_target_pairs={{0,1},{16,17},{33,32},{49,48},{2,3},{18,19},{35,34},{51,50},{4,5},... | collective-permute-start | bytes 6291464 | tf_op jit(solution)/shard_map/ppermute | solution.py:230
  179.1 26.4 %collective-permute-start.32 = (bf16[8,64,1024]{2,1,0:T(8,128)(2,1)S(1)}, bf16[8,64,1024]{2,1,0:T(8,128)(2,1)S(1)}, u32[]{:S(2)}, u32[]{:S(2)}) collective-permute-start(bf16[8,64,1024]{2,1,0:T(8,128)(2,1)S(1)} %constant_dynamic-update-slice_fusion.5.refs_1_), channel_id=1, source_target_pairs={{0,16},{16,32},{32,48},{48,0},{1,17},{17,33},{33,49},{49,1},{2,18}... | collective-permute-start | bytes 3145736 | tf_op jit(solution)/shard_map/ppermute | solution.py:155
  179.8 25.8 %collective-permute-start.33 = (bf16[8,64,1024]{2,1,0:T(8,128)(2,1)S(1)}, bf16[8,64,1024]{2,1,0:T(8,128)(2,1)}, u32[]{:S(2)}, u32[]{:S(2)}) collective-permute-start(bf16[8,64,1024]{2,1,0:T(8,128)(2,1)S(1)} %constant_dynamic-update-slice_fusion.5.refs_1_), channel_id=1, source_target_pairs={{0,48},{16,0},{32,16},{48,32},{1,49},{17,1},{33,17},{49,33},{2,50}... | collective-permute-start | bytes 3145736 | tf_op jit(solution)/shard_map/ppermute | solution.py:155
  183.7 27.2 %collective-permute-start.10 = (bf16[8,64,1024]{2,1,0:T(8,128)(2,1)}, bf16[8,64,1024]{2,1,0:T(8,128)(2,1)}, u32[]{:S(2)}, u32[]{:S(2)}) collective-permute-start(bf16[8,64,1024]{2,1,0:T(8,128)(2,1)} %constant_dynamic-update-slice_fusion.refs_1_), channel_id=1, source_target_pairs={{0,4},{4,8},{8,12},{12,0},{1,5},{5,9},{9,13},{13,1},{2,6},{6,10},{... | collective-permute-start | bytes 3145736 | tf_op jit(solution)/shard_map/ppermute | solution.py:155
  183.7 28.3 %collective-permute-start.11 = (bf16[8,64,1024]{2,1,0:T(8,128)(2,1)}, bf16[8,64,1024]{2,1,0:T(8,128)(2,1)}, u32[]{:S(2)}, u32[]{:S(2)}) collective-permute-start(bf16[8,64,1024]{2,1,0:T(8,128)(2,1)} %constant_dynamic-update-slice_fusion.refs_1_), channel_id=1, source_target_pairs={{0,12},{4,0},{8,4},{12,8},{1,13},{5,1},{9,5},{13,9},{2,14},{6,2},{... | collective-permute-start | bytes 3145736 | tf_op jit(solution)/shard_map/ppermute | solution.py:155
  205.5 16.2 %collective-permute-start.51 = (bf16[4,64,1024]{2,1,0:T(8,128)(2,1)}, bf16[4,64,1024]{2,1,0:T(8,128)(2,1)}, u32[]{:S(2)}, u32[]{:S(2)}) collective-permute-start(bf16[4,64,1024]{2,1,0:T(8,128)(2,1)} %slice.98), channel_id=1, source_target_pairs={{0,16},{16,32},{32,48},{48,0},{1,17},{17,33},{33,49},{49,1},{2,18}... | collective-permute-start | bytes 1572872 | tf_op jit(solution)/shard_map/ppermute | solution.py:155
  205.6 18.1 %collective-permute-start.52 = (bf16[4,64,1024]{2,1,0:T(8,128)(2,1)}, bf16[4,64,1024]{2,1,0:T(8,128)(2,1)}, u32[]{:S(2)}, u32[]{:S(2)}) collective-permute-start(bf16[4,64,1024]{2,1,0:T(8,128)(2,1)} %slice.99), channel_id=1, source_target_pairs={{0,48},{16,0},{32,16},{48,32},{1,49},{17,1},{33,17},{49,33},{2,50}... | collective-permute-start | bytes 1572872 | tf_op jit(solution)/shard_map/ppermute | solution.py:155
  210.9 20.3 %collective-permute-start.43 = (bf16[4,64,1024]{2,1,0:T(8,128)(2,1)S(1)}, bf16[4,64,1024]{2,1,0:T(8,128)(2,1)S(1)}, u32[]{:S(2)}, u32[]{:S(2)}) collective-permute-start(bf16[4,64,1024]{2,1,0:T(8,128)(2,1)S(1)} %slice.94), channel_id=1, source_target_pairs={{0,4},{4,8},{8,12},{12,0},{1,5},{5,9},{9,13},{13,1},{2,6},{6,10},{... | collective-permute-start | bytes 1572872 | tf_op jit(solution)/shard_map/ppermute | solution.py:155
  212.0 22.6 %collective-permute-start.44 = (bf16[4,64,1024]{2,1,0:T(8,128)(2,1)S(1)}, bf16[4,64,1024]{2,1,0:T(8,128)(2,1)S(1)}, u32[]{:S(2)}, u32[]{:S(2)}) collective-permute-start(bf16[4,64,1024]{2,1,0:T(8,128)(2,1)S(1)} %slice.95), channel_id=1, source_target_pairs={{0,12},{4,0},{8,4},{12,8},{1,13},{5,1},{9,5},{13,9},{2,14},{6,2},{... | collective-permute-start | bytes 1572872 | tf_op jit(solution)/shard_map/ppermute | solution.py:155
  216.4 25.8 %collective-permute-start.34 = (bf16[4,64,1024]{2,1,0:T(8,128)(2,1)S(1)}, bf16[4,64,1024]{2,1,0:T(8,128)(2,1)S(1)}, u32[]{:S(2)}, u32[]{:S(2)}) collective-permute-start(bf16[4,64,1024]{2,1,0:T(8,128)(2,1)S(1)} %slice.88), channel_id=1, source_target_pairs={{0,16},{16,32},{32,48},{48,0},{1,17},{17,33},{33,49},{49,1},{2,18}... | collective-permute-start | bytes 1572872 | tf_op jit(solution)/shard_map/ppermute | solution.py:155
  221.7 20.5 %collective-permute-start.35 = (bf16[4,64,1024]{2,1,0:T(8,128)(2,1)S(1)}, bf16[4,64,1024]{2,1,0:T(8,128)(2,1)S(1)}, u32[]{:S(2)}, u32[]{:S(2)}) collective-permute-start(bf16[4,64,1024]{2,1,0:T(8,128)(2,1)S(1)} %slice.89), channel_id=1, source_target_pairs={{0,48},{16,0},{32,16},{48,32},{1,49},{17,1},{33,17},{49,33},{2,50}... | collective-permute-start | bytes 1572872 | tf_op jit(solution)/shard_map/ppermute | solution.py:155
  223.7 26.2 %collective-permute-start.12 = (bf16[4,64,1024]{2,1,0:T(8,128)(2,1)S(1)}, bf16[4,64,1024]{2,1,0:T(8,128)(2,1)S(1)}, u32[]{:S(2)}, u32[]{:S(2)}) collective-permute-start(bf16[4,64,1024]{2,1,0:T(8,128)(2,1)S(1)} %slice.84), channel_id=1, source_target_pairs={{0,4},{4,8},{8,12},{12,0},{1,5},{5,9},{9,13},{13,1},{2,6},{6,10},{... | collective-permute-start | bytes 1572872 | tf_op jit(solution)/shard_map/ppermute | solution.py:155
  231.2 18.6 %collective-permute-start.13 = (bf16[4,64,1024]{2,1,0:T(8,128)(2,1)S(1)}, bf16[4,64,1024]{2,1,0:T(8,128)(2,1)S(1)}, u32[]{:S(2)}, u32[]{:S(2)}) collective-permute-start(bf16[4,64,1024]{2,1,0:T(8,128)(2,1)S(1)} %slice.85), channel_id=1, source_target_pairs={{0,12},{4,0},{8,4},{12,8},{1,13},{5,1},{9,5},{13,9},{2,14},{6,2},{... | collective-permute-start | bytes 1572872 | tf_op jit(solution)/shard_map/ppermute | solution.py:155
  (19 other events, 144.0 us)

commit v2 on v1

v2 whole, which is shorter than its diff:
```python
import jax
import jax.numpy as jnp
from jax import lax
from jax.experimental import pallas as pl
from jax.experimental.pallas import tpu as pltpu
from jax.sharding import Mesh, PartitionSpec as P

LAG = 64
contact_radius = 1.2
contact_width = 0.25
TILE = 512
MIB = 1 << 20


def feature_kernel(index_ref, coords_ref, lifted_ref, sums_ref, chosen):
    rows_all, residues = coords_ref.shape
    frames, width = lifted_ref.shape
    pieces = rows_all // frames
    atoms = pieces // 3
    scale = 0.5 / contact_width
    shift = contact_radius * scale

    numbers = lax.broadcasted_iota(jnp.int32, (residues, 256), 0)
    one_hot = jnp.where(numbers == index_ref[0:1, :], scale, 0.0).astype(jnp.bfloat16)

    @pl.loop(0, 3)
    def _(component):
        rows = pl.ds(pl.multiple_of(component * (atoms * frames), atoms * frames), atoms * frames)
        whole = coords_ref[rows, :]
        high = whole.astype(jnp.bfloat16)
        rest = whole - high.astype(jnp.float32)
        middle = rest.astype(jnp.bfloat16)
        low = (rest - middle.astype(jnp.float32)).astype(jnp.bfloat16)
        parts = [jnp.dot(part, one_hot, preferred_element_type=jnp.float32) for part in (high, middle, low)]
        chosen[rows, :] = (parts[0] + parts[1]) + parts[2]

    @pl.loop(0, frames // 8)
    def _(octet):
        start = pl.multiple_of(octet * 8, 8)
        for residue in range(width // 128):
            totals = [None, None]
            for p in range(atoms):
                ax, ay, az = [
                    jnp.broadcast_to(
                        chosen[pl.ds((c * atoms + p) * frames + start, 8), 128 + residue : 129 + residue], (8, 128)
                    )
                    for c in range(3)
                ]
                for q in range(atoms):
                    bx, by, bz = [chosen[pl.ds((c * atoms + q) * frames + start, 8), :128] for c in range(3)]
                    dx, dy, dz = ax - bx, ay - by, az - bz
                    square = jnp.maximum(dx * dx + dy * dy + dz * dz, 1e-30)
                    value = jnp.tanh(shift - square * lax.rsqrt(square))
                    totals[q % 2] = value if totals[q % 2] is None else totals[q % 2] + value
            features = (totals[0] + totals[1] + float(atoms * atoms)) * (0.5 / atoms)
            lifted_ref[pl.ds(start, 8), residue * 128 : (residue + 1) * 128] = features

    weight = index_ref[1:2, 0:1].astype(jnp.float32)
    sums_ref[...] = jnp.sum(lifted_ref[...], axis=0, keepdims=True) * weight


def contact_features(count, indices, coords):
    pieces, frames, residues = coords.shape
    width = count * 128
    pairs = frames * width * (pieces // 3) ** 2
    return pl.pallas_call(
        feature_kernel,
        out_shape=(
            jax.ShapeDtypeStruct((frames, width), jnp.float32),
            jax.ShapeDtypeStruct((1, width), jnp.float32),
        ),
        in_specs=[pl.BlockSpec(memory_space=pltpu.VMEM)] * 2,
        out_specs=[pl.BlockSpec(memory_space=pltpu.VMEM)] * 2,
        scratch_shapes=[pltpu.VMEM((pieces * frames, 256), jnp.float32)],
        compiler_params=pltpu.CompilerParams(vmem_limit_bytes=24 * MIB),
        cost_estimate=pl.CostEstimate(flops=pairs * 12, bytes_accessed=4 * MIB, transcendentals=2 * pairs),
    )(indices, coords.reshape(pieces * frames, residues))


def column_kernel(map_ref, orders_ref, cols_ref, *out_refs):
    blocks, frames, width = cols_ref.shape

    @pl.loop(0, blocks)
    def _(number):
        for stream, out_ref in enumerate(out_refs):
            block = orders_ref[stream, number]
            here = cols_ref[map_ref[block]].astype(jnp.float32)
            before = cols_ref[map_ref[jnp.maximum(block - 1, 0)]].astype(jnp.float32)
            after = cols_ref[map_ref[jnp.minimum(block + 1, blocks - 1)]].astype(jnp.float32)
            inner = jnp.logical_and(block > 0, block < blocks - 1)
            out_ref[number, :, :width] = jnp.where(inner, 2.0 * here, here).astype(jnp.bfloat16)
            lagged = jnp.where(block > 0, before, 0.0) + jnp.where(block < blocks - 1, after, 0.0)
            out_ref[number, :, width:] = lagged.astype(jnp.bfloat16)


def lagged_columns(block_map, orders, cols):
    blocks, frames, width = cols.shape
    out = jax.ShapeDtypeStruct((blocks, frames, 2 * width), jnp.bfloat16)
    return pl.pallas_call(
        column_kernel,
        out_shape=(out, out),
        in_specs=[pl.BlockSpec(memory_space=pltpu.SMEM)] * 2 + [pl.BlockSpec(memory_space=pltpu.VMEM)],
        out_specs=[pl.BlockSpec(memory_space=pltpu.VMEM)] * 2,
        compiler_params=pltpu.CompilerParams(vmem_limit_bytes=24 * MIB),
        cost_estimate=pl.CostEstimate(flops=16 * cols.size, bytes_accessed=10 * cols.size, transcendentals=0),
    )(block_map, orders, cols)


def product_kernel(count, factor, added, *refs):
    pieces, columns_ref = refs[:count], refs[count]
    c00_ref, c0t_ref = refs[-2:]
    width = c00_ref.shape[1]
    left = jnp.concatenate([piece[...].reshape(-1, piece.shape[2]) for piece in pieces], axis=0)
    right = columns_ref[...].reshape(left.shape[0], 2 * width)
    sums = lax.dot_general(left, right, (((0,), (0,)), ((), ())), preferred_element_type=jnp.float32)
    for number, ref in enumerate((c00_ref, c0t_ref)):
        part = sums[:, number * width : (number + 1) * width] * factor
        ref[...] = part + refs[count + 1 + number][...] if added else part


def products(pieces, columns, column_start, row_start, rows, factor, previous, added):
    _, frames, double = columns.shape
    width = double // 2
    features = pieces[0].shape[2]
    first = row_start // TILE
    out = jax.ShapeDtypeStruct((rows, width), jnp.float32)
    count = len(pieces)
    blocks = sum(piece.shape[0] for piece in pieces)
    passed = () if previous is None else previous
    out_spec = pl.BlockSpec((TILE, width), lambda i: (first + i, 0))
    in_specs = [pl.BlockSpec((piece.shape[0], frames, TILE), lambda i: (0, 0, i)) for piece in pieces]
    in_specs += [pl.BlockSpec((blocks, frames, double), lambda i: (column_start // blocks, 0, 0))]
    in_specs += [out_spec if added else pl.BlockSpec(memory_space=pl.ANY)] * len(passed)
    return pl.pallas_call(
        lambda *refs: product_kernel(count, factor, added, *refs),
        grid=(features // TILE,),
        in_specs=in_specs,
        out_specs=[out_spec] * 2,
        out_shape=(out, out),
        input_output_aliases={count + 1 + n: n for n in range(len(passed))},
        compiler_params=pltpu.CompilerParams(vmem_limit_bytes=36 * MIB),
        cost_estimate=pl.CostEstimate(
            flops=2 * features * blocks * frames * double,
            bytes_accessed=features * double * (8 if added else 4) + blocks * frames * (features + double) * 2,
            transcendentals=0,
        ),
    )(*pieces, columns, *passed)


def plane_kernel(*refs):
    for number, ref in enumerate(refs[:-1]):
        refs[-1][number] = ref[...]


def plane_of(blocks):
    return pl.pallas_call(
        plane_kernel,
        out_shape=jax.ShapeDtypeStruct((len(blocks), *blocks[0].shape), blocks[0].dtype),
        in_specs=[pl.BlockSpec(memory_space=pltpu.VMEM)] * len(blocks),
        out_specs=pl.BlockSpec(memory_space=pltpu.VMEM),
        compiler_params=pltpu.CompilerParams(vmem_limit_bytes=16 * MIB),
        cost_estimate=pl.CostEstimate(
            flops=0, bytes_accessed=4 * len(blocks) * blocks[0].size, transcendentals=0
        ),
    )(*blocks)


def moved(array, axis, by):
    length = lax.axis_size(axis)
    return lax.ppermute(array, axis, [(i, (i + by) % length) for i in range(length)])


def summed(array):
    for axis in ("x", "z", "yl"):
        steps = range(1, lax.axis_size(axis))
        array = sum([moved(array, axis, by) for by in steps], start=array)
    return array


OFFSETS = (0, -1, 1, 2)


def near_blocks(block, axis):
    return moved(block, axis, 1), moved(block, axis, -1)


def far_block(behind, ahead, axis):
    half = behind.shape[0] // 2
    return moved(behind[:half], axis, 1), moved(ahead[half:], axis, -1)


def block_order(first, second, place):
    order = []
    for offset in OFFSETS:
        for yl in (place["yl"], 1 - place["yl"]):
            for inner in OFFSETS:
                at = {first: (place[first] + inner) % 4, second: (place[second] + offset) % 4}
                order.append(yl * 16 + at["z"] * 4 + at["x"])
    return jnp.stack(order).astype(jnp.int32)


def columns_along_x(centered, place):
    frames, features = centered.shape
    by_owner = jnp.transpose(centered.reshape(frames, 2, 4, features // 8), (2, 1, 0, 3))
    along_x = [lax.dynamic_index_in_dim(by_owner, place["x"], 0, keepdims=False)]
    for by in (1, 2, 3):
        piece = lax.dynamic_index_in_dim(by_owner, (place["x"] + by) % 4, 0, keepdims=False)
        along_x.append(moved(piece, "x", by))
    return along_x


def columns_along_z(along_x, place):
    along_x = jnp.stack(along_x)
    along_z = [lax.dynamic_index_in_dim(along_x, place["z"] % 2, 1, keepdims=False)]
    for by in (1, 2, 3):
        piece = lax.dynamic_index_in_dim(along_x, (place["z"] + by) % 2, 1, keepdims=False)
        pairs = []
        for z in range(4):
            target = (z + by) % 4
            core = target // 2
            pairs.append((z * 2 + core, target * 2 + core))
        along_z.append(lax.ppermute(piece, ("z", "c"), pairs))
    return along_z


def columns_along_y(along_z, moves):
    pairs = []
    for z in range(4):
        for source, target in moves:
            flat = lambda y: (((y % 2) * 4 + z) * 2 + y // 2) * 2 + z // 2
            pairs.append((flat(source), flat(target)))
    return lax.ppermute(along_z, ("yl", "z", "yh", "c"), pairs)


def columns_of_chip(one, two, place):
    both = jnp.stack([one, two])
    pairs = [(z * 2 + z // 2, z * 2 + 1 - z // 2) for z in range(4)]
    passed = lax.ppermute(both, ("z", "c"), pairs)
    both = jnp.where(place["z"] // 2 == place["c"], both, passed)
    order = []
    for block in range(32):
        y, z, x = block // 16, (block // 4) % 4, block % 4
        group = jnp.where(y == 1 - place["yh"], 0, 1)
        order.append(group * 16 + ((place["z"] - z) % 4) * 4 + (place["x"] - x) % 4)
    return both.reshape(32, *both.shape[3:]), jnp.stack(order).astype(jnp.int32)


def together(*groups):
    return lax.optimization_barrier(groups)


def per_device(coords, set_a, set_b):
    place = {axis: lax.axis_index(axis) for axis in ("yl", "z", "x", "yh", "c")}
    frames, _, atoms, residues = coords.shape
    feat_index = place["yh"] * 2 + place["c"]
    time_index = place["yl"] * 16 + place["z"] * 4 + place["x"]
    rows_a = set_a.shape[0] // 4
    pairs = frames * 32 - LAG
    edge = jnp.logical_or(time_index == 0, time_index == 31)
    index_a = lax.dynamic_slice_in_dim(set_a, feat_index * rows_a, rows_a)
    chosen = jnp.concatenate([set_b, index_a, jnp.zeros((128 - rows_a,), jnp.int32)])
    weight = jnp.broadcast_to(jnp.where(edge, 1, 2).astype(jnp.int32), (256,))
    indices = jnp.stack([chosen, weight, *([weight] * 6)])
    atoms_first = jnp.transpose(coords, (1, 2, 0, 3)).reshape(3 * atoms, frames, residues)

    lifted, sums = contact_features(rows_a, indices, atoms_first)
    centered = (lifted - summed(sums) / (2.0 * pairs)).astype(jnp.bfloat16)

    rows = rows_a * 128
    half = rows // 2
    ways = (("x", "z"), ("z", "x"))
    taken = (slice(0, half), slice(half, rows))

    own = [centered[:, part] for part in taken]
    partner = moved(centered, "yl", 1)
    own_near = [near_blocks(block, way[0]) for block, way in zip(own, ways)]
    along_x = columns_along_x(centered, place)
    partner, own_near, own, along_x = together(partner, own_near, own, along_x)

    other = [partner[:, part] for part in taken]
    other_near = [near_blocks(block, way[0]) for block, way in zip(other, ways)]
    along_z = jnp.stack(columns_along_z(along_x, place))
    other_near, along_z, own_near, other = together(other_near, along_z, own_near, other)

    far = [
        (moved(mine[0], way[0], 1), moved(theirs[1], way[0], -1))
        for mine, theirs, way in zip(own_near, other_near, ways)
    ]
    one = columns_along_y(along_z, [(0, 2), (1, 0), (2, 3), (3, 1)])
    far, along_z, one = together(far, along_z, one)

    planes = [
        plane_of([own[n], *own_near[n], far[n][0], other[n], *other_near[n], far[n][1]]) for n in range(2)
    ]
    planes, along_z = together(planes, along_z)
    near = [near_blocks(plane, way[1]) for plane, way in zip(planes, ways)]
    two = columns_along_y(along_z, [(1, 2), (2, 1)])
    two = jnp.where(place["yl"] == place["yh"], along_z, two)
    cols, col_order = columns_of_chip(one, two, place)
    orders = jnp.stack([block_order(*way, place) for way in ways])
    columns = lagged_columns(col_order, orders, cols)

    last = [far_block(*blocks, way[1]) for blocks, way in zip(near, ways)]
    results = None
    for n in range(2):
        results = products([planes[n], *near[n]], columns[n], 0, n * half, rows, 0.5 / pairs, results, False)
    for n in range(2):
        results = products(last[n], columns[n], 24, n * half, rows, 0.5 / pairs, results, True)
    return results


def solution(mesh):
    fine = Mesh(mesh.devices.reshape(2, 4, 4, 2, 2), ("yl", "z", "x", "yh", "c"))
    time_axes, feat_axes = ("yl", "z", "x"), ("yh", "c")
    return jax.shard_map(
        per_device,
        mesh=fine,
        in_specs=(P(time_axes, None, None, None), P(), P()),
        out_specs=(P(feat_axes, time_axes), P(feat_axes, time_axes)),
        check_vma=False,
    )
```

time: 258 us -> 217 us (0.84)
  starting transfers between devices: 91.8 us -> 57.8 us
  waiting for transfers between devices: 41.3 us -> 65.9 us
  Pallas kernels: 89.6 us -> 71 us
  local copies, waits for them, and re-layouts: 28.2 us -> 12.8 us
    ppermute x37 -> x31, waiting for transfers between devices: 33.4 us -> 64.7 us  [moved(): lax.ppermute(array, axis, [(i, (i + by) % length) for i in range(length)])]
    ppermute x16 -> x6, starting transfers between devices: 36.4 us -> 16.2 us  [the longest x3 7.13 us: columns_along_z(): along_z.append(lax.ppermute(piece, ('z', 'c'), pairs))]
    pallas_call x7 -> x8, Pallas kernels: 89.6 us -> 71 us  [the longest x4 34.6 us: products(): pl.pallas_call(lambda *refs: product_kernel(count, factor, added, *refs),...]
    ppermute x37 -> x31, starting transfers between devices: 55.3 us -> 41.6 us  [moved(): lax.ppermute(array, axis, [(i, (i + by) % length) for i in range(length)])]
    unnamed x44 -> x16, local copies, waits for them, and re-layouts: 11.9 us -> 2.45 us
    ppermute x16 -> x6, waiting for transfers between devices: 7.87 us -> 1.14 us  [the longest x3 1.13 us: columns_along_z(): along_z.append(lax.ppermute(piece, ('z', 'c'), pairs))]
    slice x16 -> x6, local copies, waits for them, and re-layouts: 9.75 us -> 6.4 us  [the longest x4 5.29 us: far_block(): return (moved(behind[:half], axis, 1), moved(ahead[half:], axis, -1))]
    another operation x4 -> x5, other arithmetic: 2.83 us -> 5.25 us  [the longest x2 4.08 us: columns_of_chip(): both = jnp.stack([one, two])]
  transfers between devices with their start and end apart: 53 -> 37, of which waited for: 13 -> 17; matrix products, arithmetic and copies ran while one was open for 11% -> 7% of each run, Pallas kernels for 21% -> 14%
where the time goes in v2:
time: 217 us; the launch traced here: 215 us
  Pallas kernels  71 us (33%)
  waiting for transfers between devices  65.9 us (30%)
  starting transfers between devices  57.8 us (27%)
  local copies, waits for them, and re-layouts  12.8 us (6%)
  other arithmetic  6.98 us (3%)
    ppermute x31, waiting for transfers between devices, moved(): lax.ppermute(array, axis, [(i, (i + by) % length) for i in range(length)])  64.7 us
    ppermute x31, starting transfers between devices, moved(): lax.ppermute(array, axis, [(i, (i + by) % length) for i in range(length)])  41.6 us
    pallas_call x4, Pallas kernels, products(): pl.pallas_call(lambda *refs: product_kernel(count, factor, added, *refs),...  34.6 us
    pallas_call x1, Pallas kernels, contact_features(): pl.pallas_call(feature_kernel, out_shape=(jax.ShapeDtypeStruct((frames, w...  32.8 us
    ppermute x3, starting transfers between devices, columns_along_z(): along_z.append(lax.ppermute(piece, ('z', 'c'), pairs))  7.13 us
    ppermute x2, starting transfers between devices, columns_along_y(): return lax.ppermute(along_z, ('yl', 'z', 'yh', 'c'), pairs)  6.42 us
    slice x4, local copies, waits for them, and re-layouts, far_block(): return (moved(behind[:half], axis, 1), moved(ahead[half:], axis, -1))  5.29 us
  transfers between devices with their start and end apart: 37, of which 17 were waited for; matrix products, arithmetic and copies ran while one was open for 7% of the time, Pallas kernels for 14%

profile of v2, /device:TPU:0, one launch (start us, length us, event | category | flops | bytes accessed | tf_op | source)
XLA Modules:
  0.0 215.4 jit_solution(16675955143139838224)
XLA Ops:
  0.7 1.9 copy.15
  2.8 32.8 %shard_map.50 = (f32[64,4096]{1,0:T(8,128)S(1)}, f32[1,4096]{1,0:T(1,128)S(1)}) custom-call(s32[8,256]{1,0:T(8,128)S(1)} %stack.288.index_ref, f32[1536,256]{1,0:T(8,128)S(1)} %bitcast.110), custom_call_target="tpu_custom_call" | custom-call | flops 201326592 | bytes 4194304 | tf_op jit(solution)/shard_map/pallas_call | solution.py:66
  35.6 2.9 %collective-permute-start.2 = (f32[1,4096]{1,0:T(1,128)S(1)}, f32[1,4096]{1,0:T(1,128)S(1)}, u32[]{:S(2)}, u32[]{:S(2)}) collective-permute-start(f32[1,4096]{1,0:T(1,128)S(1)} %get-tuple-element.44), channel_id=1, source_target_pairs={{0,12},{4,0},{8,4},{12,8},{1,13},{5,1},{9,5},{13,9},{2,14},{6,2},{... | collective-permute-start | bytes 49160 | tf_op jit(solution)/shard_map/ppermute | solution.py:170
  40.2 3.6 %collective-permute-done.1 = f32[1,4096]{1,0:T(1,128)S(1)} collective-permute-done((f32[1,4096]{1,0:T(1,128)S(1)}, f32[1,4096]{1,0:T(1,128)S(1)}, u32[]{:S(2)}, u32[]{:S(2)}) %collective-permute-start.1) | collective-permute-done | bytes 16416 | tf_op jit(solution)/shard_map/ppermute | solution.py:170
  44.3 4.1 %collective-permute-start.5 = (f32[1,4096]{1,0:T(1,128)S(1)}, f32[1,4096]{1,0:T(1,128)S(1)}, u32[]{:S(2)}, u32[]{:S(2)}) collective-permute-start(f32[1,4096]{1,0:T(1,128)S(1)} %add_add_fusion.1), channel_id=1, source_target_pairs={{0,48},{16,0},{32,16},{48,32},{1,49},{17,1},{33,17},{49,33},{2,50}... | collective-permute-start | bytes 49160 | tf_op jit(solution)/shard_map/ppermute | solution.py:170
  49.8 3.8 %collective-permute-done.4 = f32[1,4096]{1,0:T(1,128)S(1)} collective-permute-done((f32[1,4096]{1,0:T(1,128)S(1)}, f32[1,4096]{1,0:T(1,128)S(1)}, u32[]{:S(2)}, u32[]{:S(2)}) %collective-permute-start.4) | collective-permute-done | bytes 16416 | tf_op jit(solution)/shard_map/ppermute | solution.py:170
  53.7 1.7 collective-permute-start.6
  55.3 2.3 %collective-permute-done.6 = f32[1,4096]{1,0:T(1,128)S(1)} collective-permute-done((f32[1,4096]{1,0:T(1,128)S(1)}, f32[1,4096]{1,0:T(1,128)S(1)}, u32[]{:S(2)}, u32[]{:S(2)}) %collective-permute-start.6) | collective-permute-done | bytes 16416 | tf_op jit(solution)/shard_map/ppermute | solution.py:170
  58.1 1.7 collective-permute-start.7
  61.1 1.7 collective-permute-start.13
  62.8 2.4 %collective-permute-start.14 = (bf16[2,64,512]{2,1,0:T(8,128)(2,1)S(1)}, bf16[2,64,512]{2,1,0:T(8,128)(2,1)S(1)}, u32[]{:S(2)}, u32[]{:S(2)}) collective-permute-start(bf16[2,64,512]{2,1,0:T(8,128)(2,1)S(1)} %bitcast.116), channel_id=1, source_target_pairs={{0,12},{4,0},{8,4},{12,8},{1,13},{5,1},{9,5},{13,9},{2,14},{6,2},{... | collective-permute-start | bytes 393224 | tf_op jit(solution)/shard_map/ppermute | solution.py:170
  66.1 2.8 %collective-permute-done.12 = bf16[2,64,512]{2,1,0:T(8,128)(2,1)S(1)} collective-permute-done((bf16[2,64,512]{2,1,0:T(8,128)(2,1)S(1)}, bf16[2,64,512]{2,1,0:T(8,128)(2,1)S(1)}, u32[]{:S(2)}, u32[]{:S(2)}) %collective-permute-start.12) | collective-permute-done | bytes 131104 | tf_op jit(solution)/shard_map/ppermute | solution.py:170
  68.9 3.3 %collective-permute-start.9 = (bf16[64,2048]{1,0:T(8,128)(2,1)S(1)}, bf16[64,2048]{1,0:T(8,128)(2,1)S(1)}, u32[]{:S(2)}, u32[]{:S(2)}) collective-permute-start(bf16[64,2048]{1,0:T(8,128)(2,1)S(1)} %get-tuple-element.45.refs_0_), channel_id=1, source_target_pairs={{0,12},{4,0},{8,4},{12,8},{1,13},{5,1},{9,5},{13,9},{2,14},{6,2},{... | collective-permute-start | bytes 786440 | tf_op jit(solution)/shard_map/ppermute | solution.py:170
  72.3 4.2 %collective-permute-done.10.refs_1_ = bf16[64,2048]{1,0:T(8,128)(2,1)S(1)} collective-permute-done((bf16[64,2048]{1,0:T(8,128)(2,1)S(1)}, bf16[64,2048]{1,0:T(8,128)(2,1)S(1)}, u32[]{:S(2)}, u32[]{:S(2)}) %collective-permute-start.10) | collective-permute-done | bytes 262176 | tf_op jit(solution)/shard_map/ppermute | solution.py:170
  76.4 3.4 %collective-permute-done.8.refs_1_ = bf16[64,2048]{1,0:T(8,128)(2,1)S(1)} collective-permute-done((bf16[64,2048]{1,0:T(8,128)(2,1)S(1)}, bf16[64,2048]{1,0:T(8,128)(2,1)S(1)}, u32[]{:S(2)}, u32[]{:S(2)}) %collective-permute-start.8) | collective-permute-done | bytes 262176 | tf_op jit(solution)/shard_map/ppermute | solution.py:170
  80.0 1.3 collective-permute-start.21
  81.3 1.3 collective-permute-start.20
  82.6 4.6 %collective-permute-start.19 = (bf16[4,64,512]{2,1,0:T(8,128)(2,1)S(1)}, bf16[4,64,512]{2,1,0:T(8,128)(2,1)S(1)}, u32[]{:S(2)}, u32[]{:S(2)}) collective-permute-start(bf16[4,64,512]{2,1,0:T(8,128)(2,1)S(1)} %get-tuple-element.87), channel_id=1, source_target_pairs={{0,16},{17,33},{33,49},{48,0},{2,18},{19,35},{35,51},{50,2},{4,20}... | collective-permute-start | bytes 786440 | tf_op jit(solution)/shard_map/ppermute | solution.py:222
  88.2 2.8 %collective-permute-start.18 = (bf16[64,2048]{1,0:T(8,128)(2,1)S(1)}, bf16[64,2048]{1,0:T(8,128)(2,1)S(1)}, u32[]{:S(2)}, u32[]{:S(2)}) collective-permute-start(bf16[64,2048]{1,0:T(8,128)(2,1)S(1)} %get-tuple-element.68.refs_4_), channel_id=1, source_target_pairs={{0,48},{16,0},{32,16},{48,32},{1,49},{17,1},{33,17},{49,33},{2,50}... | collective-permute-start | bytes 786440 | tf_op jit(solution)/shard_map/ppermute | solution.py:170
  91.5 1.5 collective-permute-start.15
  95.3 3.3 %collective-permute-done.17.refs_5_ = bf16[64,2048]{1,0:T(8,128)(2,1)S(1)} collective-permute-done((bf16[64,2048]{1,0:T(8,128)(2,1)S(1)}, bf16[64,2048]{1,0:T(8,128)(2,1)S(1)}, u32[]{:S(2)}, u32[]{:S(2)}) %collective-permute-start.17) | collective-permute-done | bytes 262176 | tf_op jit(solution)/shard_map/ppermute | solution.py:170
  100.2 4.8 %collective-permute-start.26 = (bf16[4,4,64,512]{3,2,1,0:T(8,128)(2,1)}, bf16[4,4,64,512]{3,2,1,0:T(8,128)(2,1)}, u32[]{:S(2)}, u32[]{:S(2)}) collective-permute-start(bf16[4,4,64,512]{3,2,1,0:T(8,128)(2,1)} %pad_maximum_fusion.1), channel_id=1, source_target_pairs={{0,2},{64,0},{2,66},{66,64},{16,18},{80,16},{18,82},{82,80},{33,35... | collective-permute-start | bytes 3145736 | tf_op jit(solution)/shard_map/ppermute | solution.py:232
  105.1 3.2 %collective-permute-start.23 = (bf16[64,2048]{1,0:T(8,128)(2,1)S(1)}, bf16[64,2048]{1,0:T(8,128)(2,1)S(1)}, u32[]{:S(2)}, u32[]{:S(2)}) collective-permute-start(bf16[64,2048]{1,0:T(8,128)(2,1)S(1)} %collective-permute-done.16.refs_6_), channel_id=1, source_target_pairs={{0,12},{4,0},{8,4},{12,8},{1,13},{5,1},{9,5},{13,9},{2,14},{6,2},{... | collective-permute-start | bytes 786440 | tf_op jit(solution)/shard_map/ppermute | solution.py:170
  108.3 1.4 collective-permute-start.24
  109.7 1.9 collective-permute-start.25
  111.5 2.0 collective-permute-done.22.refs_3_
  113.5 1.5 collective-permute-done.23.refs_7_
  115.9 3.0 %collective-permute-done.25.refs_7_ = bf16[64,2048]{1,0:T(8,128)(2,1)S(1)} collective-permute-done((bf16[64,2048]{1,0:T(8,128)(2,1)S(1)}, bf16[64,2048]{1,0:T(8,128)(2,1)S(1)}, u32[]{:S(2)}, u32[]{:S(2)}) %collective-permute-start.25) | collective-permute-done | bytes 262176 | tf_op jit(solution)/shard_map/ppermute | solution.py:170
  120.0 1.3 copy-done
  121.4 1.6 collective-permute-start.31
  123.0 2.0 collective-permute-start.27
  125.3 1.8 collective-permute-start.33
  127.1 1.3 select_bitcast_fusion
  128.4 2.7 %pad_maximum_fusion = bf16[2,4,4,64,512]{4,3,2,1,0:T(8,128)(2,1)} fusion(bf16[1,4,4,64,512]{4,3,2,1,0:T(8,128)(2,1)S(1)} %select_bitcast_fusion, bf16[1,4,4,64,512]{4,3,2,1,0:T(8,128)(2,1)} %bitcast.89), kind=kLoop, calls=%fused_computation | loop fusion | flops 1048576 | bytes 4194304 | tf_op jit(solution)/shard_map/stack | solution.py:236
  131.2 2.6 %collective-permute-start.32 = (bf16[2,4,4,64,512]{4,3,2,1,0:T(8,128)(2,1)}, bf16[2,4,4,64,512]{4,3,2,1,0:T(8,128)(2,1)}, u32[]{:S(2)}, u32[]{:S(2)}) collective-permute-start(bf16[2,4,4,64,512]{4,3,2,1,0:T(8,128)(2,1)} %pad_maximum_fusion), channel_id=1, source_target_pairs={{0,1},{16,17},{33,32},{49,48},{2,3},{18,19},{35,34},{51,50},{4,5},... | collective-permute-start | bytes 6291464 | tf_op jit(solution)/shard_map/ppermute | solution.py:238
  134.2 31.8 %collective-permute-done.29.refs_2_ = bf16[8,64,2048]{2,1,0:T(8,128)(2,1)} collective-permute-done((bf16[8,64,2048]{2,1,0:T(8,128)(2,1)S(1)}, bf16[8,64,2048]{2,1,0:T(8,128)(2,1)}, u32[]{:S(2)}, u32[]{:S(2)}) %collective-permute-start.29) | collective-permute-done | bytes 2097184 | tf_op jit(solution)/shard_map/ppermute | solution.py:170
  166.0 1.3 slice.35
  167.3 1.5 collective-permute-start.30
  168.8 1.3 slice.34
  170.8 1.3 slice.37
  172.1 1.8 collective-permute-start.36
  173.9 1.3 slice.36
  175.8 1.5 broadcast_select_fusion
  177.4 3.3 %shard_map.53 = (bf16[32,64,1024]{2,1,0:T(8,128)(2,1)S(1)}, bf16[32,64,1024]{2,1,0:T(8,128)(2,1)S(1)}) custom-call(s32[32]{0:T(128)S(1)} %stack.331.map_ref, s32[2,32]{1,0:T(2,128)S(1)} %pad_add_fusion.1.orders_ref, bf16[32,64,512]{2,1,0:T(8,128)(2,1)S(1)} %bitcast.109), custom_call_target="tpu_custom_call" | custom-call | flops 16777216 | bytes 10485760 | tf_op jit(solution)/shard_map/pallas_call | solution.py:99
  180.7 9.6 %shard_map.54 = (f32[4096,512]{1,0:T(8,128)}, f32[4096,512]{1,0:T(8,128)}) custom-call(bf16[8,64,2048]{2,1,0:T(8,128)(2,1)S(1)} %copy-done.1, bf16[8,64,2048]{2,1,0:T(8,128)(2,1)} %collective-permute-done.33.refs_1_, bf16[8,64,2048]{2,1,0:T(8,128)(2,1)} %collective-permute-done.35.refs_2_, bf16[32,64,1024]{2,1,0:T(8,128)(2,1)S(1)} %get-tuple-element.77.refs_3_.refs_2_), custom_call_target="tpu_custom_call" | custom-call | flops 6442450944 | bytes 17825792 | tf_op jit(solution)/shard_map/pallas_call | solution.py:134
  190.4 9.7 %shard_map.55 = (f32[4096,512]{1,0:T(8,128)}, f32[4096,512]{1,0:T(8,128)}) custom-call(bf16[8,64,2048]{2,1,0:T(8,128)(2,1)S(1)} %shard_map.52.refs_0_, bf16[8,64,2048]{2,1,0:T(8,128)(2,1)} %collective-permute-done.27.refs_1_, bf16[8,64,2048]{2,1,0:T(8,128)(2,1)} %collective-permute-done.29.refs_2_, ...), custom_call_target="tpu_custom_call", output_to_operand_aliasing={{0}: (4, {}), {1}: (5, {})} | custom-call | flops 6442450944 | bytes 17825792 | tf_op jit(solution)/shard_map/pallas_call | solution.py:134
  200.0 7.7 %shard_map.56 = (f32[4096,512]{1,0:T(8,128)}, f32[4096,512]{1,0:T(8,128)}) custom-call(bf16[4,64,2048]{2,1,0:T(8,128)(2,1)S(1)} %collective-permute-done.34.refs_0_, bf16[4,64,2048]{2,1,0:T(8,128)(2,1)S(1)} %collective-permute-done.36.refs_1_, ...), custom_call_target="tpu_custom_call", output_to_operand_aliasing={{0}: (3, {}), {1}: (4, {})} | custom-call | flops 2147483648 | bytes 19922944 | tf_op jit(solution)/shard_map/pallas_call | solution.py:134
  207.7 7.7 %shard_map.57 = (f32[4096,512]{1,0:T(8,128)}, f32[4096,512]{1,0:T(8,128)}) custom-call(bf16[4,64,2048]{2,1,0:T(8,128)(2,1)S(1)} %collective-permute-done.28.refs_0_, bf16[4,64,2048]{2,1,0:T(8,128)(2,1)S(1)} %collective-permute-done.30.refs_1_, ...), custom_call_target="tpu_custom_call", output_to_operand_aliasing={{0}: (3, {}), {1}: (4, {})} | custom-call | flops 2147483648 | bytes 19922944 | tf_op jit(solution)/shard_map/pallas_call | solution.py:134
  (78 shorter events, 16.2 us)
Async XLA Ops:
  0.6 2.0 copy-start.5
  0.6 2.1 copy-start.4
  35.6 4.6 %collective-permute-start.2 = (f32[1,4096]{1,0:T(1,128)S(1)}, f32[1,4096]{1,0:T(1,128)S(1)}, u32[]{:S(2)}, u32[]{:S(2)}) collective-permute-start(f32[1,4096]{1,0:T(1,128)S(1)} %get-tuple-element.44), channel_id=1, source_target_pairs={{0,12},{4,0},{8,4},{12,8},{1,13},{5,1},{9,5},{13,9},{2,14},{6,2},{... | collective-permute-start | bytes 49160 | tf_op jit(solution)/shard_map/ppermute | solution.py:170
  38.5 5.2 %collective-permute-start.1 = (f32[1,4096]{1,0:T(1,128)S(1)}, f32[1,4096]{1,0:T(1,128)S(1)}, u32[]{:S(2)}, u32[]{:S(2)}) collective-permute-start(f32[1,4096]{1,0:T(1,128)S(1)} %get-tuple-element.44), channel_id=1, source_target_pairs={{0,8},{4,12},{8,0},{12,4},{1,9},{5,13},{9,1},{13,5},{2,10},{6,14},... | collective-permute-start | bytes 49160 | tf_op jit(solution)/shard_map/ppermute | solution.py:170
  39.3 4.9 %collective-permute-start = (f32[1,4096]{1,0:T(1,128)S(1)}, f32[1,4096]{1,0:T(1,128)S(1)}, u32[]{:S(2)}, u32[]{:S(2)}) collective-permute-start(f32[1,4096]{1,0:T(1,128)S(1)} %get-tuple-element.44), channel_id=1, source_target_pairs={{0,4},{4,8},{8,12},{12,0},{1,5},{5,9},{9,13},{13,1},{2,6},{6,10},{... | collective-permute-start | bytes 49160 | tf_op jit(solution)/shard_map/ppermute | solution.py:170
  44.3 5.6 %collective-permute-start.5 = (f32[1,4096]{1,0:T(1,128)S(1)}, f32[1,4096]{1,0:T(1,128)S(1)}, u32[]{:S(2)}, u32[]{:S(2)}) collective-permute-start(f32[1,4096]{1,0:T(1,128)S(1)} %add_add_fusion.1), channel_id=1, source_target_pairs={{0,48},{16,0},{32,16},{48,32},{1,49},{17,1},{33,17},{49,33},{2,50}... | collective-permute-start | bytes 49160 | tf_op jit(solution)/shard_map/ppermute | solution.py:170
  48.4 5.2 %collective-permute-start.4 = (f32[1,4096]{1,0:T(1,128)S(1)}, f32[1,4096]{1,0:T(1,128)S(1)}, u32[]{:S(2)}, u32[]{:S(2)}) collective-permute-start(f32[1,4096]{1,0:T(1,128)S(1)} %add_add_fusion.1), channel_id=1, source_target_pairs={{0,32},{16,48},{32,0},{48,16},{1,33},{17,49},{33,1},{49,17},{2,34}... | collective-permute-start | bytes 49160 | tf_op jit(solution)/shard_map/ppermute | solution.py:170
  48.4 5.2 %collective-permute-start.3 = (f32[1,4096]{1,0:T(1,128)S(1)}, f32[1,4096]{1,0:T(1,128)S(1)}, u32[]{:S(2)}, u32[]{:S(2)}) collective-permute-start(f32[1,4096]{1,0:T(1,128)S(1)} %add_add_fusion.1), channel_id=1, source_target_pairs={{0,16},{16,32},{32,48},{48,0},{1,17},{17,33},{33,49},{49,1},{2,18}... | collective-permute-start | bytes 49160 | tf_op jit(solution)/shard_map/ppermute | solution.py:170
  53.7 4.0 %collective-permute-start.6 = (f32[1,4096]{1,0:T(1,128)S(1)}, f32[1,4096]{1,0:T(1,128)S(1)}, u32[]{:S(2)}, u32[]{:S(2)}) collective-permute-start(f32[1,4096]{1,0:T(1,128)S(1)} %add_add_fusion), channel_id=1, source_target_pairs={{0,64},{64,0},{1,65},{65,1},{2,66},{66,2},{3,67},{67,3},{4,68},{68... | collective-permute-start | bytes 49160 | tf_op jit(solution)/shard_map/ppermute | solution.py:170
  58.1 21.7 %collective-permute-start.7 = (bf16[64,4096]{1,0:T(8,128)(2,1)S(1)}, bf16[64,4096]{1,0:T(8,128)(2,1)}, u32[]{:S(2)}, u32[]{:S(2)}) collective-permute-start(bf16[64,4096]{1,0:T(8,128)(2,1)S(1)} %subtract_convert_fusion), channel_id=1, source_target_pairs={{0,64},{64,0},{1,65},{65,1},{2,66},{66,2},{3,67},{67,3},{4,68},{68... | collective-permute-start | bytes 1572872 | tf_op jit(solution)/shard_map/ppermute | solution.py:170
  61.0 7.8 %collective-permute-start.12 = (bf16[2,64,512]{2,1,0:T(8,128)(2,1)S(1)}, bf16[2,64,512]{2,1,0:T(8,128)(2,1)S(1)}, u32[]{:S(2)}, u32[]{:S(2)}) collective-permute-start(bf16[2,64,512]{2,1,0:T(8,128)(2,1)S(1)} %bitcast.118), channel_id=1, source_target_pairs={{0,4},{4,8},{8,12},{12,0},{1,5},{5,9},{9,13},{13,1},{2,6},{6,10},{... | collective-permute-start | bytes 393224 | tf_op jit(solution)/shard_map/ppermute | solution.py:170
  61.1 7.8 %collective-permute-start.13 = (bf16[2,64,512]{2,1,0:T(8,128)(2,1)S(1)}, bf16[2,64,512]{2,1,0:T(8,128)(2,1)S(1)}, u32[]{:S(2)}, u32[]{:S(2)}) collective-permute-start(bf16[2,64,512]{2,1,0:T(8,128)(2,1)S(1)} %bitcast.117), channel_id=1, source_target_pairs={{0,8},{4,12},{8,0},{12,4},{1,9},{5,13},{9,1},{13,5},{2,10},{6,14},... | collective-permute-start | bytes 393224 | tf_op jit(solution)/shard_map/ppermute | solution.py:170
  62.8 9.4 %collective-permute-start.14 = (bf16[2,64,512]{2,1,0:T(8,128)(2,1)S(1)}, bf16[2,64,512]{2,1,0:T(8,128)(2,1)S(1)}, u32[]{:S(2)}, u32[]{:S(2)}) collective-permute-start(bf16[2,64,512]{2,1,0:T(8,128)(2,1)S(1)} %bitcast.116), channel_id=1, source_target_pairs={{0,12},{4,0},{8,4},{12,8},{1,13},{5,1},{9,5},{13,9},{2,14},{6,2},{... | collective-permute-start | bytes 393224 | tf_op jit(solution)/shard_map/ppermute | solution.py:170
  65.3 7.0 %collective-permute-start.11 = (bf16[64,2048]{1,0:T(8,128)(2,1)S(1)}, bf16[64,2048]{1,0:T(8,128)(2,1)S(1)}, u32[]{:S(2)}, u32[]{:S(2)}) collective-permute-start(bf16[64,2048]{1,0:T(8,128)(2,1)S(1)} %get-tuple-element.65.refs_0_), channel_id=1, source_target_pairs={{0,48},{16,0},{32,16},{48,32},{1,49},{17,1},{33,17},{49,33},{2,50}... | collective-permute-start | bytes 786440 | tf_op jit(solution)/shard_map/ppermute | solution.py:170
  68.8 7.6 %collective-permute-start.10 = (bf16[64,2048]{1,0:T(8,128)(2,1)S(1)}, bf16[64,2048]{1,0:T(8,128)(2,1)S(1)}, u32[]{:S(2)}, u32[]{:S(2)}) collective-permute-start(bf16[64,2048]{1,0:T(8,128)(2,1)S(1)} %get-tuple-element.65.refs_0_), channel_id=1, source_target_pairs={{0,16},{16,32},{32,48},{48,0},{1,17},{17,33},{33,49},{49,1},{2,18}... | collective-permute-start | bytes 786440 | tf_op jit(solution)/shard_map/ppermute | solution.py:170
  68.9 7.5 %collective-permute-start.9 = (bf16[64,2048]{1,0:T(8,128)(2,1)S(1)}, bf16[64,2048]{1,0:T(8,128)(2,1)S(1)}, u32[]{:S(2)}, u32[]{:S(2)}) collective-permute-start(bf16[64,2048]{1,0:T(8,128)(2,1)S(1)} %get-tuple-element.45.refs_0_), channel_id=1, source_target_pairs={{0,12},{4,0},{8,4},{12,8},{1,13},{5,1},{9,5},{13,9},{2,14},{6,2},{... | collective-permute-start | bytes 786440 | tf_op jit(solution)/shard_map/ppermute | solution.py:170
  72.2 7.6 %collective-permute-start.8 = (bf16[64,2048]{1,0:T(8,128)(2,1)S(1)}, bf16[64,2048]{1,0:T(8,128)(2,1)S(1)}, u32[]{:S(2)}, u32[]{:S(2)}) collective-permute-start(bf16[64,2048]{1,0:T(8,128)(2,1)S(1)} %get-tuple-element.45.refs_0_), channel_id=1, source_target_pairs={{0,4},{4,8},{8,12},{12,0},{1,5},{5,9},{9,13},{13,1},{2,6},{6,10},{... | collective-permute-start | bytes 786440 | tf_op jit(solution)/shard_map/ppermute | solution.py:170
  79.8 25.2 %copy-start.2 = (bf16[64,2048]{1,0:T(8,128)(2,1)}, bf16[64,2048]{1,0:T(8,128)(2,1)S(1)}, u32[]{:S(2)}) copy-start(bf16[64,2048]{1,0:T(8,128)(2,1)S(1)} %collective-permute-done.8.refs_1_) | copy-start | bytes 786436
  80.0 11.0 %collective-permute-start.21 = (bf16[4,64,512]{2,1,0:T(8,128)(2,1)S(1)}, bf16[4,64,512]{2,1,0:T(8,128)(2,1)S(1)}, u32[]{:S(2)}, u32[]{:S(2)}) collective-permute-start(bf16[4,64,512]{2,1,0:T(8,128)(2,1)S(1)} %get-tuple-element.85), channel_id=1, source_target_pairs={{1,49},{16,0},{32,16},{49,33},{3,51},{18,2},{34,18},{51,35},{5,53}... | collective-permute-start | bytes 786440 | tf_op jit(solution)/shard_map/ppermute | solution.py:222
  81.3 10.2 %collective-permute-start.20 = (bf16[4,64,512]{2,1,0:T(8,128)(2,1)S(1)}, bf16[4,64,512]{2,1,0:T(8,128)(2,1)S(1)}, u32[]{:S(2)}, u32[]{:S(2)}) collective-permute-start(bf16[4,64,512]{2,1,0:T(8,128)(2,1)S(1)} %get-tuple-element.86), channel_id=1, source_target_pairs={{1,33},{17,49},{32,0},{48,16},{3,35},{19,51},{34,2},{50,18},{5,37}... | collective-permute-start | bytes 786440 | tf_op jit(solution)/shard_map/ppermute | solution.py:222
  82.6 11.6 %collective-permute-start.19 = (bf16[4,64,512]{2,1,0:T(8,128)(2,1)S(1)}, bf16[4,64,512]{2,1,0:T(8,128)(2,1)S(1)}, u32[]{:S(2)}, u32[]{:S(2)}) collective-permute-start(bf16[4,64,512]{2,1,0:T(8,128)(2,1)S(1)} %get-tuple-element.87), channel_id=1, source_target_pairs={{0,16},{17,33},{33,49},{48,0},{2,18},{19,35},{35,51},{50,2},{4,20}... | collective-permute-start | bytes 786440 | tf_op jit(solution)/shard_map/ppermute | solution.py:222
  88.2 7.0 %collective-permute-start.18 = (bf16[64,2048]{1,0:T(8,128)(2,1)S(1)}, bf16[64,2048]{1,0:T(8,128)(2,1)S(1)}, u32[]{:S(2)}, u32[]{:S(2)}) collective-permute-start(bf16[64,2048]{1,0:T(8,128)(2,1)S(1)} %get-tuple-element.68.refs_4_), channel_id=1, source_target_pairs={{0,48},{16,0},{32,16},{48,32},{1,49},{17,1},{33,17},{49,33},{2,50}... | collective-permute-start | bytes 786440 | tf_op jit(solution)/shard_map/ppermute | solution.py:170
  91.0 7.6 %collective-permute-start.17 = (bf16[64,2048]{1,0:T(8,128)(2,1)S(1)}, bf16[64,2048]{1,0:T(8,128)(2,1)S(1)}, u32[]{:S(2)}, u32[]{:S(2)}) collective-permute-start(bf16[64,2048]{1,0:T(8,128)(2,1)S(1)} %get-tuple-element.68.refs_4_), channel_id=1, source_target_pairs={{0,16},{16,32},{32,48},{48,0},{1,17},{17,33},{33,49},{49,1},{2,18}... | collective-permute-start | bytes 786440 | tf_op jit(solution)/shard_map/ppermute | solution.py:170
  91.0 8.0 %collective-permute-start.16 = (bf16[64,2048]{1,0:T(8,128)(2,1)S(1)}, bf16[64,2048]{1,0:T(8,128)(2,1)S(1)}, u32[]{:S(2)}, u32[]{:S(2)}) collective-permute-start(bf16[64,2048]{1,0:T(8,128)(2,1)S(1)} %get-tuple-element.62.refs_4_), channel_id=1, source_target_pairs={{0,12},{4,0},{8,4},{12,8},{1,13},{5,1},{9,5},{13,9},{2,14},{6,2},{... | collective-permute-start | bytes 786440 | tf_op jit(solution)/shard_map/ppermute | solution.py:170
  91.5 8.7 %collective-permute-start.15 = (bf16[64,2048]{1,0:T(8,128)(2,1)S(1)}, bf16[64,2048]{1,0:T(8,128)(2,1)S(1)}, u32[]{:S(2)}, u32[]{:S(2)}) collective-permute-start(bf16[64,2048]{1,0:T(8,128)(2,1)S(1)} %get-tuple-element.62.refs_4_), channel_id=1, source_target_pairs={{0,4},{4,8},{8,12},{12,0},{1,5},{5,9},{9,13},{13,1},{2,6},{6,10},{... | collective-permute-start | bytes 786440 | tf_op jit(solution)/shard_map/ppermute | solution.py:170
  100.2 18.7 %collective-permute-start.26 = (bf16[4,4,64,512]{3,2,1,0:T(8,128)(2,1)}, bf16[4,4,64,512]{3,2,1,0:T(8,128)(2,1)}, u32[]{:S(2)}, u32[]{:S(2)}) collective-permute-start(bf16[4,4,64,512]{3,2,1,0:T(8,128)(2,1)} %pad_maximum_fusion.1), channel_id=1, source_target_pairs={{0,2},{64,0},{2,66},{66,64},{16,18},{80,16},{18,82},{82,80},{33,35... | collective-permute-start | bytes 3145736 | tf_op jit(solution)/shard_map/ppermute | solution.py:232
  105.0 8.6 %collective-permute-start.22 = (bf16[64,2048]{1,0:T(8,128)(2,1)S(1)}, bf16[64,2048]{1,0:T(8,128)(2,1)S(1)}, u32[]{:S(2)}, u32[]{:S(2)}) collective-permute-start(bf16[64,2048]{1,0:T(8,128)(2,1)S(1)} %collective-permute-done.8.refs_1_), channel_id=1, source_target_pairs={{0,4},{4,8},{8,12},{12,0},{1,5},{5,9},{9,13},{13,1},{2,6},{6,10},{... | collective-permute-start | bytes 786440 | tf_op jit(solution)/shard_map/ppermute | solution.py:170
  105.1 9.9 %collective-permute-start.23 = (bf16[64,2048]{1,0:T(8,128)(2,1)S(1)}, bf16[64,2048]{1,0:T(8,128)(2,1)S(1)}, u32[]{:S(2)}, u32[]{:S(2)}) collective-permute-start(bf16[64,2048]{1,0:T(8,128)(2,1)S(1)} %collective-permute-done.16.refs_6_), channel_id=1, source_target_pairs={{0,12},{4,0},{8,4},{12,8},{1,13},{5,1},{9,5},{13,9},{2,14},{6,2},{... | collective-permute-start | bytes 786440 | tf_op jit(solution)/shard_map/ppermute | solution.py:170
  108.3 7.6 %collective-permute-start.24 = (bf16[64,2048]{1,0:T(8,128)(2,1)S(1)}, bf16[64,2048]{1,0:T(8,128)(2,1)S(1)}, u32[]{:S(2)}, u32[]{:S(2)}) collective-permute-start(bf16[64,2048]{1,0:T(8,128)(2,1)S(1)} %collective-permute-done.10.refs_1_), channel_id=1, source_target_pairs={{0,16},{16,32},{32,48},{48,0},{1,17},{17,33},{33,49},{49,1},{2,18}... | collective-permute-start | bytes 786440 | tf_op jit(solution)/shard_map/ppermute | solution.py:170
  109.7 9.2 %collective-permute-start.25 = (bf16[64,2048]{1,0:T(8,128)(2,1)S(1)}, bf16[64,2048]{1,0:T(8,128)(2,1)S(1)}, u32[]{:S(2)}, u32[]{:S(2)}) collective-permute-start(bf16[64,2048]{1,0:T(8,128)(2,1)S(1)} %collective-permute-done.18.refs_6_), channel_id=1, source_target_pairs={{0,48},{16,0},{32,16},{48,32},{1,49},{17,1},{33,17},{49,33},{2,50}... | collective-permute-start | bytes 786440 | tf_op jit(solution)/shard_map/ppermute | solution.py:170
  118.8 1.0 copy-start.3
  119.9 1.3 copy-start
  121.4 5.7 %collective-permute-start.31 = (bf16[4,4,64,512]{3,2,1,0:T(8,128)(2,1)}, bf16[4,4,64,512]{3,2,1,0:T(8,128)(2,1)}, u32[]{:S(2)}, u32[]{:S(2)}) collective-permute-start(bf16[4,4,64,512]{3,2,1,0:T(8,128)(2,1)} %pad_maximum_fusion.1), channel_id=1, source_target_pairs={{64,2},{2,64},{80,18},{18,80},{97,35},{35,97},{113,51},{51,113},{6... | collective-permute-start | bytes 3145736 | tf_op jit(solution)/shard_map/ppermute | solution.py:232
  123.0 42.9 %collective-permute-start.29 = (bf16[8,64,2048]{2,1,0:T(8,128)(2,1)S(1)}, bf16[8,64,2048]{2,1,0:T(8,128)(2,1)}, u32[]{:S(2)}, u32[]{:S(2)}) collective-permute-start(bf16[8,64,2048]{2,1,0:T(8,128)(2,1)S(1)} %shard_map.52.refs_0_), channel_id=1, source_target_pairs={{0,12},{4,0},{8,4},{12,8},{1,13},{5,1},{9,5},{13,9},{2,14},{6,2},{... | collective-permute-start | bytes 6291464 | tf_op jit(solution)/shard_map/ppermute | solution.py:170
  123.0 45.8 %collective-permute-start.27 = (bf16[8,64,2048]{2,1,0:T(8,128)(2,1)S(1)}, bf16[8,64,2048]{2,1,0:T(8,128)(2,1)}, u32[]{:S(2)}, u32[]{:S(2)}) collective-permute-start(bf16[8,64,2048]{2,1,0:T(8,128)(2,1)S(1)} %shard_map.52.refs_0_), channel_id=1, source_target_pairs={{0,4},{4,8},{8,12},{12,0},{1,5},{5,9},{9,13},{13,1},{2,6},{6,10},{... | collective-permute-start | bytes 6291464 | tf_op jit(solution)/shard_map/ppermute | solution.py:170
  125.1 45.7 %collective-permute-start.35 = (bf16[8,64,2048]{2,1,0:T(8,128)(2,1)}, bf16[8,64,2048]{2,1,0:T(8,128)(2,1)}, u32[]{:S(2)}, u32[]{:S(2)}) collective-permute-start(bf16[8,64,2048]{2,1,0:T(8,128)(2,1)} %copy-done), channel_id=1, source_target_pairs={{0,48},{16,0},{32,16},{48,32},{1,49},{17,1},{33,17},{49,33},{2,50}... | collective-permute-start | bytes 6291464 | tf_op jit(solution)/shard_map/ppermute | solution.py:170
  125.3 48.6 %collective-permute-start.33 = (bf16[8,64,2048]{2,1,0:T(8,128)(2,1)}, bf16[8,64,2048]{2,1,0:T(8,128)(2,1)}, u32[]{:S(2)}, u32[]{:S(2)}) collective-permute-start(bf16[8,64,2048]{2,1,0:T(8,128)(2,1)} %copy-done), channel_id=1, source_target_pairs={{0,16},{16,32},{32,48},{48,0},{1,17},{17,33},{33,49},{49,1},{2,18}... | collective-permute-start | bytes 6291464 | tf_op jit(solution)/shard_map/ppermute | solution.py:170
  131.2 44.7 %collective-permute-start.32 = (bf16[2,4,4,64,512]{4,3,2,1,0:T(8,128)(2,1)}, bf16[2,4,4,64,512]{4,3,2,1,0:T(8,128)(2,1)}, u32[]{:S(2)}, u32[]{:S(2)}) collective-permute-start(bf16[2,4,4,64,512]{4,3,2,1,0:T(8,128)(2,1)} %pad_maximum_fusion), channel_id=1, source_target_pairs={{0,1},{16,17},{33,32},{49,48},{2,3},{18,19},{35,34},{51,50},{4,5},... | collective-permute-start | bytes 6291464 | tf_op jit(solution)/shard_map/ppermute | solution.py:238
  167.3 40.4 %collective-permute-start.30 = (bf16[4,64,2048]{2,1,0:T(8,128)(2,1)S(1)}, bf16[4,64,2048]{2,1,0:T(8,128)(2,1)S(1)}, u32[]{:S(2)}, u32[]{:S(2)}) collective-permute-start(bf16[4,64,2048]{2,1,0:T(8,128)(2,1)S(1)} %slice.35), channel_id=1, source_target_pairs={{0,12},{4,0},{8,4},{12,8},{1,13},{5,1},{9,5},{13,9},{2,14},{6,2},{... | collective-permute-start | bytes 3145736 | tf_op jit(solution)/shard_map/ppermute | solution.py:170
  170.2 37.5 %collective-permute-start.28 = (bf16[4,64,2048]{2,1,0:T(8,128)(2,1)S(1)}, bf16[4,64,2048]{2,1,0:T(8,128)(2,1)S(1)}, u32[]{:S(2)}, u32[]{:S(2)}) collective-permute-start(bf16[4,64,2048]{2,1,0:T(8,128)(2,1)S(1)} %slice.34), channel_id=1, source_target_pairs={{0,4},{4,8},{8,12},{12,0},{1,5},{5,9},{9,13},{13,1},{2,6},{6,10},{... | collective-permute-start | bytes 3145736 | tf_op jit(solution)/shard_map/ppermute | solution.py:170
  172.1 27.9 %collective-permute-start.36 = (bf16[4,64,2048]{2,1,0:T(8,128)(2,1)S(1)}, bf16[4,64,2048]{2,1,0:T(8,128)(2,1)S(1)}, u32[]{:S(2)}, u32[]{:S(2)}) collective-permute-start(bf16[4,64,2048]{2,1,0:T(8,128)(2,1)S(1)} %slice.37), channel_id=1, source_target_pairs={{0,48},{16,0},{32,16},{48,32},{1,49},{17,1},{33,17},{49,33},{2,50}... | collective-permute-start | bytes 3145736 | tf_op jit(solution)/shard_map/ppermute | solution.py:170
  175.3 24.8 %collective-permute-start.34 = (bf16[4,64,2048]{2,1,0:T(8,128)(2,1)S(1)}, bf16[4,64,2048]{2,1,0:T(8,128)(2,1)S(1)}, u32[]{:S(2)}, u32[]{:S(2)}) collective-permute-start(bf16[4,64,2048]{2,1,0:T(8,128)(2,1)S(1)} %slice.36), channel_id=1, source_target_pairs={{0,16},{16,32},{32,48},{48,0},{1,17},{17,33},{33,49},{49,1},{2,18}... | collective-permute-start | bytes 3145736 | tf_op jit(solution)/shard_map/ppermute | solution.py:170
  177.3 3.4 %copy-start.1 = (bf16[8,64,2048]{2,1,0:T(8,128)(2,1)S(1)}, bf16[8,64,2048]{2,1,0:T(8,128)(2,1)}, u32[]{:S(2)}) copy-start(bf16[8,64,2048]{2,1,0:T(8,128)(2,1)} %copy-done) | copy-start | bytes 6291460

commit v3 on v2

--- a/solution.py
+++ b/solution.py
@@ -77,92 +77,103 @@
     )(indices, coords.reshape(pieces * frames, residues))
 
 
-def column_kernel(map_ref, orders_ref, cols_ref, *out_refs):
-    blocks, frames, width = cols_ref.shape
-
-    @pl.loop(0, blocks)
-    def _(number):
-        for stream, out_ref in enumerate(out_refs):
-            block = orders_ref[stream, number]
-            here = cols_ref[map_ref[block]].astype(jnp.float32)
-            before = cols_ref[map_ref[jnp.maximum(block - 1, 0)]].astype(jnp.float32)
-            after = cols_ref[map_ref[jnp.minimum(block + 1, blocks - 1)]].astype(jnp.float32)
+def column_kernel(map_ref, places_ref, own_ref, passed_ref, *out_refs):
+    blocks, frames, width = own_ref.shape
+
+    def fill(cols_ref, skipped):
+        def block_at(number):
+            return cols_ref[map_ref[number] - skipped].astype(jnp.float32)
+
+        @pl.loop(0, blocks)
+        def _(block):
+            here = block_at(block)
+            before = block_at(jnp.maximum(block - 1, 0))
+            after = block_at(jnp.minimum(block + 1, blocks - 1))
             inner = jnp.logical_and(block > 0, block < blocks - 1)
-            out_ref[number, :, :width] = jnp.where(inner, 2.0 * here, here).astype(jnp.bfloat16)
+            weighted = jnp.where(inner, 2.0 * here, here).astype(jnp.bfloat16)
             lagged = jnp.where(block > 0, before, 0.0) + jnp.where(block < blocks - 1, after, 0.0)
-            out_ref[number, :, width:] = lagged.astype(jnp.bfloat16)
-
-
-def lagged_columns(block_map, orders, cols):
-    blocks, frames, width = cols.shape
+            lagged = lagged.astype(jnp.bfloat16)
+            for stream, out_ref in enumerate(out_refs):
+                out_ref[places_ref[stream, block], :, :width] = weighted
+                out_ref[places_ref[stream, block], :, width:] = lagged
+
+    pl.when(map_ref[0] < blocks)(lambda: fill(own_ref, 0))
+    pl.when(map_ref[0] >= blocks)(lambda: fill(passed_ref, blocks))
+
+
+def lagged_columns(block_map, places, own, passed):
+    blocks, frames, width = own.shape
     out = jax.ShapeDtypeStruct((blocks, frames, 2 * width), jnp.bfloat16)
     return pl.pallas_call(
         column_kernel,
         out_shape=(out, out),
-        in_specs=[pl.BlockSpec(memory_space=pltpu.SMEM)] * 2 + [pl.BlockSpec(memory_space=pltpu.VMEM)],
+        in_specs=[pl.BlockSpec(memory_space=pltpu.SMEM)] * 2 + [pl.BlockSpec(memory_space=pltpu.VMEM)] * 2,
         out_specs=[pl.BlockSpec(memory_space=pltpu.VMEM)] * 2,
-        compiler_params=pltpu.CompilerParams(vmem_limit_bytes=24 * MIB),
-        cost_estimate=pl.CostEstimate(flops=16 * cols.size, bytes_accessed=10 * cols.size, transcendentals=0),
-    )(block_map, orders, cols)
-
-
-def product_kernel(count, factor, added, *refs):
+        compiler_params=pltpu.CompilerParams(vmem_limit_bytes=20 * MIB),
+        cost_estimate=pl.CostEstimate(flops=16 * own.size, bytes_accessed=12 * own.size, transcendentals=0),
+    )(block_map, places, own, passed)
+
+
+def product_kernel(count, factor, started, *refs):
     pieces, columns_ref = refs[:count], refs[count]
-    c00_ref, c0t_ref = refs[-2:]
-    width = c00_ref.shape[1]
+    outs = refs[-2:]
+    width = outs[0].shape[1]
     left = jnp.concatenate([piece[...].reshape(-1, piece.shape[2]) for piece in pieces], axis=0)
     right = columns_ref[...].reshape(left.shape[0], 2 * width)
     sums = lax.dot_general(left, right, (((0,), (0,)), ((), ())), preferred_element_type=jnp.float32)
-    for number, ref in enumerate((c00_ref, c0t_ref)):
-        part = sums[:, number * width : (number + 1) * width] * factor
-        ref[...] = part + refs[count + 1 + number][...] if added else part
-
-
-def products(pieces, columns, column_start, row_start, rows, factor, previous, added):
+    for number, ref in enumerate(outs):
+        part = sums[:, number * width : (number + 1) * width]
+        ref[...] = (part + refs[count + 1 + number][...]) * factor if started else part
+
+
+def products(pieces, columns, column_start, start=None, row_start=0, rows=None, factor=1.0, previous=()):
     _, frames, double = columns.shape
     width = double // 2
     features = pieces[0].shape[2]
     first = row_start // TILE
-    out = jax.ShapeDtypeStruct((rows, width), jnp.float32)
+    started = start is not None
+    out = jax.ShapeDtypeStruct((rows if started else features, width), jnp.float32)
     count = len(pieces)
     blocks = sum(piece.shape[0] for piece in pieces)
-    passed = () if previous is None else previous
-    out_spec = pl.BlockSpec((TILE, width), lambda i: (first + i, 0))
     in_specs = [pl.BlockSpec((piece.shape[0], frames, TILE), lambda i: (0, 0, i)) for piece in pieces]
-    in_specs += [pl.BlockSpec((blocks, frames, double), lambda i: (column_start // blocks, 0, 0))]
-    in_specs += [out_spec if added else pl.BlockSpec(memory_space=pl.ANY)] * len(passed)
+    in_specs += [
+        pl.BlockSpec(
+            (blocks, frames, double), lambda i: (column_start // blocks, 0, 0), pipeline_mode=pl.Buffered(1)
+        )
+    ]
+    in_specs += [pl.BlockSpec((TILE, width), lambda i: (i, 0))] * (2 * started)
+    in_specs += [pl.BlockSpec(memory_space=pl.ANY)] * len(previous)
     return pl.pallas_call(
-        lambda *refs: product_kernel(count, factor, added, *refs),
+        lambda *refs: product_kernel(count, factor, started, *refs),
         grid=(features // TILE,),
         in_specs=in_specs,
-        out_specs=[out_spec] * 2,
+        out_specs=[pl.BlockSpec((TILE, width), lambda i: (first + i, 0))] * 2,
         out_shape=(out, out),
-        input_output_aliases={count + 1 + n: n for n in range(len(passed))},
-        compiler_params=pltpu.CompilerParams(vmem_limit_bytes=36 * MIB),
+        input_output_aliases={count + 3 + n: n for n in range(len(previous))},
+        compiler_params=pltpu.CompilerParams(vmem_limit_bytes=16 * MIB),
         cost_estimate=pl.CostEstimate(
-            flops=2 * features * blocks * frames * double,
-            bytes_accessed=features * double * (8 if added else 4) + blocks * frames * (features + double) * 2,
+            flops=4 * features * blocks * frames * double,
+            bytes_accessed=features * double * (8 if started else 4) + blocks * frames * (features + double) * 2,
             transcendentals=0,
         ),
-    )(*pieces, columns, *passed)
-
-
-def plane_kernel(*refs):
-    for number, ref in enumerate(refs[:-1]):
-        refs[-1][number] = ref[...]
-
-
-def plane_of(blocks):
+    )(*pieces, columns, *(start or ()), *previous)
+
+
+def plane_kernel(own_ref, behind_ref, ahead_ref, first_ref, last_ref, out_ref):
+    for number, far_ref in enumerate((first_ref, last_ref)):
+        for at, block in enumerate((own_ref[number], behind_ref[number], ahead_ref[number], far_ref[...])):
+            out_ref[4 * number + at] = block
+
+
+def plane_of(own, behind, ahead, far):
     return pl.pallas_call(
         plane_kernel,
-        out_shape=jax.ShapeDtypeStruct((len(blocks), *blocks[0].shape), blocks[0].dtype),
-        in_specs=[pl.BlockSpec(memory_space=pltpu.VMEM)] * len(blocks),
+        out_shape=jax.ShapeDtypeStruct((8, *own.shape[1:]), own.dtype),
+        in_specs=[pl.BlockSpec(memory_space=pltpu.VMEM)] * 5,
         out_specs=pl.BlockSpec(memory_space=pltpu.VMEM),
         compiler_params=pltpu.CompilerParams(vmem_limit_bytes=16 * MIB),
-        cost_estimate=pl.CostEstimate(
-            flops=0, bytes_accessed=4 * len(blocks) * blocks[0].size, transcendentals=0
-        ),
-    )(*blocks)
+        cost_estimate=pl.CostEstimate(flops=0, bytes_accessed=16 * own.size, transcendentals=0),
+    )(own, behind, ahead, *far)
 
 
 def moved(array, axis, by):
@@ -189,14 +200,19 @@
     return moved(behind[:half], axis, 1), moved(ahead[half:], axis, -1)
 
 
-def block_order(first, second, place):
-    order = []
-    for offset in OFFSETS:
-        for yl in (place["yl"], 1 - place["yl"]):
-            for inner in OFFSETS:
-                at = {first: (place[first] + inner) % 4, second: (place[second] + offset) % 4}
-                order.append(yl * 16 + at["z"] * 4 + at["x"])
-    return jnp.stack(order).astype(jnp.int32)
+def block_places(first, second, place):
+    def number(at, own):
+        ahead = (at - own) % 4
+        return jnp.where(ahead == 0, 0, jnp.where(ahead == 3, 1, ahead + 1))
+
+    places = []
+    for block in range(32):
+        at = {"z": (block // 4) % 4, "x": block % 4}
+        partner = jnp.where(place["yl"] == block // 16, 0, 4)
+        places.append(
+            number(at[second], place[second]) * 8 + partner + number(at[first], place[first])
+        )
+    return jnp.stack(places).astype(jnp.int32)
 
 
 def columns_along_x(centered, place):
@@ -236,13 +252,14 @@
     both = jnp.stack([one, two])
     pairs = [(z * 2 + z // 2, z * 2 + 1 - z // 2) for z in range(4)]
     passed = lax.ppermute(both, ("z", "c"), pairs)
-    both = jnp.where(place["z"] // 2 == place["c"], both, passed)
+    skipped = jnp.where(place["z"] // 2 == place["c"], 0, 32)
     order = []
     for block in range(32):
         y, z, x = block // 16, (block // 4) % 4, block % 4
         group = jnp.where(y == 1 - place["yh"], 0, 1)
-        order.append(group * 16 + ((place["z"] - z) % 4) * 4 + (place["x"] - x) % 4)
-    return both.reshape(32, *both.shape[3:]), jnp.stack(order).astype(jnp.int32)
+        order.append(skipped + group * 16 + ((place["z"] - z) % 4) * 4 + (place["x"] - x) % 4)
+    own, passed = [part.reshape(32, *part.shape[3:]) for part in (both, passed)]
+    return own, passed, jnp.stack(order).astype(jnp.int32)
 
 
 def together(*groups):
@@ -271,41 +288,36 @@
     ways = (("x", "z"), ("z", "x"))
     taken = (slice(0, half), slice(half, rows))
 
-    own = [centered[:, part] for part in taken]
     partner = moved(centered, "yl", 1)
-    own_near = [near_blocks(block, way[0]) for block, way in zip(own, ways)]
     along_x = columns_along_x(centered, place)
-    partner, own_near, own, along_x = together(partner, own_near, own, along_x)
-
-    other = [partner[:, part] for part in taken]
-    other_near = [near_blocks(block, way[0]) for block, way in zip(other, ways)]
+    partner, along_x = together(partner, along_x)
+
+    pairs_of = [jnp.stack([centered[:, part], partner[:, part]]) for part in taken]
+    pair_near = [near_blocks(pair, way[0]) for pair, way in zip(pairs_of, ways)]
     along_z = jnp.stack(columns_along_z(along_x, place))
-    other_near, along_z, own_near, other = together(other_near, along_z, own_near, other)
+    pair_near, along_z, pairs_of = together(pair_near, along_z, pairs_of)
 
     far = [
-        (moved(mine[0], way[0], 1), moved(theirs[1], way[0], -1))
-        for mine, theirs, way in zip(own_near, other_near, ways)
+        (moved(behind[0], way[0], 1), moved(ahead[1], way[0], -1)) for (behind, ahead), way in zip(pair_near, ways)
     ]
-    one = columns_along_y(along_z, [(0, 2), (1, 0), (2, 3), (3, 1)])
-    far, along_z, one = together(far, along_z, one)
-
-    planes = [
-        plane_of([own[n], *own_near[n], far[n][0], other[n], *other_near[n], far[n][1]]) for n in range(2)
-    ]
+    two = columns_along_y(along_z, [(1, 2), (2, 1)])
+    far, along_z, two = together(far, along_z, two)
+
+    planes = [plane_of(pairs_of[n], *pair_near[n], far[n]) for n in range(2)]
     planes, along_z = together(planes, along_z)
     near = [near_blocks(plane, way[1]) for plane, way in zip(planes, ways)]
-    two = columns_along_y(along_z, [(1, 2), (2, 1)])
+    one = columns_along_y(along_z, [(0, 2), (1, 0), (2, 3), (3, 1)])
     two = jnp.where(place["yl"] == place["yh"], along_z, two)
-    cols, col_order = columns_of_chip(one, two, place)
-    orders = jnp.stack([block_order(*way, place) for way in ways])
-    columns = lagged_columns(col_order, orders, cols)
+    own_cols, passed_cols, col_order = columns_of_chip(one, two, place)
+    places = jnp.stack([block_places(*way, place) for way in ways])
+    columns = lagged_columns(col_order, places, own_cols, passed_cols)
 
     last = [far_block(*blocks, way[1]) for blocks, way in zip(near, ways)]
-    results = None
+    starts = [products([planes[n], *near[n]], columns[n], 0) for n in range(2)]
+    starts, last = together(starts, last)
+    results = ()
     for n in range(2):
-        results = products([planes[n], *near[n]], columns[n], 0, n * half, rows, 0.5 / pairs, results, False)
-    for n in range(2):
-        results = products(last[n], columns[n], 24, n * half, rows, 0.5 / pairs, results, True)
+        results = products(last[n], columns[n], 24, starts[n], n * half, rows, 0.5 / pairs, results)
     return results
 
 

time: 217 us -> 201 us (0.926)
  other arithmetic: 6.98 us -> 0.84 us
  Pallas kernels: 71 us -> 65 us
  starting transfers between devices: 57.8 us -> 62.6 us
  waiting for transfers between devices: 65.9 us -> 61.5 us
  local copies, waits for them, and re-layouts: 12.8 us -> 9.55 us
    ppermute x31 -> x27, waiting for transfers between devices: 64.7 us -> 46.7 us  [moved(): lax.ppermute(array, axis, [(i, (i + by) % length) for i in range(length)])]
    ppermute x2, waiting for transfers between devices: 0.01 us -> 6.85 us  [columns_along_y(): return lax.ppermute(along_z, ('yl', 'z', 'yh', 'c'), pairs)]
    ppermute x3, waiting for transfers between devices: 1.13 us -> 7.93 us  [columns_along_z(): along_z.append(lax.ppermute(piece, ('z', 'c'), pairs))]
    pallas_call x6, Pallas kernels: 34.9 us -> 29.2 us  [the longest x4 26.3 us: products(): pl.pallas_call(lambda *refs: product_kernel(count, factor, started, *refs...]
    ppermute x31 -> x27, starting transfers between devices: 41.6 us -> 45.7 us  [moved(): lax.ppermute(array, axis, [(i, (i + by) % length) for i in range(length)])]
    another operation x2, other arithmetic: 4.08 us -> 0.3 us  [columns_of_chip(): both = jnp.stack([one, two])]
    unnamed x16 -> x8, local copies, waits for them, and re-layouts: 2.45 us -> 0.18 us
  transfers between devices with their start and end apart: 37 -> 33, of which waited for: 17 -> 16; matrix products, arithmetic and copies ran while one was open for 7% -> 4% of each run, Pallas kernels for 14% -> 10%
where the time goes in v3:
time: 201 us
  Pallas kernels  65 us (32%)
  starting transfers between devices  62.6 us (31%)
  waiting for transfers between devices  61.5 us (31%)
  local copies, waits for them, and re-layouts  9.55 us (5%)
    ppermute x27, waiting for transfers between devices, moved(): lax.ppermute(array, axis, [(i, (i + by) % length) for i in range(length)])  46.7 us
    ppermute x27, starting transfers between devices, moved(): lax.ppermute(array, axis, [(i, (i + by) % length) for i in range(length)])  45.7 us
    pallas_call x1, Pallas kernels, contact_features(): pl.pallas_call(feature_kernel, out_shape=(jax.ShapeDtypeStruct((frames, w...  32.8 us
    pallas_call x4, Pallas kernels, products(): pl.pallas_call(lambda *refs: product_kernel(count, factor, started, *refs...  26.3 us
    ppermute x2, starting transfers between devices, columns_along_y(): return lax.ppermute(along_z, ('yl', 'z', 'yh', 'c'), pairs)  7.98 us
    ppermute x3, waiting for transfers between devices, columns_along_z(): along_z.append(lax.ppermute(piece, ('z', 'c'), pairs))  7.93 us
    ppermute x2, waiting for transfers between devices, columns_along_y(): return lax.ppermute(along_z, ('yl', 'z', 'yh', 'c'), pairs)  6.85 us
    ppermute x3, starting transfers between devices, columns_along_z(): along_z.append(lax.ppermute(piece, ('z', 'c'), pairs))  6.31 us
  transfers between devices with their start and end apart: 33, of which 16 were waited for; matrix products, arithmetic and copies ran while one was open for 4% of the time, Pallas kernels for 10%

profile of v3, /device:TPU:0, one launch (start us, length us, event | category | flops | bytes accessed | tf_op | source)
XLA Modules:
  0.0 200.6 jit_solution(445268095636173897)
XLA Ops:
  0.7 1.9 copy.11
  2.8 32.8 %shard_map.50 = (f32[64,4096]{1,0:T(8,128)S(1)}, f32[1,4096]{1,0:T(1,128)S(1)}) custom-call(s32[8,256]{1,0:T(8,128)S(1)} %stack.370.index_ref, f32[1536,256]{1,0:T(8,128)S(1)} %bitcast.159), custom_call_target="tpu_custom_call" | custom-call | flops 201326592 | bytes 4194304 | tf_op jit(solution)/shard_map/pallas_call | solution.py:66
  35.6 2.9 %collective-permute-start.2 = (f32[1,4096]{1,0:T(1,128)S(1)}, f32[1,4096]{1,0:T(1,128)S(1)}, u32[]{:S(2)}, u32[]{:S(2)}) collective-permute-start(f32[1,4096]{1,0:T(1,128)S(1)} %get-tuple-element.42), channel_id=1, source_target_pairs={{0,12},{4,0},{8,4},{12,8},{1,13},{5,1},{9,5},{13,9},{2,14},{6,2},{... | collective-permute-start | bytes 49160 | tf_op jit(solution)/shard_map/ppermute | solution.py:181
  40.2 3.5 %collective-permute-done.1 = f32[1,4096]{1,0:T(1,128)S(1)} collective-permute-done((f32[1,4096]{1,0:T(1,128)S(1)}, f32[1,4096]{1,0:T(1,128)S(1)}, u32[]{:S(2)}, u32[]{:S(2)}) %collective-permute-start.1) | collective-permute-done | bytes 16416 | tf_op jit(solution)/shard_map/ppermute | solution.py:181
  44.3 4.1 %collective-permute-start.5 = (f32[1,4096]{1,0:T(1,128)S(1)}, f32[1,4096]{1,0:T(1,128)S(1)}, u32[]{:S(2)}, u32[]{:S(2)}) collective-permute-start(f32[1,4096]{1,0:T(1,128)S(1)} %add_add_fusion.1), channel_id=1, source_target_pairs={{0,48},{16,0},{32,16},{48,32},{1,49},{17,1},{33,17},{49,33},{2,50}... | collective-permute-start | bytes 49160 | tf_op jit(solution)/shard_map/ppermute | solution.py:181
  48.4 1.3 collective-permute-start.3
  49.8 3.8 %collective-permute-done.4 = f32[1,4096]{1,0:T(1,128)S(1)} collective-permute-done((f32[1,4096]{1,0:T(1,128)S(1)}, f32[1,4096]{1,0:T(1,128)S(1)}, u32[]{:S(2)}, u32[]{:S(2)}) %collective-permute-start.4) | collective-permute-done | bytes 16416 | tf_op jit(solution)/shard_map/ppermute | solution.py:181
  53.7 1.6 collective-permute-start.6
  55.3 2.3 %collective-permute-done.6 = f32[1,4096]{1,0:T(1,128)S(1)} collective-permute-done((f32[1,4096]{1,0:T(1,128)S(1)}, f32[1,4096]{1,0:T(1,128)S(1)}, u32[]{:S(2)}, u32[]{:S(2)}) %collective-permute-start.6) | collective-permute-done | bytes 16416 | tf_op jit(solution)/shard_map/ppermute | solution.py:181
  58.1 1.6 collective-permute-start.7
  59.8 1.1 constant_dynamic-slice_fusion
  61.1 1.7 collective-permute-start.9
  62.8 2.4 %collective-permute-start.10 = (bf16[2,64,512]{2,1,0:T(8,128)(2,1)S(1)}, bf16[2,64,512]{2,1,0:T(8,128)(2,1)S(1)}, u32[]{:S(2)}, u32[]{:S(2)}) collective-permute-start(bf16[2,64,512]{2,1,0:T(8,128)(2,1)S(1)} %bitcast.166), channel_id=1, source_target_pairs={{0,12},{4,0},{8,4},{12,8},{1,13},{5,1},{9,5},{13,9},{2,14},{6,2},{... | collective-permute-start | bytes 393224 | tf_op jit(solution)/shard_map/ppermute | solution.py:181
  65.3 3.3 %collective-permute-done.8 = bf16[2,64,512]{2,1,0:T(8,128)(2,1)S(1)} collective-permute-done((bf16[2,64,512]{2,1,0:T(8,128)(2,1)S(1)}, bf16[2,64,512]{2,1,0:T(8,128)(2,1)S(1)}, u32[]{:S(2)}, u32[]{:S(2)}) %collective-permute-start.8) | collective-permute-done | bytes 131104 | tf_op jit(solution)/shard_map/ppermute | solution.py:181
  68.6 1.2 collective-permute-done.10
  70.0 1.3 collective-permute-start.17
  71.4 2.4 %collective-permute-start.12 = (bf16[2,64,2048]{2,1,0:T(8,128)(2,1)S(1)}, bf16[2,64,2048]{2,1,0:T(8,128)(2,1)S(1)}, u32[]{:S(2)}, u32[]{:S(2)}) collective-permute-start(bf16[2,64,2048]{2,1,0:T(8,128)(2,1)S(1)} %pad_maximum_fusion.2.own_ref), channel_id=1, source_target_pairs={{0,12},{4,0},{8,4},{12,8},{1,13},{5,1},{9,5},{13,9},{2,14},{6,2},{... | collective-permute-start | bytes 1572872 | tf_op jit(solution)/shard_map/ppermute | solution.py:181
  73.8 1.3 collective-permute-start.16
  75.2 6.0 %collective-permute-start.14 = (bf16[2,64,2048]{2,1,0:T(8,128)(2,1)S(1)}, bf16[2,64,2048]{2,1,0:T(8,128)(2,1)S(1)}, u32[]{:S(2)}, u32[]{:S(2)}) collective-permute-start(bf16[2,64,2048]{2,1,0:T(8,128)(2,1)S(1)} %pad_maximum_fusion.3.own_ref), channel_id=1, source_target_pairs={{0,48},{16,0},{32,16},{48,32},{1,49},{17,1},{33,17},{49,33},{2,50}... | collective-permute-start | bytes 1572872 | tf_op jit(solution)/shard_map/ppermute | solution.py:181
  81.2 1.9 collective-permute-start.13
  83.1 1.4 collective-permute-done.16
  84.5 3.7 %collective-permute-start.15 = (bf16[4,64,512]{2,1,0:T(8,128)(2,1)S(1)}, bf16[4,64,512]{2,1,0:T(8,128)(2,1)S(1)}, u32[]{:S(2)}, u32[]{:S(2)}) collective-permute-start(bf16[4,64,512]{2,1,0:T(8,128)(2,1)S(1)} %get-tuple-element.83), channel_id=1, source_target_pairs={{0,16},{17,33},{33,49},{48,0},{2,18},{19,35},{35,51},{50,2},{4,20}... | collective-permute-start | bytes 786440 | tf_op jit(solution)/shard_map/ppermute | solution.py:238
  88.2 6.6 %collective-permute-done.15 = bf16[4,64,512]{2,1,0:T(8,128)(2,1)S(1)} collective-permute-done((bf16[4,64,512]{2,1,0:T(8,128)(2,1)S(1)}, bf16[4,64,512]{2,1,0:T(8,128)(2,1)S(1)}, u32[]{:S(2)}, u32[]{:S(2)}) %collective-permute-start.15) | collective-permute-done | bytes 262176 | tf_op jit(solution)/shard_map/ppermute | solution.py:238
  95.9 2.3 %collective-permute-start.20 = (bf16[64,2048]{1,0:T(8,128)(2,1)S(1)}, bf16[64,2048]{1,0:T(8,128)(2,1)S(1)}, u32[]{:S(2)}, u32[]{:S(2)}) collective-permute-start(bf16[64,2048]{1,0:T(8,128)(2,1)S(1)} %slice_bitcast_fusion.3), channel_id=1, source_target_pairs={{0,16},{16,32},{32,48},{48,0},{1,17},{17,33},{33,49},{49,1},{2,18}... | collective-permute-start | bytes 786440 | tf_op jit(solution)/shard_map/ppermute | solution.py:181
  98.2 3.1 %collective-permute-start.19 = (bf16[64,2048]{1,0:T(8,128)(2,1)S(1)}, bf16[64,2048]{1,0:T(8,128)(2,1)S(1)}, u32[]{:S(2)}, u32[]{:S(2)}) collective-permute-start(bf16[64,2048]{1,0:T(8,128)(2,1)S(1)} %slice_bitcast_fusion.4), channel_id=1, source_target_pairs={{0,12},{4,0},{8,4},{12,8},{1,13},{5,1},{9,5},{13,9},{2,14},{6,2},{... | collective-permute-start | bytes 786440 | tf_op jit(solution)/shard_map/ppermute | solution.py:181
  101.3 1.2 collective-permute-done.21.last_ref
  102.5 1.1 collective-permute-done.20.first_ref
  103.6 1.6 collective-permute-done.19.last_ref
  105.2 3.7 %collective-permute-done.18.first_ref = bf16[64,2048]{1,0:T(8,128)(2,1)S(1)} collective-permute-done((bf16[64,2048]{1,0:T(8,128)(2,1)S(1)}, bf16[64,2048]{1,0:T(8,128)(2,1)S(1)}, u32[]{:S(2)}, u32[]{:S(2)}) %collective-permute-start.18) | collective-permute-done | bytes 262176 | tf_op jit(solution)/shard_map/ppermute | solution.py:181
  108.9 1.5 shard_map.51.refs_0_
  110.3 1.5 shard_map.52.refs_0_
  111.8 7.3 %collective-permute-start.25 = (bf16[4,4,64,512]{3,2,1,0:T(8,128)(2,1)S(1)}, bf16[4,4,64,512]{3,2,1,0:T(8,128)(2,1)S(1)}, u32[]{:S(2)}, u32[]{:S(2)}) collective-permute-start(bf16[4,4,64,512]{3,2,1,0:T(8,128)(2,1)S(1)} %pad_maximum_fusion.1), channel_id=1, source_target_pairs={{0,2},{64,0},{2,66},{66,64},{16,18},{80,16},{18,82},{82,80},{33,35... | collective-permute-start | bytes 3145736 | tf_op jit(solution)/shard_map/ppermute | solution.py:248
  119.1 2.0 %collective-permute-start.23 = (bf16[8,64,2048]{2,1,0:T(8,128)(2,1)}, bf16[8,64,2048]{2,1,0:T(8,128)(2,1)}, u32[]{:S(2)}, u32[]{:S(2)}) collective-permute-start(bf16[8,64,2048]{2,1,0:T(8,128)(2,1)} %shard_map.51.refs_0_), channel_id=1, source_target_pairs={{0,16},{16,32},{32,48},{48,0},{1,17},{17,33},{33,49},{49,1},{2,18}... | collective-permute-start | bytes 6291464 | tf_op jit(solution)/shard_map/ppermute | solution.py:181
  121.1 3.2 %collective-permute-start.28 = (bf16[8,64,2048]{2,1,0:T(8,128)(2,1)}, bf16[8,64,2048]{2,1,0:T(8,128)(2,1)}, u32[]{:S(2)}, u32[]{:S(2)}) collective-permute-start(bf16[8,64,2048]{2,1,0:T(8,128)(2,1)} %shard_map.52.refs_0_), channel_id=1, source_target_pairs={{0,12},{4,0},{8,4},{12,8},{1,13},{5,1},{9,5},{13,9},{2,14},{6,2},{... | collective-permute-start | bytes 6291464 | tf_op jit(solution)/shard_map/ppermute | solution.py:181
  124.5 6.8 %collective-permute-done.25 = bf16[4,4,64,512]{3,2,1,0:T(8,128)(2,1)S(1)} collective-permute-done((bf16[4,4,64,512]{3,2,1,0:T(8,128)(2,1)S(1)}, bf16[4,4,64,512]{3,2,1,0:T(8,128)(2,1)S(1)}, u32[]{:S(2)}, u32[]{:S(2)}) %collective-permute-start.25) | collective-permute-done | bytes 1048608 | tf_op jit(solution)/shard_map/ppermute | solution.py:248
  131.5 2.7 %collective-permute-start.26 = (bf16[2,4,4,64,512]{4,3,2,1,0:T(8,128)(2,1)S(1)}, bf16[2,4,4,64,512]{4,3,2,1,0:T(8,128)(2,1)}, u32[]{:S(2)}, u32[]{:S(2)}) collective-permute-start(bf16[2,4,4,64,512]{4,3,2,1,0:T(8,128)(2,1)S(1)} %pad_maximum_fusion), channel_id=1, source_target_pairs={{0,1},{16,17},{33,32},{49,48},{2,3},{18,19},{35,34},{51,50},{4,5},... | collective-permute-start | bytes 6291464 | tf_op jit(solution)/shard_map/ppermute | solution.py:254
  134.5 23.8 %collective-permute-done.24.refs_2_ = bf16[8,64,2048]{2,1,0:T(8,128)(2,1)} collective-permute-done((bf16[8,64,2048]{2,1,0:T(8,128)(2,1)}, bf16[8,64,2048]{2,1,0:T(8,128)(2,1)}, u32[]{:S(2)}, u32[]{:S(2)}) %collective-permute-start.24) | collective-permute-done | bytes 2097184 | tf_op jit(solution)/shard_map/ppermute | solution.py:181
  158.3 1.3 slice.51
  159.6 3.8 %collective-permute-start.30 = (bf16[4,64,2048]{2,1,0:T(8,128)(2,1)S(1)}, bf16[4,64,2048]{2,1,0:T(8,128)(2,1)S(1)}, u32[]{:S(2)}, u32[]{:S(2)}) collective-permute-start(bf16[4,64,2048]{2,1,0:T(8,128)(2,1)S(1)} %slice.51), channel_id=1, source_target_pairs={{0,48},{16,0},{32,16},{48,32},{1,49},{17,1},{33,17},{49,33},{2,50}... | collective-permute-start | bytes 3145736 | tf_op jit(solution)/shard_map/ppermute | solution.py:181
  163.4 1.3 slice.50
  164.8 1.3 slice.53
  166.1 3.1 %collective-permute-start.32 = (bf16[4,64,2048]{2,1,0:T(8,128)(2,1)S(1)}, bf16[4,64,2048]{2,1,0:T(8,128)(2,1)S(1)}, u32[]{:S(2)}, u32[]{:S(2)}) collective-permute-start(bf16[4,64,2048]{2,1,0:T(8,128)(2,1)S(1)} %slice.53), channel_id=1, source_target_pairs={{0,12},{4,0},{8,4},{12,8},{1,13},{5,1},{9,5},{13,9},{2,14},{6,2},{... | collective-permute-start | bytes 3145736 | tf_op jit(solution)/shard_map/ppermute | solution.py:181
  169.3 1.3 slice.52
  170.7 3.1 %shard_map.53 = (bf16[32,64,1024]{2,1,0:T(8,128)(2,1)S(1)}, bf16[32,64,1024]{2,1,0:T(8,128)(2,1)S(1)}) custom-call(s32[32]{0:T(128)S(1)} %stack.419.map_ref, s32[2,32]{1,0:T(2,128)S(1)} %pad_add_fusion.1.places_ref, bf16[32,64,512]{2,1,0:T(8,128)(2,1)S(1)} %bitcast.158, bf16[32,64,512]{2,1,0:T(8,128)(2,1)} %bitcast.132.passed_ref), custom_call_target="tpu_custom_call" | custom-call | flops 16777216 | bytes 12582912 | tf_op jit(solution)/shard_map/pallas_call | solution.py:107
  173.8 8.7 %shard_map.54 = (f32[2048,512]{1,0:T(8,128)S(1)}, f32[2048,512]{1,0:T(8,128)S(1)}) custom-call(bf16[8,64,2048]{2,1,0:T(8,128)(2,1)} %shard_map.51.refs_0_, bf16[8,64,2048]{2,1,0:T(8,128)(2,1)} %collective-permute-done.23.refs_1_, bf16[8,64,2048]{2,1,0:T(8,128)(2,1)} %collective-permute-done.24.refs_2_, ...), custom_call_target="tpu_custom_call" | custom-call | flops 12884901888 | bytes 17825792 | tf_op jit(solution)/shard_map/pallas_call | solution.py:146
  182.5 8.7 %shard_map.55 = (f32[2048,512]{1,0:T(8,128)S(1)}, f32[2048,512]{1,0:T(8,128)S(1)}) custom-call(bf16[8,64,2048]{2,1,0:T(8,128)(2,1)} %shard_map.52.refs_0_, bf16[8,64,2048]{2,1,0:T(8,128)(2,1)} %collective-permute-done.27.refs_1_, bf16[8,64,2048]{2,1,0:T(8,128)(2,1)} %collective-permute-done.28.refs_2_, ...), custom_call_target="tpu_custom_call" | custom-call | flops 12884901888 | bytes 17825792 | tf_op jit(solution)/shard_map/pallas_call | solution.py:146
  191.7 4.4 %shard_map.56 = (f32[4096,512]{1,0:T(8,128)}, f32[4096,512]{1,0:T(8,128)}) custom-call(bf16[4,64,2048]{2,1,0:T(8,128)(2,1)S(1)} %collective-permute-done.29.refs_0_, bf16[4,64,2048]{2,1,0:T(8,128)(2,1)S(1)} %collective-permute-done.30.refs_1_, bf16[32,64,1024]{2,1,0:T(8,128)(2,1)S(1)} %get-tuple-element.63.refs_3_.refs_2_, ...), custom_call_target="tpu_custom_call" | custom-call | flops 4294967296 | bytes 19922944 | tf_op jit(solution)/shard_map/pallas_call | solution.py:146
  196.1 4.4 %shard_map.57 = (f32[4096,512]{1,0:T(8,128)}, f32[4096,512]{1,0:T(8,128)}) custom-call(bf16[4,64,2048]{2,1,0:T(8,128)(2,1)S(1)} %collective-permute-done.31.refs_0_, bf16[4,64,2048]{2,1,0:T(8,128)(2,1)S(1)} %collective-permute-done.32.refs_1_, ...), custom_call_target="tpu_custom_call", output_to_operand_aliasing={{0}: (5, {}), {1}: (6, {})} | custom-call | flops 4294967296 | bytes 19922944 | tf_op jit(solution)/shard_map/pallas_call | solution.py:146
  (67 shorter events, 6.1 us)
Async XLA Ops:
  0.6 2.0 copy-start.1
  0.6 2.1 %copy-start = (s32[128]{0:T(128)S(1)}, s32[128]{0:T(128)}, u32[]{:S(2)}) copy-start(s32[128]{0:T(128)} %param.5) | copy-start | bytes 1540
  35.6 4.6 %collective-permute-start.2 = (f32[1,4096]{1,0:T(1,128)S(1)}, f32[1,4096]{1,0:T(1,128)S(1)}, u32[]{:S(2)}, u32[]{:S(2)}) collective-permute-start(f32[1,4096]{1,0:T(1,128)S(1)} %get-tuple-element.42), channel_id=1, source_target_pairs={{0,12},{4,0},{8,4},{12,8},{1,13},{5,1},{9,5},{13,9},{2,14},{6,2},{... | collective-permute-start | bytes 49160 | tf_op jit(solution)/shard_map/ppermute | solution.py:181
  38.5 5.2 %collective-permute-start.1 = (f32[1,4096]{1,0:T(1,128)S(1)}, f32[1,4096]{1,0:T(1,128)S(1)}, u32[]{:S(2)}, u32[]{:S(2)}) collective-permute-start(f32[1,4096]{1,0:T(1,128)S(1)} %get-tuple-element.42), channel_id=1, source_target_pairs={{0,8},{4,12},{8,0},{12,4},{1,9},{5,13},{9,1},{13,5},{2,10},{6,14},... | collective-permute-start | bytes 49160 | tf_op jit(solution)/shard_map/ppermute | solution.py:181
  39.3 4.9 %collective-permute-start = (f32[1,4096]{1,0:T(1,128)S(1)}, f32[1,4096]{1,0:T(1,128)S(1)}, u32[]{:S(2)}, u32[]{:S(2)}) collective-permute-start(f32[1,4096]{1,0:T(1,128)S(1)} %get-tuple-element.42), channel_id=1, source_target_pairs={{0,4},{4,8},{8,12},{12,0},{1,5},{5,9},{9,13},{13,1},{2,6},{6,10},{... | collective-permute-start | bytes 49160 | tf_op jit(solution)/shard_map/ppermute | solution.py:181
  44.3 5.6 %collective-permute-start.5 = (f32[1,4096]{1,0:T(1,128)S(1)}, f32[1,4096]{1,0:T(1,128)S(1)}, u32[]{:S(2)}, u32[]{:S(2)}) collective-permute-start(f32[1,4096]{1,0:T(1,128)S(1)} %add_add_fusion.1), channel_id=1, source_target_pairs={{0,48},{16,0},{32,16},{48,32},{1,49},{17,1},{33,17},{49,33},{2,50}... | collective-permute-start | bytes 49160 | tf_op jit(solution)/shard_map/ppermute | solution.py:181
  48.4 5.2 %collective-permute-start.4 = (f32[1,4096]{1,0:T(1,128)S(1)}, f32[1,4096]{1,0:T(1,128)S(1)}, u32[]{:S(2)}, u32[]{:S(2)}) collective-permute-start(f32[1,4096]{1,0:T(1,128)S(1)} %add_add_fusion.1), channel_id=1, source_target_pairs={{0,32},{16,48},{32,0},{48,16},{1,33},{17,49},{33,1},{49,17},{2,34}... | collective-permute-start | bytes 49160 | tf_op jit(solution)/shard_map/ppermute | solution.py:181
  48.4 5.2 %collective-permute-start.3 = (f32[1,4096]{1,0:T(1,128)S(1)}, f32[1,4096]{1,0:T(1,128)S(1)}, u32[]{:S(2)}, u32[]{:S(2)}) collective-permute-start(f32[1,4096]{1,0:T(1,128)S(1)} %add_add_fusion.1), channel_id=1, source_target_pairs={{0,16},{16,32},{32,48},{48,0},{1,17},{17,33},{33,49},{49,1},{2,18}... | collective-permute-start | bytes 49160 | tf_op jit(solution)/shard_map/ppermute | solution.py:181
  53.7 4.0 %collective-permute-start.6 = (f32[1,4096]{1,0:T(1,128)S(1)}, f32[1,4096]{1,0:T(1,128)S(1)}, u32[]{:S(2)}, u32[]{:S(2)}) collective-permute-start(f32[1,4096]{1,0:T(1,128)S(1)} %add_add_fusion), channel_id=1, source_target_pairs={{0,64},{64,0},{1,65},{65,1},{2,66},{66,2},{3,67},{67,3},{4,68},{68... | collective-permute-start | bytes 49160 | tf_op jit(solution)/shard_map/ppermute | solution.py:181
  58.1 11.7 %collective-permute-start.7 = (bf16[64,4096]{1,0:T(8,128)(2,1)S(1)}, bf16[64,4096]{1,0:T(8,128)(2,1)S(1)}, u32[]{:S(2)}, u32[]{:S(2)}) collective-permute-start(bf16[64,4096]{1,0:T(8,128)(2,1)S(1)} %subtract_convert_fusion), channel_id=1, source_target_pairs={{0,64},{64,0},{1,65},{65,1},{2,66},{66,2},{3,67},{67,3},{4,68},{68... | collective-permute-start | bytes 1572872 | tf_op jit(solution)/shard_map/ppermute | solution.py:181
  61.0 7.7 %collective-permute-start.8 = (bf16[2,64,512]{2,1,0:T(8,128)(2,1)S(1)}, bf16[2,64,512]{2,1,0:T(8,128)(2,1)S(1)}, u32[]{:S(2)}, u32[]{:S(2)}) collective-permute-start(bf16[2,64,512]{2,1,0:T(8,128)(2,1)S(1)} %bitcast.168), channel_id=1, source_target_pairs={{0,4},{4,8},{8,12},{12,0},{1,5},{5,9},{9,13},{13,1},{2,6},{6,10},{... | collective-permute-start | bytes 393224 | tf_op jit(solution)/shard_map/ppermute | solution.py:181
  61.1 7.6 %collective-permute-start.9 = (bf16[2,64,512]{2,1,0:T(8,128)(2,1)S(1)}, bf16[2,64,512]{2,1,0:T(8,128)(2,1)S(1)}, u32[]{:S(2)}, u32[]{:S(2)}) collective-permute-start(bf16[2,64,512]{2,1,0:T(8,128)(2,1)S(1)} %bitcast.167), channel_id=1, source_target_pairs={{0,8},{4,12},{8,0},{12,4},{1,9},{5,13},{9,1},{13,5},{2,10},{6,14},... | collective-permute-start | bytes 393224 | tf_op jit(solution)/shard_map/ppermute | solution.py:181
  62.8 7.0 %collective-permute-start.10 = (bf16[2,64,512]{2,1,0:T(8,128)(2,1)S(1)}, bf16[2,64,512]{2,1,0:T(8,128)(2,1)S(1)}, u32[]{:S(2)}, u32[]{:S(2)}) collective-permute-start(bf16[2,64,512]{2,1,0:T(8,128)(2,1)S(1)} %bitcast.166), channel_id=1, source_target_pairs={{0,12},{4,0},{8,4},{12,8},{1,13},{5,1},{9,5},{13,9},{2,14},{6,2},{... | collective-permute-start | bytes 393224 | tf_op jit(solution)/shard_map/ppermute | solution.py:181
  70.0 11.2 %collective-permute-start.17 = (bf16[4,64,512]{2,1,0:T(8,128)(2,1)S(1)}, bf16[4,64,512]{2,1,0:T(8,128)(2,1)S(1)}, u32[]{:S(2)}, u32[]{:S(2)}) collective-permute-start(bf16[4,64,512]{2,1,0:T(8,128)(2,1)S(1)} %get-tuple-element.81), channel_id=1, source_target_pairs={{1,49},{16,0},{32,16},{49,33},{3,51},{18,2},{34,18},{51,35},{5,53}... | collective-permute-start | bytes 786440 | tf_op jit(solution)/shard_map/ppermute | solution.py:238
  71.4 23.5 %collective-permute-start.12 = (bf16[2,64,2048]{2,1,0:T(8,128)(2,1)S(1)}, bf16[2,64,2048]{2,1,0:T(8,128)(2,1)S(1)}, u32[]{:S(2)}, u32[]{:S(2)}) collective-permute-start(bf16[2,64,2048]{2,1,0:T(8,128)(2,1)S(1)} %pad_maximum_fusion.2.own_ref), channel_id=1, source_target_pairs={{0,12},{4,0},{8,4},{12,8},{1,13},{5,1},{9,5},{13,9},{2,14},{6,2},{... | collective-permute-start | bytes 1572872 | tf_op jit(solution)/shard_map/ppermute | solution.py:181
  73.8 21.1 %collective-permute-start.11 = (bf16[2,64,2048]{2,1,0:T(8,128)(2,1)S(1)}, bf16[2,64,2048]{2,1,0:T(8,128)(2,1)S(1)}, u32[]{:S(2)}, u32[]{:S(2)}) collective-permute-start(bf16[2,64,2048]{2,1,0:T(8,128)(2,1)S(1)} %pad_maximum_fusion.2.own_ref), channel_id=1, source_target_pairs={{0,4},{4,8},{8,12},{12,0},{1,5},{5,9},{9,13},{13,1},{2,6},{6,10},{... | collective-permute-start | bytes 1572872 | tf_op jit(solution)/shard_map/ppermute | solution.py:181
  73.8 10.7 %collective-permute-start.16 = (bf16[4,64,512]{2,1,0:T(8,128)(2,1)S(1)}, bf16[4,64,512]{2,1,0:T(8,128)(2,1)S(1)}, u32[]{:S(2)}, u32[]{:S(2)}) collective-permute-start(bf16[4,64,512]{2,1,0:T(8,128)(2,1)S(1)} %get-tuple-element.82), channel_id=1, source_target_pairs={{1,33},{17,49},{32,0},{48,16},{3,35},{19,51},{34,2},{50,18},{5,37}... | collective-permute-start | bytes 786440 | tf_op jit(solution)/shard_map/ppermute | solution.py:238
  75.2 19.8 %collective-permute-start.14 = (bf16[2,64,2048]{2,1,0:T(8,128)(2,1)S(1)}, bf16[2,64,2048]{2,1,0:T(8,128)(2,1)S(1)}, u32[]{:S(2)}, u32[]{:S(2)}) collective-permute-start(bf16[2,64,2048]{2,1,0:T(8,128)(2,1)S(1)} %pad_maximum_fusion.3.own_ref), channel_id=1, source_target_pairs={{0,48},{16,0},{32,16},{48,32},{1,49},{17,1},{33,17},{49,33},{2,50}... | collective-permute-start | bytes 1572872 | tf_op jit(solution)/shard_map/ppermute | solution.py:181
  81.2 13.8 %collective-permute-start.13 = (bf16[2,64,2048]{2,1,0:T(8,128)(2,1)S(1)}, bf16[2,64,2048]{2,1,0:T(8,128)(2,1)S(1)}, u32[]{:S(2)}, u32[]{:S(2)}) collective-permute-start(bf16[2,64,2048]{2,1,0:T(8,128)(2,1)S(1)} %pad_maximum_fusion.3.own_ref), channel_id=1, source_target_pairs={{0,16},{16,32},{32,48},{48,0},{1,17},{17,33},{33,49},{49,1},{2,18}... | collective-permute-start | bytes 1572872 | tf_op jit(solution)/shard_map/ppermute | solution.py:181
  84.5 10.3 %collective-permute-start.15 = (bf16[4,64,512]{2,1,0:T(8,128)(2,1)S(1)}, bf16[4,64,512]{2,1,0:T(8,128)(2,1)S(1)}, u32[]{:S(2)}, u32[]{:S(2)}) collective-permute-start(bf16[4,64,512]{2,1,0:T(8,128)(2,1)S(1)} %get-tuple-element.83), channel_id=1, source_target_pairs={{0,16},{17,33},{33,49},{48,0},{2,18},{19,35},{35,51},{50,2},{4,20}... | collective-permute-start | bytes 786440 | tf_op jit(solution)/shard_map/ppermute | solution.py:238
  95.0 13.8 %collective-permute-start.22 = (bf16[4,4,64,512]{3,2,1,0:T(8,128)(2,1)S(1)}, bf16[4,4,64,512]{3,2,1,0:T(8,128)(2,1)S(1)}, u32[]{:S(2)}, u32[]{:S(2)}) collective-permute-start(bf16[4,4,64,512]{3,2,1,0:T(8,128)(2,1)S(1)} %pad_maximum_fusion.1), channel_id=1, source_target_pairs={{64,2},{2,64},{80,18},{18,80},{97,35},{35,97},{113,51},{51,113},{6... | collective-permute-start | bytes 3145736 | tf_op jit(solution)/shard_map/ppermute | solution.py:248
  95.8 6.6 %collective-permute-start.21 = (bf16[64,2048]{1,0:T(8,128)(2,1)S(1)}, bf16[64,2048]{1,0:T(8,128)(2,1)S(1)}, u32[]{:S(2)}, u32[]{:S(2)}) collective-permute-start(bf16[64,2048]{1,0:T(8,128)(2,1)S(1)} %slice_bitcast_fusion.2), channel_id=1, source_target_pairs={{0,48},{16,0},{32,16},{48,32},{1,49},{17,1},{33,17},{49,33},{2,50}... | collective-permute-start | bytes 786440 | tf_op jit(solution)/shard_map/ppermute | solution.py:181
  95.9 7.7 %collective-permute-start.20 = (bf16[64,2048]{1,0:T(8,128)(2,1)S(1)}, bf16[64,2048]{1,0:T(8,128)(2,1)S(1)}, u32[]{:S(2)}, u32[]{:S(2)}) collective-permute-start(bf16[64,2048]{1,0:T(8,128)(2,1)S(1)} %slice_bitcast_fusion.3), channel_id=1, source_target_pairs={{0,16},{16,32},{32,48},{48,0},{1,17},{17,33},{33,49},{49,1},{2,18}... | collective-permute-start | bytes 786440 | tf_op jit(solution)/shard_map/ppermute | solution.py:181
  98.2 7.0 %collective-permute-start.19 = (bf16[64,2048]{1,0:T(8,128)(2,1)S(1)}, bf16[64,2048]{1,0:T(8,128)(2,1)S(1)}, u32[]{:S(2)}, u32[]{:S(2)}) collective-permute-start(bf16[64,2048]{1,0:T(8,128)(2,1)S(1)} %slice_bitcast_fusion.4), channel_id=1, source_target_pairs={{0,12},{4,0},{8,4},{12,8},{1,13},{5,1},{9,5},{13,9},{2,14},{6,2},{... | collective-permute-start | bytes 786440 | tf_op jit(solution)/shard_map/ppermute | solution.py:181
  101.3 7.6 %collective-permute-start.18 = (bf16[64,2048]{1,0:T(8,128)(2,1)S(1)}, bf16[64,2048]{1,0:T(8,128)(2,1)S(1)}, u32[]{:S(2)}, u32[]{:S(2)}) collective-permute-start(bf16[64,2048]{1,0:T(8,128)(2,1)S(1)} %slice_bitcast_fusion.5), channel_id=1, source_target_pairs={{0,4},{4,8},{8,12},{12,0},{1,5},{5,9},{9,13},{13,1},{2,6},{6,10},{... | collective-permute-start | bytes 786440 | tf_op jit(solution)/shard_map/ppermute | solution.py:181
  111.8 19.6 %collective-permute-start.25 = (bf16[4,4,64,512]{3,2,1,0:T(8,128)(2,1)S(1)}, bf16[4,4,64,512]{3,2,1,0:T(8,128)(2,1)S(1)}, u32[]{:S(2)}, u32[]{:S(2)}) collective-permute-start(bf16[4,4,64,512]{3,2,1,0:T(8,128)(2,1)S(1)} %pad_maximum_fusion.1), channel_id=1, source_target_pairs={{0,2},{64,0},{2,66},{66,64},{16,18},{80,16},{18,82},{82,80},{33,35... | collective-permute-start | bytes 3145736 | tf_op jit(solution)/shard_map/ppermute | solution.py:248
  119.0 39.3 %collective-permute-start.24 = (bf16[8,64,2048]{2,1,0:T(8,128)(2,1)}, bf16[8,64,2048]{2,1,0:T(8,128)(2,1)}, u32[]{:S(2)}, u32[]{:S(2)}) collective-permute-start(bf16[8,64,2048]{2,1,0:T(8,128)(2,1)} %shard_map.51.refs_0_), channel_id=1, source_target_pairs={{0,48},{16,0},{32,16},{48,32},{1,49},{17,1},{33,17},{49,33},{2,50}... | collective-permute-start | bytes 6291464 | tf_op jit(solution)/shard_map/ppermute | solution.py:181
  119.1 44.3 %collective-permute-start.23 = (bf16[8,64,2048]{2,1,0:T(8,128)(2,1)}, bf16[8,64,2048]{2,1,0:T(8,128)(2,1)}, u32[]{:S(2)}, u32[]{:S(2)}) collective-permute-start(bf16[8,64,2048]{2,1,0:T(8,128)(2,1)} %shard_map.51.refs_0_), channel_id=1, source_target_pairs={{0,16},{16,32},{32,48},{48,0},{1,17},{17,33},{33,49},{49,1},{2,18}... | collective-permute-start | bytes 6291464 | tf_op jit(solution)/shard_map/ppermute | solution.py:181
  121.1 43.7 %collective-permute-start.28 = (bf16[8,64,2048]{2,1,0:T(8,128)(2,1)}, bf16[8,64,2048]{2,1,0:T(8,128)(2,1)}, u32[]{:S(2)}, u32[]{:S(2)}) collective-permute-start(bf16[8,64,2048]{2,1,0:T(8,128)(2,1)} %shard_map.52.refs_0_), channel_id=1, source_target_pairs={{0,12},{4,0},{8,4},{12,8},{1,13},{5,1},{9,5},{13,9},{2,14},{6,2},{... | collective-permute-start | bytes 6291464 | tf_op jit(solution)/shard_map/ppermute | solution.py:181
  124.4 44.9 %collective-permute-start.27 = (bf16[8,64,2048]{2,1,0:T(8,128)(2,1)}, bf16[8,64,2048]{2,1,0:T(8,128)(2,1)}, u32[]{:S(2)}, u32[]{:S(2)}) collective-permute-start(bf16[8,64,2048]{2,1,0:T(8,128)(2,1)} %shard_map.52.refs_0_), channel_id=1, source_target_pairs={{0,4},{4,8},{8,12},{12,0},{1,5},{5,9},{9,13},{13,1},{2,6},{6,10},{... | collective-permute-start | bytes 6291464 | tf_op jit(solution)/shard_map/ppermute | solution.py:181
  131.5 39.2 %collective-permute-start.26 = (bf16[2,4,4,64,512]{4,3,2,1,0:T(8,128)(2,1)S(1)}, bf16[2,4,4,64,512]{4,3,2,1,0:T(8,128)(2,1)}, u32[]{:S(2)}, u32[]{:S(2)}) collective-permute-start(bf16[2,4,4,64,512]{4,3,2,1,0:T(8,128)(2,1)S(1)} %pad_maximum_fusion), channel_id=1, source_target_pairs={{0,1},{16,17},{33,32},{49,48},{2,3},{18,19},{35,34},{51,50},{4,5},... | collective-permute-start | bytes 6291464 | tf_op jit(solution)/shard_map/ppermute | solution.py:254
  159.6 31.6 %collective-permute-start.30 = (bf16[4,64,2048]{2,1,0:T(8,128)(2,1)S(1)}, bf16[4,64,2048]{2,1,0:T(8,128)(2,1)S(1)}, u32[]{:S(2)}, u32[]{:S(2)}) collective-permute-start(bf16[4,64,2048]{2,1,0:T(8,128)(2,1)S(1)} %slice.51), channel_id=1, source_target_pairs={{0,48},{16,0},{32,16},{48,32},{1,49},{17,1},{33,17},{49,33},{2,50}... | collective-permute-start | bytes 3145736 | tf_op jit(solution)/shard_map/ppermute | solution.py:181
  164.7 26.5 %collective-permute-start.29 = (bf16[4,64,2048]{2,1,0:T(8,128)(2,1)S(1)}, bf16[4,64,2048]{2,1,0:T(8,128)(2,1)S(1)}, u32[]{:S(2)}, u32[]{:S(2)}) collective-permute-start(bf16[4,64,2048]{2,1,0:T(8,128)(2,1)S(1)} %slice.50), channel_id=1, source_target_pairs={{0,16},{16,32},{32,48},{48,0},{1,17},{17,33},{33,49},{49,1},{2,18}... | collective-permute-start | bytes 3145736 | tf_op jit(solution)/shard_map/ppermute | solution.py:181
  166.1 25.1 %collective-permute-start.32 = (bf16[4,64,2048]{2,1,0:T(8,128)(2,1)S(1)}, bf16[4,64,2048]{2,1,0:T(8,128)(2,1)S(1)}, u32[]{:S(2)}, u32[]{:S(2)}) collective-permute-start(bf16[4,64,2048]{2,1,0:T(8,128)(2,1)S(1)} %slice.53), channel_id=1, source_target_pairs={{0,12},{4,0},{8,4},{12,8},{1,13},{5,1},{9,5},{13,9},{2,14},{6,2},{... | collective-permute-start | bytes 3145736 | tf_op jit(solution)/shard_map/ppermute | solution.py:181
  170.6 21.1 %collective-permute-start.31 = (bf16[4,64,2048]{2,1,0:T(8,128)(2,1)S(1)}, bf16[4,64,2048]{2,1,0:T(8,128)(2,1)S(1)}, u32[]{:S(2)}, u32[]{:S(2)}) collective-permute-start(bf16[4,64,2048]{2,1,0:T(8,128)(2,1)S(1)} %slice.52), channel_id=1, source_target_pairs={{0,4},{4,8},{8,12},{12,0},{1,5},{5,9},{9,13},{13,1},{2,6},{6,10},{... | collective-permute-start | bytes 3145736 | tf_op jit(solution)/shard_map/ppermute | solution.py:181

commit v4 on v3

--- a/solution.py
+++ b/solution.py
@@ -290,12 +290,11 @@
 
     partner = moved(centered, "yl", 1)
     along_x = columns_along_x(centered, place)
-    partner, along_x = together(partner, along_x)
 
     pairs_of = [jnp.stack([centered[:, part], partner[:, part]]) for part in taken]
     pair_near = [near_blocks(pair, way[0]) for pair, way in zip(pairs_of, ways)]
     along_z = jnp.stack(columns_along_z(along_x, place))
-    pair_near, along_z, pairs_of = together(pair_near, along_z, pairs_of)
+    pair_near, along_z = together(pair_near, along_z)
 
     far = [
         (moved(behind[0], way[0], 1), moved(ahead[1], way[0], -1)) for (behind, ahead), way in zip(pair_near, ways)

time: 201 us -> 200 us (level)
  starting transfers between devices: 62.6 us -> 56.3 us
  waiting for transfers between devices: 61.5 us -> 66.8 us
    ppermute x27, starting transfers between devices: 45.7 us -> 40.5 us  [moved(): lax.ppermute(array, axis, [(i, (i + by) % length) for i in range(length)])]
    ppermute x3, waiting for transfers between devices: 7.93 us -> 12.2 us  [columns_along_z(): along_z.append(lax.ppermute(piece, ('z', 'c'), pairs))]
  transfers between devices with their start and end apart: 33 -> 33, of which waited for: 16 -> 18; matrix products, arithmetic and copies ran while one was open for 4% -> 4% of each run, Pallas kernels for 10% -> 10%
where the time goes in v4:
time: 200 us
  waiting for transfers between devices  66.8 us (33%)
  Pallas kernels  65 us (32%)
  starting transfers between devices  56.3 us (28%)
  local copies, waits for them, and re-layouts  9.54 us (5%)
    ppermute x27, waiting for transfers between devices, moved(): lax.ppermute(array, axis, [(i, (i + by) % length) for i in range(length)])  47 us
    ppermute x27, starting transfers between devices, moved(): lax.ppermute(array, axis, [(i, (i + by) % length) for i in range(length)])  40.5 us
    pallas_call x1, Pallas kernels, contact_features(): pl.pallas_call(feature_kernel, out_shape=(jax.ShapeDtypeStruct((frames, w...  32.8 us
    pallas_call x4, Pallas kernels, products(): pl.pallas_call(lambda *refs: product_kernel(count, factor, started, *refs...  26.2 us
    ppermute x3, waiting for transfers between devices, columns_along_z(): along_z.append(lax.ppermute(piece, ('z', 'c'), pairs))  12.2 us
    ppermute x2, starting transfers between devices, columns_along_y(): return lax.ppermute(along_z, ('yl', 'z', 'yh', 'c'), pairs)  8.63 us
    ppermute x2, waiting for transfers between devices, columns_along_y(): return lax.ppermute(along_z, ('yl', 'z', 'yh', 'c'), pairs)  7.64 us
    slice x4, local copies, waits for them, and re-layouts, far_block(): return (moved(behind[:half], axis, 1), moved(ahead[half:], axis, -1))  5.29 us
  transfers between devices with their start and end apart: 33, of which 18 were waited for; matrix products, arithmetic and copies ran while one was open for 4% of the time, Pallas kernels for 10%

profile of v4, /device:TPU:0, one launch (start us, length us, event | category | flops | bytes accessed | tf_op | source)
XLA Modules:
  0.0 199.6 jit_solution(11187376368397409021)
XLA Ops:
  0.7 1.9 copy.11
  2.8 32.8 %shard_map.50 = (f32[64,4096]{1,0:T(8,128)S(1)}, f32[1,4096]{1,0:T(1,128)S(1)}) custom-call(s32[8,256]{1,0:T(8,128)S(1)} %stack.368.index_ref, f32[1536,256]{1,0:T(8,128)S(1)} %bitcast.156), custom_call_target="tpu_custom_call" | custom-call | flops 201326592 | bytes 4194304 | tf_op jit(solution)/shard_map/pallas_call | solution.py:66
  35.6 2.9 %collective-permute-start.2 = (f32[1,4096]{1,0:T(1,128)S(1)}, f32[1,4096]{1,0:T(1,128)S(1)}, u32[]{:S(2)}, u32[]{:S(2)}) collective-permute-start(f32[1,4096]{1,0:T(1,128)S(1)} %get-tuple-element.35), channel_id=1, source_target_pairs={{0,12},{4,0},{8,4},{12,8},{1,13},{5,1},{9,5},{13,9},{2,14},{6,2},{... | collective-permute-start | bytes 49160 | tf_op jit(solution)/shard_map/ppermute | solution.py:181
  39.3 0.9 collective-permute-start
  40.2 3.5 %collective-permute-done.1 = f32[1,4096]{1,0:T(1,128)S(1)} collective-permute-done((f32[1,4096]{1,0:T(1,128)S(1)}, f32[1,4096]{1,0:T(1,128)S(1)}, u32[]{:S(2)}, u32[]{:S(2)}) %collective-permute-start.1) | collective-permute-done | bytes 16416 | tf_op jit(solution)/shard_map/ppermute | solution.py:181
  44.3 4.1 %collective-permute-start.5 = (f32[1,4096]{1,0:T(1,128)S(1)}, f32[1,4096]{1,0:T(1,128)S(1)}, u32[]{:S(2)}, u32[]{:S(2)}) collective-permute-start(f32[1,4096]{1,0:T(1,128)S(1)} %add_add_fusion.1), channel_id=1, source_target_pairs={{0,48},{16,0},{32,16},{48,32},{1,49},{17,1},{33,17},{49,33},{2,50}... | collective-permute-start | bytes 49160 | tf_op jit(solution)/shard_map/ppermute | solution.py:181
  48.4 1.3 collective-permute-start.3
  49.8 3.8 %collective-permute-done.4 = f32[1,4096]{1,0:T(1,128)S(1)} collective-permute-done((f32[1,4096]{1,0:T(1,128)S(1)}, f32[1,4096]{1,0:T(1,128)S(1)}, u32[]{:S(2)}, u32[]{:S(2)}) %collective-permute-start.4) | collective-permute-done | bytes 16416 | tf_op jit(solution)/shard_map/ppermute | solution.py:181
  53.7 1.6 collective-permute-start.6
  55.3 2.3 %collective-permute-done.6 = f32[1,4096]{1,0:T(1,128)S(1)} collective-permute-done((f32[1,4096]{1,0:T(1,128)S(1)}, f32[1,4096]{1,0:T(1,128)S(1)}, u32[]{:S(2)}, u32[]{:S(2)}) %collective-permute-start.6) | collective-permute-done | bytes 16416 | tf_op jit(solution)/shard_map/ppermute | solution.py:181
  58.1 1.6 collective-permute-start.7
  59.8 1.1 constant_dynamic-slice_fusion.3
  61.3 1.8 collective-permute-start.12
  63.1 1.5 collective-permute-start.13
  64.7 1.3 collective-permute-done.14
  66.0 1.5 collective-permute-done.12
  67.5 2.0 %collective-permute-done.13 = bf16[2,64,512]{2,1,0:T(8,128)(2,1)S(1)} collective-permute-done((bf16[2,64,512]{2,1,0:T(8,128)(2,1)S(1)}, bf16[2,64,512]{2,1,0:T(8,128)(2,1)S(1)}, u32[]{:S(2)}, u32[]{:S(2)}) %collective-permute-start.13) | collective-permute-done | bytes 131104 | tf_op jit(solution)/shard_map/ppermute | solution.py:181
  69.7 1.3 collective-permute-start.17
  71.0 1.3 collective-permute-start.16
  72.4 1.6 collective-permute-start.9
  74.6 6.0 %collective-permute-start.11 = (bf16[2,64,2048]{2,1,0:T(8,128)(2,1)S(1)}, bf16[2,64,2048]{2,1,0:T(8,128)(2,1)S(1)}, u32[]{:S(2)}, u32[]{:S(2)}) collective-permute-start(bf16[2,64,2048]{2,1,0:T(8,128)(2,1)S(1)} %pad_maximum_fusion.3.own_ref), channel_id=1, source_target_pairs={{0,48},{16,0},{32,16},{48,32},{1,49},{17,1},{33,17},{49,33},{2,50}... | collective-permute-start | bytes 1572872 | tf_op jit(solution)/shard_map/ppermute | solution.py:181
  80.9 2.8 %collective-permute-done.16 = bf16[4,64,512]{2,1,0:T(8,128)(2,1)S(1)} collective-permute-done((bf16[4,64,512]{2,1,0:T(8,128)(2,1)S(1)}, bf16[4,64,512]{2,1,0:T(8,128)(2,1)S(1)}, u32[]{:S(2)}, u32[]{:S(2)}) %collective-permute-start.16) | collective-permute-done | bytes 262176 | tf_op jit(solution)/shard_map/ppermute | solution.py:238
  83.7 1.9 collective-permute-start.15
  85.6 9.2 %collective-permute-done.15 = bf16[4,64,512]{2,1,0:T(8,128)(2,1)S(1)} collective-permute-done((bf16[4,64,512]{2,1,0:T(8,128)(2,1)S(1)}, bf16[4,64,512]{2,1,0:T(8,128)(2,1)S(1)}, u32[]{:S(2)}, u32[]{:S(2)}) %collective-permute-start.15) | collective-permute-done | bytes 262176 | tf_op jit(solution)/shard_map/ppermute | solution.py:238
  95.9 2.0 %collective-permute-start.20 = (bf16[64,2048]{1,0:T(8,128)(2,1)S(1)}, bf16[64,2048]{1,0:T(8,128)(2,1)S(1)}, u32[]{:S(2)}, u32[]{:S(2)}) collective-permute-start(bf16[64,2048]{1,0:T(8,128)(2,1)S(1)} %slice_bitcast_fusion.5), channel_id=1, source_target_pairs={{0,16},{16,32},{32,48},{48,0},{1,17},{17,33},{33,49},{49,1},{2,18}... | collective-permute-start | bytes 786440 | tf_op jit(solution)/shard_map/ppermute | solution.py:181
  97.9 2.4 %collective-permute-start.19 = (bf16[64,2048]{1,0:T(8,128)(2,1)S(1)}, bf16[64,2048]{1,0:T(8,128)(2,1)S(1)}, u32[]{:S(2)}, u32[]{:S(2)}) collective-permute-start(bf16[64,2048]{1,0:T(8,128)(2,1)S(1)} %slice_bitcast_fusion.6), channel_id=1, source_target_pairs={{0,12},{4,0},{8,4},{12,8},{1,13},{5,1},{9,5},{13,9},{2,14},{6,2},{... | collective-permute-start | bytes 786440 | tf_op jit(solution)/shard_map/ppermute | solution.py:181
  100.3 1.9 collective-permute-done.21.last_ref
  102.2 1.3 collective-permute-done.20.first_ref
  104.2 3.6 %collective-permute-done.18.first_ref = bf16[64,2048]{1,0:T(8,128)(2,1)S(1)} collective-permute-done((bf16[64,2048]{1,0:T(8,128)(2,1)S(1)}, bf16[64,2048]{1,0:T(8,128)(2,1)S(1)}, u32[]{:S(2)}, u32[]{:S(2)}) %collective-permute-start.18) | collective-permute-done | bytes 262176 | tf_op jit(solution)/shard_map/ppermute | solution.py:181
  107.9 1.5 shard_map.51.refs_0_
  109.3 1.5 shard_map.52.refs_0_
  110.8 7.9 %collective-permute-start.25 = (bf16[4,4,64,512]{3,2,1,0:T(8,128)(2,1)S(1)}, bf16[4,4,64,512]{3,2,1,0:T(8,128)(2,1)S(1)}, u32[]{:S(2)}, u32[]{:S(2)}) collective-permute-start(bf16[4,4,64,512]{3,2,1,0:T(8,128)(2,1)S(1)} %pad_maximum_fusion.1), channel_id=1, source_target_pairs={{0,2},{64,0},{2,66},{66,64},{16,18},{80,16},{18,82},{82,80},{33,35... | collective-permute-start | bytes 3145736 | tf_op jit(solution)/shard_map/ppermute | solution.py:248
  118.8 2.0 %collective-permute-start.23 = (bf16[8,64,2048]{2,1,0:T(8,128)(2,1)}, bf16[8,64,2048]{2,1,0:T(8,128)(2,1)}, u32[]{:S(2)}, u32[]{:S(2)}) collective-permute-start(bf16[8,64,2048]{2,1,0:T(8,128)(2,1)} %shard_map.51.refs_0_), channel_id=1, source_target_pairs={{0,16},{16,32},{32,48},{48,0},{1,17},{17,33},{33,49},{49,1},{2,18}... | collective-permute-start | bytes 6291464 | tf_op jit(solution)/shard_map/ppermute | solution.py:181
  120.8 2.4 %collective-permute-start.28 = (bf16[8,64,2048]{2,1,0:T(8,128)(2,1)}, bf16[8,64,2048]{2,1,0:T(8,128)(2,1)}, u32[]{:S(2)}, u32[]{:S(2)}) collective-permute-start(bf16[8,64,2048]{2,1,0:T(8,128)(2,1)} %shard_map.52.refs_0_), channel_id=1, source_target_pairs={{0,12},{4,0},{8,4},{12,8},{1,13},{5,1},{9,5},{13,9},{2,14},{6,2},{... | collective-permute-start | bytes 6291464 | tf_op jit(solution)/shard_map/ppermute | solution.py:181
  123.4 7.6 %collective-permute-done.25 = bf16[4,4,64,512]{3,2,1,0:T(8,128)(2,1)S(1)} collective-permute-done((bf16[4,4,64,512]{3,2,1,0:T(8,128)(2,1)S(1)}, bf16[4,4,64,512]{3,2,1,0:T(8,128)(2,1)S(1)}, u32[]{:S(2)}, u32[]{:S(2)}) %collective-permute-start.25) | collective-permute-done | bytes 1048608 | tf_op jit(solution)/shard_map/ppermute | solution.py:248
  131.2 2.7 %collective-permute-start.26 = (bf16[2,4,4,64,512]{4,3,2,1,0:T(8,128)(2,1)S(1)}, bf16[2,4,4,64,512]{4,3,2,1,0:T(8,128)(2,1)}, u32[]{:S(2)}, u32[]{:S(2)}) collective-permute-start(bf16[2,4,4,64,512]{4,3,2,1,0:T(8,128)(2,1)S(1)} %pad_maximum_fusion), channel_id=1, source_target_pairs={{0,1},{16,17},{33,32},{49,48},{2,3},{18,19},{35,34},{51,50},{4,5},... | collective-permute-start | bytes 6291464 | tf_op jit(solution)/shard_map/ppermute | solution.py:254
  134.2 23.4 %collective-permute-done.24.refs_2_ = bf16[8,64,2048]{2,1,0:T(8,128)(2,1)} collective-permute-done((bf16[8,64,2048]{2,1,0:T(8,128)(2,1)}, bf16[8,64,2048]{2,1,0:T(8,128)(2,1)}, u32[]{:S(2)}, u32[]{:S(2)}) %collective-permute-start.24) | collective-permute-done | bytes 2097184 | tf_op jit(solution)/shard_map/ppermute | solution.py:181
  157.6 1.3 slice.53
  159.0 3.8 %collective-permute-start.30 = (bf16[4,64,2048]{2,1,0:T(8,128)(2,1)S(1)}, bf16[4,64,2048]{2,1,0:T(8,128)(2,1)S(1)}, u32[]{:S(2)}, u32[]{:S(2)}) collective-permute-start(bf16[4,64,2048]{2,1,0:T(8,128)(2,1)S(1)} %slice.53), channel_id=1, source_target_pairs={{0,48},{16,0},{32,16},{48,32},{1,49},{17,1},{33,17},{49,33},{2,50}... | collective-permute-start | bytes 3145736 | tf_op jit(solution)/shard_map/ppermute | solution.py:181
  162.7 1.3 slice.52
  164.2 1.3 slice.55
  165.5 2.5 %collective-permute-start.32 = (bf16[4,64,2048]{2,1,0:T(8,128)(2,1)S(1)}, bf16[4,64,2048]{2,1,0:T(8,128)(2,1)S(1)}, u32[]{:S(2)}, u32[]{:S(2)}) collective-permute-start(bf16[4,64,2048]{2,1,0:T(8,128)(2,1)S(1)} %slice.55), channel_id=1, source_target_pairs={{0,12},{4,0},{8,4},{12,8},{1,13},{5,1},{9,5},{13,9},{2,14},{6,2},{... | collective-permute-start | bytes 3145736 | tf_op jit(solution)/shard_map/ppermute | solution.py:181
  168.0 1.3 slice.54
  169.5 3.1 %shard_map.53 = (bf16[32,64,1024]{2,1,0:T(8,128)(2,1)S(1)}, bf16[32,64,1024]{2,1,0:T(8,128)(2,1)S(1)}) custom-call(s32[32]{0:T(128)S(1)} %stack.416.map_ref, s32[2,32]{1,0:T(2,128)S(1)} %pad_add_fusion.1.places_ref, bf16[32,64,512]{2,1,0:T(8,128)(2,1)S(1)} %bitcast.155, bf16[32,64,512]{2,1,0:T(8,128)(2,1)} %bitcast.130.passed_ref), custom_call_target="tpu_custom_call" | custom-call | flops 16777216 | bytes 12582912 | tf_op jit(solution)/shard_map/pallas_call | solution.py:107
  172.5 8.7 %shard_map.54 = (f32[2048,512]{1,0:T(8,128)S(1)}, f32[2048,512]{1,0:T(8,128)S(1)}) custom-call(bf16[8,64,2048]{2,1,0:T(8,128)(2,1)} %shard_map.51.refs_0_, bf16[8,64,2048]{2,1,0:T(8,128)(2,1)} %collective-permute-done.23.refs_1_, bf16[8,64,2048]{2,1,0:T(8,128)(2,1)} %collective-permute-done.24.refs_2_, ...), custom_call_target="tpu_custom_call" | custom-call | flops 12884901888 | bytes 17825792 | tf_op jit(solution)/shard_map/pallas_call | solution.py:146
  181.2 8.7 %shard_map.55 = (f32[2048,512]{1,0:T(8,128)S(1)}, f32[2048,512]{1,0:T(8,128)S(1)}) custom-call(bf16[8,64,2048]{2,1,0:T(8,128)(2,1)} %shard_map.52.refs_0_, bf16[8,64,2048]{2,1,0:T(8,128)(2,1)} %collective-permute-done.27.refs_1_, bf16[8,64,2048]{2,1,0:T(8,128)(2,1)} %collective-permute-done.28.refs_2_, ...), custom_call_target="tpu_custom_call" | custom-call | flops 12884901888 | bytes 17825792 | tf_op jit(solution)/shard_map/pallas_call | solution.py:146
  190.7 4.4 %shard_map.56 = (f32[4096,512]{1,0:T(8,128)}, f32[4096,512]{1,0:T(8,128)}) custom-call(bf16[4,64,2048]{2,1,0:T(8,128)(2,1)S(1)} %collective-permute-done.29.refs_0_, bf16[4,64,2048]{2,1,0:T(8,128)(2,1)S(1)} %collective-permute-done.30.refs_1_, bf16[32,64,1024]{2,1,0:T(8,128)(2,1)S(1)} %get-tuple-element.49.refs_3_.refs_2_, ...), custom_call_target="tpu_custom_call" | custom-call | flops 4294967296 | bytes 19922944 | tf_op jit(solution)/shard_map/pallas_call | solution.py:146
  195.1 4.4 %shard_map.57 = (f32[4096,512]{1,0:T(8,128)}, f32[4096,512]{1,0:T(8,128)}) custom-call(bf16[4,64,2048]{2,1,0:T(8,128)(2,1)S(1)} %collective-permute-done.31.refs_0_, bf16[4,64,2048]{2,1,0:T(8,128)(2,1)S(1)} %collective-permute-done.32.refs_1_, ...), custom_call_target="tpu_custom_call", output_to_operand_aliasing={{0}: (5, {}), {1}: (6, {})} | custom-call | flops 4294967296 | bytes 19922944 | tf_op jit(solution)/shard_map/pallas_call | solution.py:146
  (67 shorter events, 7.2 us)
Async XLA Ops:
  0.6 2.0 copy-start.1
  0.6 2.1 %copy-start = (s32[128]{0:T(128)S(1)}, s32[128]{0:T(128)}, u32[]{:S(2)}) copy-start(s32[128]{0:T(128)} %param.5) | copy-start | bytes 1540
  35.6 4.6 %collective-permute-start.2 = (f32[1,4096]{1,0:T(1,128)S(1)}, f32[1,4096]{1,0:T(1,128)S(1)}, u32[]{:S(2)}, u32[]{:S(2)}) collective-permute-start(f32[1,4096]{1,0:T(1,128)S(1)} %get-tuple-element.35), channel_id=1, source_target_pairs={{0,12},{4,0},{8,4},{12,8},{1,13},{5,1},{9,5},{13,9},{2,14},{6,2},{... | collective-permute-start | bytes 49160 | tf_op jit(solution)/shard_map/ppermute | solution.py:181
  38.5 5.2 %collective-permute-start.1 = (f32[1,4096]{1,0:T(1,128)S(1)}, f32[1,4096]{1,0:T(1,128)S(1)}, u32[]{:S(2)}, u32[]{:S(2)}) collective-permute-start(f32[1,4096]{1,0:T(1,128)S(1)} %get-tuple-element.35), channel_id=1, source_target_pairs={{0,8},{4,12},{8,0},{12,4},{1,9},{5,13},{9,1},{13,5},{2,10},{6,14},... | collective-permute-start | bytes 49160 | tf_op jit(solution)/shard_map/ppermute | solution.py:181
  39.3 4.9 %collective-permute-start = (f32[1,4096]{1,0:T(1,128)S(1)}, f32[1,4096]{1,0:T(1,128)S(1)}, u32[]{:S(2)}, u32[]{:S(2)}) collective-permute-start(f32[1,4096]{1,0:T(1,128)S(1)} %get-tuple-element.35), channel_id=1, source_target_pairs={{0,4},{4,8},{8,12},{12,0},{1,5},{5,9},{9,13},{13,1},{2,6},{6,10},{... | collective-permute-start | bytes 49160 | tf_op jit(solution)/shard_map/ppermute | solution.py:181
  44.3 5.6 %collective-permute-start.5 = (f32[1,4096]{1,0:T(1,128)S(1)}, f32[1,4096]{1,0:T(1,128)S(1)}, u32[]{:S(2)}, u32[]{:S(2)}) collective-permute-start(f32[1,4096]{1,0:T(1,128)S(1)} %add_add_fusion.1), channel_id=1, source_target_pairs={{0,48},{16,0},{32,16},{48,32},{1,49},{17,1},{33,17},{49,33},{2,50}... | collective-permute-start | bytes 49160 | tf_op jit(solution)/shard_map/ppermute | solution.py:181
  48.4 5.2 %collective-permute-start.4 = (f32[1,4096]{1,0:T(1,128)S(1)}, f32[1,4096]{1,0:T(1,128)S(1)}, u32[]{:S(2)}, u32[]{:S(2)}) collective-permute-start(f32[1,4096]{1,0:T(1,128)S(1)} %add_add_fusion.1), channel_id=1, source_target_pairs={{0,32},{16,48},{32,0},{48,16},{1,33},{17,49},{33,1},{49,17},{2,34}... | collective-permute-start | bytes 49160 | tf_op jit(solution)/shard_map/ppermute | solution.py:181
  48.4 5.2 %collective-permute-start.3 = (f32[1,4096]{1,0:T(1,128)S(1)}, f32[1,4096]{1,0:T(1,128)S(1)}, u32[]{:S(2)}, u32[]{:S(2)}) collective-permute-start(f32[1,4096]{1,0:T(1,128)S(1)} %add_add_fusion.1), channel_id=1, source_target_pairs={{0,16},{16,32},{32,48},{48,0},{1,17},{17,33},{33,49},{49,1},{2,18}... | collective-permute-start | bytes 49160 | tf_op jit(solution)/shard_map/ppermute | solution.py:181
  53.7 4.0 %collective-permute-start.6 = (f32[1,4096]{1,0:T(1,128)S(1)}, f32[1,4096]{1,0:T(1,128)S(1)}, u32[]{:S(2)}, u32[]{:S(2)}) collective-permute-start(f32[1,4096]{1,0:T(1,128)S(1)} %add_add_fusion), channel_id=1, source_target_pairs={{0,64},{64,0},{1,65},{65,1},{2,66},{66,2},{3,67},{67,3},{4,68},{68... | collective-permute-start | bytes 49160 | tf_op jit(solution)/shard_map/ppermute | solution.py:181
  58.1 14.2 %collective-permute-start.7 = (bf16[64,4096]{1,0:T(8,128)(2,1)S(1)}, bf16[64,4096]{1,0:T(8,128)(2,1)S(1)}, u32[]{:S(2)}, u32[]{:S(2)}) collective-permute-start(bf16[64,4096]{1,0:T(8,128)(2,1)S(1)} %subtract_convert_fusion), channel_id=1, source_target_pairs={{0,64},{64,0},{1,65},{65,1},{2,66},{66,2},{3,67},{67,3},{4,68},{68... | collective-permute-start | bytes 1572872 | tf_op jit(solution)/shard_map/ppermute | solution.py:181
  61.0 5.0 %collective-permute-start.14 = (bf16[2,64,512]{2,1,0:T(8,128)(2,1)S(1)}, bf16[2,64,512]{2,1,0:T(8,128)(2,1)S(1)}, u32[]{:S(2)}, u32[]{:S(2)}) collective-permute-start(bf16[2,64,512]{2,1,0:T(8,128)(2,1)S(1)} %bitcast.165), channel_id=1, source_target_pairs={{0,12},{4,0},{8,4},{12,8},{1,13},{5,1},{9,5},{13,9},{2,14},{6,2},{... | collective-permute-start | bytes 393224 | tf_op jit(solution)/shard_map/ppermute | solution.py:181
  61.3 6.2 %collective-permute-start.12 = (bf16[2,64,512]{2,1,0:T(8,128)(2,1)S(1)}, bf16[2,64,512]{2,1,0:T(8,128)(2,1)S(1)}, u32[]{:S(2)}, u32[]{:S(2)}) collective-permute-start(bf16[2,64,512]{2,1,0:T(8,128)(2,1)S(1)} %bitcast.164), channel_id=1, source_target_pairs={{0,4},{4,8},{8,12},{12,0},{1,5},{5,9},{9,13},{13,1},{2,6},{6,10},{... | collective-permute-start | bytes 393224 | tf_op jit(solution)/shard_map/ppermute | solution.py:181
  63.1 6.5 %collective-permute-start.13 = (bf16[2,64,512]{2,1,0:T(8,128)(2,1)S(1)}, bf16[2,64,512]{2,1,0:T(8,128)(2,1)S(1)}, u32[]{:S(2)}, u32[]{:S(2)}) collective-permute-start(bf16[2,64,512]{2,1,0:T(8,128)(2,1)S(1)} %bitcast.163), channel_id=1, source_target_pairs={{0,8},{4,12},{8,0},{12,4},{1,9},{5,13},{9,1},{13,5},{2,10},{6,14},... | collective-permute-start | bytes 393224 | tf_op jit(solution)/shard_map/ppermute | solution.py:181
  69.7 11.1 %collective-permute-start.17 = (bf16[4,64,512]{2,1,0:T(8,128)(2,1)S(1)}, bf16[4,64,512]{2,1,0:T(8,128)(2,1)S(1)}, u32[]{:S(2)}, u32[]{:S(2)}) collective-permute-start(bf16[4,64,512]{2,1,0:T(8,128)(2,1)S(1)} %get-tuple-element.67), channel_id=1, source_target_pairs={{1,49},{16,0},{32,16},{49,33},{3,51},{18,2},{34,18},{51,35},{5,53}... | collective-permute-start | bytes 786440 | tf_op jit(solution)/shard_map/ppermute | solution.py:238
  71.0 12.6 %collective-permute-start.16 = (bf16[4,64,512]{2,1,0:T(8,128)(2,1)S(1)}, bf16[4,64,512]{2,1,0:T(8,128)(2,1)S(1)}, u32[]{:S(2)}, u32[]{:S(2)}) collective-permute-start(bf16[4,64,512]{2,1,0:T(8,128)(2,1)S(1)} %get-tuple-element.68), channel_id=1, source_target_pairs={{1,33},{17,49},{32,0},{48,16},{3,35},{19,51},{34,2},{50,18},{5,37}... | collective-permute-start | bytes 786440 | tf_op jit(solution)/shard_map/ppermute | solution.py:238
  72.4 22.5 %collective-permute-start.9 = (bf16[2,64,2048]{2,1,0:T(8,128)(2,1)S(1)}, bf16[2,64,2048]{2,1,0:T(8,128)(2,1)S(1)}, u32[]{:S(2)}, u32[]{:S(2)}) collective-permute-start(bf16[2,64,2048]{2,1,0:T(8,128)(2,1)S(1)} %pad_maximum_fusion.2.own_ref), channel_id=1, source_target_pairs={{0,12},{4,0},{8,4},{12,8},{1,13},{5,1},{9,5},{13,9},{2,14},{6,2},{... | collective-permute-start | bytes 1572872 | tf_op jit(solution)/shard_map/ppermute | solution.py:181
  74.0 20.9 %collective-permute-start.8 = (bf16[2,64,2048]{2,1,0:T(8,128)(2,1)S(1)}, bf16[2,64,2048]{2,1,0:T(8,128)(2,1)S(1)}, u32[]{:S(2)}, u32[]{:S(2)}) collective-permute-start(bf16[2,64,2048]{2,1,0:T(8,128)(2,1)S(1)} %pad_maximum_fusion.2.own_ref), channel_id=1, source_target_pairs={{0,4},{4,8},{8,12},{12,0},{1,5},{5,9},{9,13},{13,1},{2,6},{6,10},{... | collective-permute-start | bytes 1572872 | tf_op jit(solution)/shard_map/ppermute | solution.py:181
  74.6 20.3 %collective-permute-start.11 = (bf16[2,64,2048]{2,1,0:T(8,128)(2,1)S(1)}, bf16[2,64,2048]{2,1,0:T(8,128)(2,1)S(1)}, u32[]{:S(2)}, u32[]{:S(2)}) collective-permute-start(bf16[2,64,2048]{2,1,0:T(8,128)(2,1)S(1)} %pad_maximum_fusion.3.own_ref), channel_id=1, source_target_pairs={{0,48},{16,0},{32,16},{48,32},{1,49},{17,1},{33,17},{49,33},{2,50}... | collective-permute-start | bytes 1572872 | tf_op jit(solution)/shard_map/ppermute | solution.py:181
  80.9 14.1 %collective-permute-start.10 = (bf16[2,64,2048]{2,1,0:T(8,128)(2,1)S(1)}, bf16[2,64,2048]{2,1,0:T(8,128)(2,1)S(1)}, u32[]{:S(2)}, u32[]{:S(2)}) collective-permute-start(bf16[2,64,2048]{2,1,0:T(8,128)(2,1)S(1)} %pad_maximum_fusion.3.own_ref), channel_id=1, source_target_pairs={{0,16},{16,32},{32,48},{48,0},{1,17},{17,33},{33,49},{49,1},{2,18}... | collective-permute-start | bytes 1572872 | tf_op jit(solution)/shard_map/ppermute | solution.py:181
  83.7 11.1 %collective-permute-start.15 = (bf16[4,64,512]{2,1,0:T(8,128)(2,1)S(1)}, bf16[4,64,512]{2,1,0:T(8,128)(2,1)S(1)}, u32[]{:S(2)}, u32[]{:S(2)}) collective-permute-start(bf16[4,64,512]{2,1,0:T(8,128)(2,1)S(1)} %get-tuple-element.69), channel_id=1, source_target_pairs={{0,16},{17,33},{33,49},{48,0},{2,18},{19,35},{35,51},{50,2},{4,20}... | collective-permute-start | bytes 786440 | tf_op jit(solution)/shard_map/ppermute | solution.py:238
  95.0 12.9 %collective-permute-start.22 = (bf16[4,4,64,512]{3,2,1,0:T(8,128)(2,1)S(1)}, bf16[4,4,64,512]{3,2,1,0:T(8,128)(2,1)S(1)}, u32[]{:S(2)}, u32[]{:S(2)}) collective-permute-start(bf16[4,4,64,512]{3,2,1,0:T(8,128)(2,1)S(1)} %pad_maximum_fusion.1), channel_id=1, source_target_pairs={{64,2},{2,64},{80,18},{18,80},{97,35},{35,97},{113,51},{51,113},{6... | collective-permute-start | bytes 3145736 | tf_op jit(solution)/shard_map/ppermute | solution.py:248
  95.8 6.4 %collective-permute-start.21 = (bf16[64,2048]{1,0:T(8,128)(2,1)S(1)}, bf16[64,2048]{1,0:T(8,128)(2,1)S(1)}, u32[]{:S(2)}, u32[]{:S(2)}) collective-permute-start(bf16[64,2048]{1,0:T(8,128)(2,1)S(1)} %slice_bitcast_fusion.4), channel_id=1, source_target_pairs={{0,48},{16,0},{32,16},{48,32},{1,49},{17,1},{33,17},{49,33},{2,50}... | collective-permute-start | bytes 786440 | tf_op jit(solution)/shard_map/ppermute | solution.py:181
  95.9 7.7 %collective-permute-start.20 = (bf16[64,2048]{1,0:T(8,128)(2,1)S(1)}, bf16[64,2048]{1,0:T(8,128)(2,1)S(1)}, u32[]{:S(2)}, u32[]{:S(2)}) collective-permute-start(bf16[64,2048]{1,0:T(8,128)(2,1)S(1)} %slice_bitcast_fusion.5), channel_id=1, source_target_pairs={{0,16},{16,32},{32,48},{48,0},{1,17},{17,33},{33,49},{49,1},{2,18}... | collective-permute-start | bytes 786440 | tf_op jit(solution)/shard_map/ppermute | solution.py:181
  97.9 6.4 %collective-permute-start.19 = (bf16[64,2048]{1,0:T(8,128)(2,1)S(1)}, bf16[64,2048]{1,0:T(8,128)(2,1)S(1)}, u32[]{:S(2)}, u32[]{:S(2)}) collective-permute-start(bf16[64,2048]{1,0:T(8,128)(2,1)S(1)} %slice_bitcast_fusion.6), channel_id=1, source_target_pairs={{0,12},{4,0},{8,4},{12,8},{1,13},{5,1},{9,5},{13,9},{2,14},{6,2},{... | collective-permute-start | bytes 786440 | tf_op jit(solution)/shard_map/ppermute | solution.py:181
  100.3 7.6 %collective-permute-start.18 = (bf16[64,2048]{1,0:T(8,128)(2,1)S(1)}, bf16[64,2048]{1,0:T(8,128)(2,1)S(1)}, u32[]{:S(2)}, u32[]{:S(2)}) collective-permute-start(bf16[64,2048]{1,0:T(8,128)(2,1)S(1)} %slice_bitcast_fusion.7), channel_id=1, source_target_pairs={{0,4},{4,8},{8,12},{12,0},{1,5},{5,9},{9,13},{13,1},{2,6},{6,10},{... | collective-permute-start | bytes 786440 | tf_op jit(solution)/shard_map/ppermute | solution.py:181
  110.8 20.2 %collective-permute-start.25 = (bf16[4,4,64,512]{3,2,1,0:T(8,128)(2,1)S(1)}, bf16[4,4,64,512]{3,2,1,0:T(8,128)(2,1)S(1)}, u32[]{:S(2)}, u32[]{:S(2)}) collective-permute-start(bf16[4,4,64,512]{3,2,1,0:T(8,128)(2,1)S(1)} %pad_maximum_fusion.1), channel_id=1, source_target_pairs={{0,2},{64,0},{2,66},{66,64},{16,18},{80,16},{18,82},{82,80},{33,35... | collective-permute-start | bytes 3145736 | tf_op jit(solution)/shard_map/ppermute | solution.py:248
  118.7 38.9 %collective-permute-start.24 = (bf16[8,64,2048]{2,1,0:T(8,128)(2,1)}, bf16[8,64,2048]{2,1,0:T(8,128)(2,1)}, u32[]{:S(2)}, u32[]{:S(2)}) collective-permute-start(bf16[8,64,2048]{2,1,0:T(8,128)(2,1)} %shard_map.51.refs_0_), channel_id=1, source_target_pairs={{0,48},{16,0},{32,16},{48,32},{1,49},{17,1},{33,17},{49,33},{2,50}... | collective-permute-start | bytes 6291464 | tf_op jit(solution)/shard_map/ppermute | solution.py:181
  118.8 43.9 %collective-permute-start.23 = (bf16[8,64,2048]{2,1,0:T(8,128)(2,1)}, bf16[8,64,2048]{2,1,0:T(8,128)(2,1)}, u32[]{:S(2)}, u32[]{:S(2)}) collective-permute-start(bf16[8,64,2048]{2,1,0:T(8,128)(2,1)} %shard_map.51.refs_0_), channel_id=1, source_target_pairs={{0,16},{16,32},{32,48},{48,0},{1,17},{17,33},{33,49},{49,1},{2,18}... | collective-permute-start | bytes 6291464 | tf_op jit(solution)/shard_map/ppermute | solution.py:181
  120.8 43.4 %collective-permute-start.28 = (bf16[8,64,2048]{2,1,0:T(8,128)(2,1)}, bf16[8,64,2048]{2,1,0:T(8,128)(2,1)}, u32[]{:S(2)}, u32[]{:S(2)}) collective-permute-start(bf16[8,64,2048]{2,1,0:T(8,128)(2,1)} %shard_map.52.refs_0_), channel_id=1, source_target_pairs={{0,12},{4,0},{8,4},{12,8},{1,13},{5,1},{9,5},{13,9},{2,14},{6,2},{... | collective-permute-start | bytes 6291464 | tf_op jit(solution)/shard_map/ppermute | solution.py:181
  123.2 44.8 %collective-permute-start.27 = (bf16[8,64,2048]{2,1,0:T(8,128)(2,1)}, bf16[8,64,2048]{2,1,0:T(8,128)(2,1)}, u32[]{:S(2)}, u32[]{:S(2)}) collective-permute-start(bf16[8,64,2048]{2,1,0:T(8,128)(2,1)} %shard_map.52.refs_0_), channel_id=1, source_target_pairs={{0,4},{4,8},{8,12},{12,0},{1,5},{5,9},{9,13},{13,1},{2,6},{6,10},{... | collective-permute-start | bytes 6291464 | tf_op jit(solution)/shard_map/ppermute | solution.py:181
  131.2 38.3 %collective-permute-start.26 = (bf16[2,4,4,64,512]{4,3,2,1,0:T(8,128)(2,1)S(1)}, bf16[2,4,4,64,512]{4,3,2,1,0:T(8,128)(2,1)}, u32[]{:S(2)}, u32[]{:S(2)}) collective-permute-start(bf16[2,4,4,64,512]{4,3,2,1,0:T(8,128)(2,1)S(1)} %pad_maximum_fusion), channel_id=1, source_target_pairs={{0,1},{16,17},{33,32},{49,48},{2,3},{18,19},{35,34},{51,50},{4,5},... | collective-permute-start | bytes 6291464 | tf_op jit(solution)/shard_map/ppermute | solution.py:254
  159.0 31.0 %collective-permute-start.30 = (bf16[4,64,2048]{2,1,0:T(8,128)(2,1)S(1)}, bf16[4,64,2048]{2,1,0:T(8,128)(2,1)S(1)}, u32[]{:S(2)}, u32[]{:S(2)}) collective-permute-start(bf16[4,64,2048]{2,1,0:T(8,128)(2,1)S(1)} %slice.53), channel_id=1, source_target_pairs={{0,48},{16,0},{32,16},{48,32},{1,49},{17,1},{33,17},{49,33},{2,50}... | collective-permute-start | bytes 3145736 | tf_op jit(solution)/shard_map/ppermute | solution.py:181
  164.1 25.9 %collective-permute-start.29 = (bf16[4,64,2048]{2,1,0:T(8,128)(2,1)S(1)}, bf16[4,64,2048]{2,1,0:T(8,128)(2,1)S(1)}, u32[]{:S(2)}, u32[]{:S(2)}) collective-permute-start(bf16[4,64,2048]{2,1,0:T(8,128)(2,1)S(1)} %slice.52), channel_id=1, source_target_pairs={{0,16},{16,32},{32,48},{48,0},{1,17},{17,33},{33,49},{49,1},{2,18}... | collective-permute-start | bytes 3145736 | tf_op jit(solution)/shard_map/ppermute | solution.py:181
  165.5 24.5 %collective-permute-start.32 = (bf16[4,64,2048]{2,1,0:T(8,128)(2,1)S(1)}, bf16[4,64,2048]{2,1,0:T(8,128)(2,1)S(1)}, u32[]{:S(2)}, u32[]{:S(2)}) collective-permute-start(bf16[4,64,2048]{2,1,0:T(8,128)(2,1)S(1)} %slice.55), channel_id=1, source_target_pairs={{0,12},{4,0},{8,4},{12,8},{1,13},{5,1},{9,5},{13,9},{2,14},{6,2},{... | collective-permute-start | bytes 3145736 | tf_op jit(solution)/shard_map/ppermute | solution.py:181
  169.4 21.3 %collective-permute-start.31 = (bf16[4,64,2048]{2,1,0:T(8,128)(2,1)S(1)}, bf16[4,64,2048]{2,1,0:T(8,128)(2,1)S(1)}, u32[]{:S(2)}, u32[]{:S(2)}) collective-permute-start(bf16[4,64,2048]{2,1,0:T(8,128)(2,1)S(1)} %slice.54), channel_id=1, source_target_pairs={{0,4},{4,8},{8,12},{12,0},{1,5},{5,9},{9,13},{13,1},{2,6},{6,10},{... | collective-permute-start | bytes 3145736 | tf_op jit(solution)/shard_map/ppermute | solution.py:181

commit v5 on v4

--- a/solution.py
+++ b/solution.py
@@ -84,13 +84,13 @@
         def block_at(number):
             return cols_ref[map_ref[number] - skipped].astype(jnp.float32)
 
-        @pl.loop(0, blocks)
+        @pl.loop(0, blocks, unroll=4)
         def _(block):
             here = block_at(block)
             before = block_at(jnp.maximum(block - 1, 0))
             after = block_at(jnp.minimum(block + 1, blocks - 1))
             inner = jnp.logical_and(block > 0, block < blocks - 1)
-            weighted = jnp.where(inner, 2.0 * here, here).astype(jnp.bfloat16)
+            weighted = (here * jnp.where(inner, 2.0, 1.0)).astype(jnp.bfloat16)
             lagged = jnp.where(block > 0, before, 0.0) + jnp.where(block < blocks - 1, after, 0.0)
             lagged = lagged.astype(jnp.bfloat16)
             for stream, out_ref in enumerate(out_refs):

time: 200 us -> 200 us (level)
  no operation moved by 1% of the time
where the time goes in v5:
time: 200 us
  waiting for transfers between devices  66.6 us (33%)
  Pallas kernels  65.2 us (33%)
  starting transfers between devices  56.3 us (28%)
  local copies, waits for them, and re-layouts  9.54 us (5%)
    ppermute x27, waiting for transfers between devices, moved(): lax.ppermute(array, axis, [(i, (i + by) % length) for i in range(length)])  46.8 us
    ppermute x27, starting transfers between devices, moved(): lax.ppermute(array, axis, [(i, (i + by) % length) for i in range(length)])  40.5 us
    pallas_call x1, Pallas kernels, contact_features(): pl.pallas_call(feature_kernel, out_shape=(jax.ShapeDtypeStruct((frames, w...  32.8 us
    pallas_call x4, Pallas kernels, products(): pl.pallas_call(lambda *refs: product_kernel(count, factor, started, *refs...  26.3 us
    ppermute x3, waiting for transfers between devices, columns_along_z(): along_z.append(lax.ppermute(piece, ('z', 'c'), pairs))  12.2 us
    ppermute x2, starting transfers between devices, columns_along_y(): return lax.ppermute(along_z, ('yl', 'z', 'yh', 'c'), pairs)  8.63 us
    ppermute x2, waiting for transfers between devices, columns_along_y(): return lax.ppermute(along_z, ('yl', 'z', 'yh', 'c'), pairs)  7.64 us
    slice x4, local copies, waits for them, and re-layouts, far_block(): return (moved(behind[:half], axis, 1), moved(ahead[half:], axis, -1))  5.29 us
  transfers between devices with their start and end apart: 33, of which 18 were waited for; matrix products, arithmetic and copies ran while one was open for 4% of the time, Pallas kernels for 10%

profile of v5, /device:TPU:0, one launch (start us, length us, event | category | flops | bytes accessed | tf_op | source)
XLA Modules:
  0.0 199.6 jit_solution(17289833483925846099)
XLA Ops:
  0.7 1.9 copy.11
  2.8 32.8 %shard_map.50 = (f32[64,4096]{1,0:T(8,128)S(1)}, f32[1,4096]{1,0:T(1,128)S(1)}) custom-call(s32[8,256]{1,0:T(8,128)S(1)} %stack.368.index_ref, f32[1536,256]{1,0:T(8,128)S(1)} %bitcast.156), custom_call_target="tpu_custom_call" | custom-call | flops 201326592 | bytes 4194304 | tf_op jit(solution)/shard_map/pallas_call | solution.py:66
  35.6 2.9 %collective-permute-start.2 = (f32[1,4096]{1,0:T(1,128)S(1)}, f32[1,4096]{1,0:T(1,128)S(1)}, u32[]{:S(2)}, u32[]{:S(2)}) collective-permute-start(f32[1,4096]{1,0:T(1,128)S(1)} %get-tuple-element.35), channel_id=1, source_target_pairs={{0,12},{4,0},{8,4},{12,8},{1,13},{5,1},{9,5},{13,9},{2,14},{6,2},{... | collective-permute-start | bytes 49160 | tf_op jit(solution)/shard_map/ppermute | solution.py:181
  39.3 0.9 collective-permute-start
  40.2 3.5 %collective-permute-done.1 = f32[1,4096]{1,0:T(1,128)S(1)} collective-permute-done((f32[1,4096]{1,0:T(1,128)S(1)}, f32[1,4096]{1,0:T(1,128)S(1)}, u32[]{:S(2)}, u32[]{:S(2)}) %collective-permute-start.1) | collective-permute-done | bytes 16416 | tf_op jit(solution)/shard_map/ppermute | solution.py:181
  44.3 4.1 %collective-permute-start.5 = (f32[1,4096]{1,0:T(1,128)S(1)}, f32[1,4096]{1,0:T(1,128)S(1)}, u32[]{:S(2)}, u32[]{:S(2)}) collective-permute-start(f32[1,4096]{1,0:T(1,128)S(1)} %add_add_fusion.1), channel_id=1, source_target_pairs={{0,48},{16,0},{32,16},{48,32},{1,49},{17,1},{33,17},{49,33},{2,50}... | collective-permute-start | bytes 49160 | tf_op jit(solution)/shard_map/ppermute | solution.py:181
  48.4 1.3 collective-permute-start.3
  49.8 3.8 %collective-permute-done.4 = f32[1,4096]{1,0:T(1,128)S(1)} collective-permute-done((f32[1,4096]{1,0:T(1,128)S(1)}, f32[1,4096]{1,0:T(1,128)S(1)}, u32[]{:S(2)}, u32[]{:S(2)}) %collective-permute-start.4) | collective-permute-done | bytes 16416 | tf_op jit(solution)/shard_map/ppermute | solution.py:181
  53.7 1.6 collective-permute-start.6
  55.3 2.3 %collective-permute-done.6 = f32[1,4096]{1,0:T(1,128)S(1)} collective-permute-done((f32[1,4096]{1,0:T(1,128)S(1)}, f32[1,4096]{1,0:T(1,128)S(1)}, u32[]{:S(2)}, u32[]{:S(2)}) %collective-permute-start.6) | collective-permute-done | bytes 16416 | tf_op jit(solution)/shard_map/ppermute | solution.py:181
  58.1 1.6 collective-permute-start.7
  59.8 1.1 constant_dynamic-slice_fusion.3
  61.3 1.8 collective-permute-start.12
  63.1 1.5 collective-permute-start.13
  64.7 1.3 collective-permute-done.14
  66.0 1.5 collective-permute-done.12
  67.5 2.0 %collective-permute-done.13 = bf16[2,64,512]{2,1,0:T(8,128)(2,1)S(1)} collective-permute-done((bf16[2,64,512]{2,1,0:T(8,128)(2,1)S(1)}, bf16[2,64,512]{2,1,0:T(8,128)(2,1)S(1)}, u32[]{:S(2)}, u32[]{:S(2)}) %collective-permute-start.13) | collective-permute-done | bytes 131104 | tf_op jit(solution)/shard_map/ppermute | solution.py:181
  69.7 1.3 collective-permute-start.17
  71.0 1.3 collective-permute-start.16
  72.4 1.6 collective-permute-start.9
  74.6 6.0 %collective-permute-start.11 = (bf16[2,64,2048]{2,1,0:T(8,128)(2,1)S(1)}, bf16[2,64,2048]{2,1,0:T(8,128)(2,1)S(1)}, u32[]{:S(2)}, u32[]{:S(2)}) collective-permute-start(bf16[2,64,2048]{2,1,0:T(8,128)(2,1)S(1)} %pad_maximum_fusion.3.own_ref), channel_id=1, source_target_pairs={{0,48},{16,0},{32,16},{48,32},{1,49},{17,1},{33,17},{49,33},{2,50}... | collective-permute-start | bytes 1572872 | tf_op jit(solution)/shard_map/ppermute | solution.py:181
  80.9 2.8 %collective-permute-done.16 = bf16[4,64,512]{2,1,0:T(8,128)(2,1)S(1)} collective-permute-done((bf16[4,64,512]{2,1,0:T(8,128)(2,1)S(1)}, bf16[4,64,512]{2,1,0:T(8,128)(2,1)S(1)}, u32[]{:S(2)}, u32[]{:S(2)}) %collective-permute-start.16) | collective-permute-done | bytes 262176 | tf_op jit(solution)/shard_map/ppermute | solution.py:238
  83.7 1.9 collective-permute-start.15
  85.6 9.2 %collective-permute-done.15 = bf16[4,64,512]{2,1,0:T(8,128)(2,1)S(1)} collective-permute-done((bf16[4,64,512]{2,1,0:T(8,128)(2,1)S(1)}, bf16[4,64,512]{2,1,0:T(8,128)(2,1)S(1)}, u32[]{:S(2)}, u32[]{:S(2)}) %collective-permute-start.15) | collective-permute-done | bytes 262176 | tf_op jit(solution)/shard_map/ppermute | solution.py:238
  95.9 2.0 %collective-permute-start.20 = (bf16[64,2048]{1,0:T(8,128)(2,1)S(1)}, bf16[64,2048]{1,0:T(8,128)(2,1)S(1)}, u32[]{:S(2)}, u32[]{:S(2)}) collective-permute-start(bf16[64,2048]{1,0:T(8,128)(2,1)S(1)} %slice_bitcast_fusion.5), channel_id=1, source_target_pairs={{0,16},{16,32},{32,48},{48,0},{1,17},{17,33},{33,49},{49,1},{2,18}... | collective-permute-start | bytes 786440 | tf_op jit(solution)/shard_map/ppermute | solution.py:181
  97.9 2.4 %collective-permute-start.19 = (bf16[64,2048]{1,0:T(8,128)(2,1)S(1)}, bf16[64,2048]{1,0:T(8,128)(2,1)S(1)}, u32[]{:S(2)}, u32[]{:S(2)}) collective-permute-start(bf16[64,2048]{1,0:T(8,128)(2,1)S(1)} %slice_bitcast_fusion.6), channel_id=1, source_target_pairs={{0,12},{4,0},{8,4},{12,8},{1,13},{5,1},{9,5},{13,9},{2,14},{6,2},{... | collective-permute-start | bytes 786440 | tf_op jit(solution)/shard_map/ppermute | solution.py:181
  100.3 1.9 collective-permute-done.21.last_ref
  102.2 1.3 collective-permute-done.20.first_ref
  104.2 3.6 %collective-permute-done.18.first_ref = bf16[64,2048]{1,0:T(8,128)(2,1)S(1)} collective-permute-done((bf16[64,2048]{1,0:T(8,128)(2,1)S(1)}, bf16[64,2048]{1,0:T(8,128)(2,1)S(1)}, u32[]{:S(2)}, u32[]{:S(2)}) %collective-permute-start.18) | collective-permute-done | bytes 262176 | tf_op jit(solution)/shard_map/ppermute | solution.py:181
  107.9 1.5 shard_map.51.refs_0_
  109.3 1.5 shard_map.52.refs_0_
  110.8 7.9 %collective-permute-start.25 = (bf16[4,4,64,512]{3,2,1,0:T(8,128)(2,1)S(1)}, bf16[4,4,64,512]{3,2,1,0:T(8,128)(2,1)S(1)}, u32[]{:S(2)}, u32[]{:S(2)}) collective-permute-start(bf16[4,4,64,512]{3,2,1,0:T(8,128)(2,1)S(1)} %pad_maximum_fusion.1), channel_id=1, source_target_pairs={{0,2},{64,0},{2,66},{66,64},{16,18},{80,16},{18,82},{82,80},{33,35... | collective-permute-start | bytes 3145736 | tf_op jit(solution)/shard_map/ppermute | solution.py:248
  118.8 2.0 %collective-permute-start.23 = (bf16[8,64,2048]{2,1,0:T(8,128)(2,1)}, bf16[8,64,2048]{2,1,0:T(8,128)(2,1)}, u32[]{:S(2)}, u32[]{:S(2)}) collective-permute-start(bf16[8,64,2048]{2,1,0:T(8,128)(2,1)} %shard_map.51.refs_0_), channel_id=1, source_target_pairs={{0,16},{16,32},{32,48},{48,0},{1,17},{17,33},{33,49},{49,1},{2,18}... | collective-permute-start | bytes 6291464 | tf_op jit(solution)/shard_map/ppermute | solution.py:181
  120.8 2.4 %collective-permute-start.28 = (bf16[8,64,2048]{2,1,0:T(8,128)(2,1)}, bf16[8,64,2048]{2,1,0:T(8,128)(2,1)}, u32[]{:S(2)}, u32[]{:S(2)}) collective-permute-start(bf16[8,64,2048]{2,1,0:T(8,128)(2,1)} %shard_map.52.refs_0_), channel_id=1, source_target_pairs={{0,12},{4,0},{8,4},{12,8},{1,13},{5,1},{9,5},{13,9},{2,14},{6,2},{... | collective-permute-start | bytes 6291464 | tf_op jit(solution)/shard_map/ppermute | solution.py:181
  123.4 7.6 %collective-permute-done.25 = bf16[4,4,64,512]{3,2,1,0:T(8,128)(2,1)S(1)} collective-permute-done((bf16[4,4,64,512]{3,2,1,0:T(8,128)(2,1)S(1)}, bf16[4,4,64,512]{3,2,1,0:T(8,128)(2,1)S(1)}, u32[]{:S(2)}, u32[]{:S(2)}) %collective-permute-start.25) | collective-permute-done | bytes 1048608 | tf_op jit(solution)/shard_map/ppermute | solution.py:248
  131.2 2.7 %collective-permute-start.26 = (bf16[2,4,4,64,512]{4,3,2,1,0:T(8,128)(2,1)S(1)}, bf16[2,4,4,64,512]{4,3,2,1,0:T(8,128)(2,1)}, u32[]{:S(2)}, u32[]{:S(2)}) collective-permute-start(bf16[2,4,4,64,512]{4,3,2,1,0:T(8,128)(2,1)S(1)} %pad_maximum_fusion), channel_id=1, source_target_pairs={{0,1},{16,17},{33,32},{49,48},{2,3},{18,19},{35,34},{51,50},{4,5},... | collective-permute-start | bytes 6291464 | tf_op jit(solution)/shard_map/ppermute | solution.py:254
  134.2 23.4 %collective-permute-done.24.refs_2_ = bf16[8,64,2048]{2,1,0:T(8,128)(2,1)} collective-permute-done((bf16[8,64,2048]{2,1,0:T(8,128)(2,1)}, bf16[8,64,2048]{2,1,0:T(8,128)(2,1)}, u32[]{:S(2)}, u32[]{:S(2)}) %collective-permute-start.24) | collective-permute-done | bytes 2097184 | tf_op jit(solution)/shard_map/ppermute | solution.py:181
  157.6 1.3 slice.53
  159.0 3.8 %collective-permute-start.30 = (bf16[4,64,2048]{2,1,0:T(8,128)(2,1)S(1)}, bf16[4,64,2048]{2,1,0:T(8,128)(2,1)S(1)}, u32[]{:S(2)}, u32[]{:S(2)}) collective-permute-start(bf16[4,64,2048]{2,1,0:T(8,128)(2,1)S(1)} %slice.53), channel_id=1, source_target_pairs={{0,48},{16,0},{32,16},{48,32},{1,49},{17,1},{33,17},{49,33},{2,50}... | collective-permute-start | bytes 3145736 | tf_op jit(solution)/shard_map/ppermute | solution.py:181
  162.7 1.3 slice.52
  164.2 1.3 slice.55
  165.5 2.5 %collective-permute-start.32 = (bf16[4,64,2048]{2,1,0:T(8,128)(2,1)S(1)}, bf16[4,64,2048]{2,1,0:T(8,128)(2,1)S(1)}, u32[]{:S(2)}, u32[]{:S(2)}) collective-permute-start(bf16[4,64,2048]{2,1,0:T(8,128)(2,1)S(1)} %slice.55), channel_id=1, source_target_pairs={{0,12},{4,0},{8,4},{12,8},{1,13},{5,1},{9,5},{13,9},{2,14},{6,2},{... | collective-permute-start | bytes 3145736 | tf_op jit(solution)/shard_map/ppermute | solution.py:181
  168.0 1.3 slice.54
  169.5 3.3 %shard_map.53 = (bf16[32,64,1024]{2,1,0:T(8,128)(2,1)S(1)}, bf16[32,64,1024]{2,1,0:T(8,128)(2,1)S(1)}) custom-call(s32[32]{0:T(128)S(1)} %stack.416.map_ref, s32[2,32]{1,0:T(2,128)S(1)} %pad_add_fusion.1.places_ref, bf16[32,64,512]{2,1,0:T(8,128)(2,1)S(1)} %bitcast.155, bf16[32,64,512]{2,1,0:T(8,128)(2,1)} %bitcast.130.passed_ref), custom_call_target="tpu_custom_call" | custom-call | flops 16777216 | bytes 12582912 | tf_op jit(solution)/shard_map/pallas_call | solution.py:107
  172.7 8.7 %shard_map.54 = (f32[2048,512]{1,0:T(8,128)S(1)}, f32[2048,512]{1,0:T(8,128)S(1)}) custom-call(bf16[8,64,2048]{2,1,0:T(8,128)(2,1)} %shard_map.51.refs_0_, bf16[8,64,2048]{2,1,0:T(8,128)(2,1)} %collective-permute-done.23.refs_1_, bf16[8,64,2048]{2,1,0:T(8,128)(2,1)} %collective-permute-done.24.refs_2_, ...), custom_call_target="tpu_custom_call" | custom-call | flops 12884901888 | bytes 17825792 | tf_op jit(solution)/shard_map/pallas_call | solution.py:146
  181.4 8.7 %shard_map.55 = (f32[2048,512]{1,0:T(8,128)S(1)}, f32[2048,512]{1,0:T(8,128)S(1)}) custom-call(bf16[8,64,2048]{2,1,0:T(8,128)(2,1)} %shard_map.52.refs_0_, bf16[8,64,2048]{2,1,0:T(8,128)(2,1)} %collective-permute-done.27.refs_1_, bf16[8,64,2048]{2,1,0:T(8,128)(2,1)} %collective-permute-done.28.refs_2_, ...), custom_call_target="tpu_custom_call" | custom-call | flops 12884901888 | bytes 17825792 | tf_op jit(solution)/shard_map/pallas_call | solution.py:146
  190.7 4.4 %shard_map.56 = (f32[4096,512]{1,0:T(8,128)}, f32[4096,512]{1,0:T(8,128)}) custom-call(bf16[4,64,2048]{2,1,0:T(8,128)(2,1)S(1)} %collective-permute-done.29.refs_0_, bf16[4,64,2048]{2,1,0:T(8,128)(2,1)S(1)} %collective-permute-done.30.refs_1_, bf16[32,64,1024]{2,1,0:T(8,128)(2,1)S(1)} %get-tuple-element.49.refs_3_.refs_2_, ...), custom_call_target="tpu_custom_call" | custom-call | flops 4294967296 | bytes 19922944 | tf_op jit(solution)/shard_map/pallas_call | solution.py:146
  195.1 4.4 %shard_map.57 = (f32[4096,512]{1,0:T(8,128)}, f32[4096,512]{1,0:T(8,128)}) custom-call(bf16[4,64,2048]{2,1,0:T(8,128)(2,1)S(1)} %collective-permute-done.31.refs_0_, bf16[4,64,2048]{2,1,0:T(8,128)(2,1)S(1)} %collective-permute-done.32.refs_1_, ...), custom_call_target="tpu_custom_call", output_to_operand_aliasing={{0}: (5, {}), {1}: (6, {})} | custom-call | flops 4294967296 | bytes 19922944 | tf_op jit(solution)/shard_map/pallas_call | solution.py:146
  (67 shorter events, 7.0 us)
Async XLA Ops:
  0.6 2.0 copy-start.1
  0.6 2.1 %copy-start = (s32[128]{0:T(128)S(1)}, s32[128]{0:T(128)}, u32[]{:S(2)}) copy-start(s32[128]{0:T(128)} %param.5) | copy-start | bytes 1540
  35.6 4.6 %collective-permute-start.2 = (f32[1,4096]{1,0:T(1,128)S(1)}, f32[1,4096]{1,0:T(1,128)S(1)}, u32[]{:S(2)}, u32[]{:S(2)}) collective-permute-start(f32[1,4096]{1,0:T(1,128)S(1)} %get-tuple-element.35), channel_id=1, source_target_pairs={{0,12},{4,0},{8,4},{12,8},{1,13},{5,1},{9,5},{13,9},{2,14},{6,2},{... | collective-permute-start | bytes 49160 | tf_op jit(solution)/shard_map/ppermute | solution.py:181
  38.5 5.2 %collective-permute-start.1 = (f32[1,4096]{1,0:T(1,128)S(1)}, f32[1,4096]{1,0:T(1,128)S(1)}, u32[]{:S(2)}, u32[]{:S(2)}) collective-permute-start(f32[1,4096]{1,0:T(1,128)S(1)} %get-tuple-element.35), channel_id=1, source_target_pairs={{0,8},{4,12},{8,0},{12,4},{1,9},{5,13},{9,1},{13,5},{2,10},{6,14},... | collective-permute-start | bytes 49160 | tf_op jit(solution)/shard_map/ppermute | solution.py:181
  39.3 4.9 %collective-permute-start = (f32[1,4096]{1,0:T(1,128)S(1)}, f32[1,4096]{1,0:T(1,128)S(1)}, u32[]{:S(2)}, u32[]{:S(2)}) collective-permute-start(f32[1,4096]{1,0:T(1,128)S(1)} %get-tuple-element.35), channel_id=1, source_target_pairs={{0,4},{4,8},{8,12},{12,0},{1,5},{5,9},{9,13},{13,1},{2,6},{6,10},{... | collective-permute-start | bytes 49160 | tf_op jit(solution)/shard_map/ppermute | solution.py:181
  44.3 5.6 %collective-permute-start.5 = (f32[1,4096]{1,0:T(1,128)S(1)}, f32[1,4096]{1,0:T(1,128)S(1)}, u32[]{:S(2)}, u32[]{:S(2)}) collective-permute-start(f32[1,4096]{1,0:T(1,128)S(1)} %add_add_fusion.1), channel_id=1, source_target_pairs={{0,48},{16,0},{32,16},{48,32},{1,49},{17,1},{33,17},{49,33},{2,50}... | collective-permute-start | bytes 49160 | tf_op jit(solution)/shard_map/ppermute | solution.py:181
  48.4 5.2 %collective-permute-start.4 = (f32[1,4096]{1,0:T(1,128)S(1)}, f32[1,4096]{1,0:T(1,128)S(1)}, u32[]{:S(2)}, u32[]{:S(2)}) collective-permute-start(f32[1,4096]{1,0:T(1,128)S(1)} %add_add_fusion.1), channel_id=1, source_target_pairs={{0,32},{16,48},{32,0},{48,16},{1,33},{17,49},{33,1},{49,17},{2,34}... | collective-permute-start | bytes 49160 | tf_op jit(solution)/shard_map/ppermute | solution.py:181
  48.4 5.2 %collective-permute-start.3 = (f32[1,4096]{1,0:T(1,128)S(1)}, f32[1,4096]{1,0:T(1,128)S(1)}, u32[]{:S(2)}, u32[]{:S(2)}) collective-permute-start(f32[1,4096]{1,0:T(1,128)S(1)} %add_add_fusion.1), channel_id=1, source_target_pairs={{0,16},{16,32},{32,48},{48,0},{1,17},{17,33},{33,49},{49,1},{2,18}... | collective-permute-start | bytes 49160 | tf_op jit(solution)/shard_map/ppermute | solution.py:181
  53.7 4.0 %collective-permute-start.6 = (f32[1,4096]{1,0:T(1,128)S(1)}, f32[1,4096]{1,0:T(1,128)S(1)}, u32[]{:S(2)}, u32[]{:S(2)}) collective-permute-start(f32[1,4096]{1,0:T(1,128)S(1)} %add_add_fusion), channel_id=1, source_target_pairs={{0,64},{64,0},{1,65},{65,1},{2,66},{66,2},{3,67},{67,3},{4,68},{68... | collective-permute-start | bytes 49160 | tf_op jit(solution)/shard_map/ppermute | solution.py:181
  58.1 14.2 %collective-permute-start.7 = (bf16[64,4096]{1,0:T(8,128)(2,1)S(1)}, bf16[64,4096]{1,0:T(8,128)(2,1)S(1)}, u32[]{:S(2)}, u32[]{:S(2)}) collective-permute-start(bf16[64,4096]{1,0:T(8,128)(2,1)S(1)} %subtract_convert_fusion), channel_id=1, source_target_pairs={{0,64},{64,0},{1,65},{65,1},{2,66},{66,2},{3,67},{67,3},{4,68},{68... | collective-permute-start | bytes 1572872 | tf_op jit(solution)/shard_map/ppermute | solution.py:181
  61.0 5.0 %collective-permute-start.14 = (bf16[2,64,512]{2,1,0:T(8,128)(2,1)S(1)}, bf16[2,64,512]{2,1,0:T(8,128)(2,1)S(1)}, u32[]{:S(2)}, u32[]{:S(2)}) collective-permute-start(bf16[2,64,512]{2,1,0:T(8,128)(2,1)S(1)} %bitcast.165), channel_id=1, source_target_pairs={{0,12},{4,0},{8,4},{12,8},{1,13},{5,1},{9,5},{13,9},{2,14},{6,2},{... | collective-permute-start | bytes 393224 | tf_op jit(solution)/shard_map/ppermute | solution.py:181
  61.3 6.2 %collective-permute-start.12 = (bf16[2,64,512]{2,1,0:T(8,128)(2,1)S(1)}, bf16[2,64,512]{2,1,0:T(8,128)(2,1)S(1)}, u32[]{:S(2)}, u32[]{:S(2)}) collective-permute-start(bf16[2,64,512]{2,1,0:T(8,128)(2,1)S(1)} %bitcast.164), channel_id=1, source_target_pairs={{0,4},{4,8},{8,12},{12,0},{1,5},{5,9},{9,13},{13,1},{2,6},{6,10},{... | collective-permute-start | bytes 393224 | tf_op jit(solution)/shard_map/ppermute | solution.py:181
  63.1 6.5 %collective-permute-start.13 = (bf16[2,64,512]{2,1,0:T(8,128)(2,1)S(1)}, bf16[2,64,512]{2,1,0:T(8,128)(2,1)S(1)}, u32[]{:S(2)}, u32[]{:S(2)}) collective-permute-start(bf16[2,64,512]{2,1,0:T(8,128)(2,1)S(1)} %bitcast.163), channel_id=1, source_target_pairs={{0,8},{4,12},{8,0},{12,4},{1,9},{5,13},{9,1},{13,5},{2,10},{6,14},... | collective-permute-start | bytes 393224 | tf_op jit(solution)/shard_map/ppermute | solution.py:181
  69.7 11.1 %collective-permute-start.17 = (bf16[4,64,512]{2,1,0:T(8,128)(2,1)S(1)}, bf16[4,64,512]{2,1,0:T(8,128)(2,1)S(1)}, u32[]{:S(2)}, u32[]{:S(2)}) collective-permute-start(bf16[4,64,512]{2,1,0:T(8,128)(2,1)S(1)} %get-tuple-element.67), channel_id=1, source_target_pairs={{1,49},{16,0},{32,16},{49,33},{3,51},{18,2},{34,18},{51,35},{5,53}... | collective-permute-start | bytes 786440 | tf_op jit(solution)/shard_map/ppermute | solution.py:238
  71.0 12.6 %collective-permute-start.16 = (bf16[4,64,512]{2,1,0:T(8,128)(2,1)S(1)}, bf16[4,64,512]{2,1,0:T(8,128)(2,1)S(1)}, u32[]{:S(2)}, u32[]{:S(2)}) collective-permute-start(bf16[4,64,512]{2,1,0:T(8,128)(2,1)S(1)} %get-tuple-element.68), channel_id=1, source_target_pairs={{1,33},{17,49},{32,0},{48,16},{3,35},{19,51},{34,2},{50,18},{5,37}... | collective-permute-start | bytes 786440 | tf_op jit(solution)/shard_map/ppermute | solution.py:238
  72.4 22.5 %collective-permute-start.9 = (bf16[2,64,2048]{2,1,0:T(8,128)(2,1)S(1)}, bf16[2,64,2048]{2,1,0:T(8,128)(2,1)S(1)}, u32[]{:S(2)}, u32[]{:S(2)}) collective-permute-start(bf16[2,64,2048]{2,1,0:T(8,128)(2,1)S(1)} %pad_maximum_fusion.2.own_ref), channel_id=1, source_target_pairs={{0,12},{4,0},{8,4},{12,8},{1,13},{5,1},{9,5},{13,9},{2,14},{6,2},{... | collective-permute-start | bytes 1572872 | tf_op jit(solution)/shard_map/ppermute | solution.py:181
  74.0 20.9 %collective-permute-start.8 = (bf16[2,64,2048]{2,1,0:T(8,128)(2,1)S(1)}, bf16[2,64,2048]{2,1,0:T(8,128)(2,1)S(1)}, u32[]{:S(2)}, u32[]{:S(2)}) collective-permute-start(bf16[2,64,2048]{2,1,0:T(8,128)(2,1)S(1)} %pad_maximum_fusion.2.own_ref), channel_id=1, source_target_pairs={{0,4},{4,8},{8,12},{12,0},{1,5},{5,9},{9,13},{13,1},{2,6},{6,10},{... | collective-permute-start | bytes 1572872 | tf_op jit(solution)/shard_map/ppermute | solution.py:181
  74.6 20.3 %collective-permute-start.11 = (bf16[2,64,2048]{2,1,0:T(8,128)(2,1)S(1)}, bf16[2,64,2048]{2,1,0:T(8,128)(2,1)S(1)}, u32[]{:S(2)}, u32[]{:S(2)}) collective-permute-start(bf16[2,64,2048]{2,1,0:T(8,128)(2,1)S(1)} %pad_maximum_fusion.3.own_ref), channel_id=1, source_target_pairs={{0,48},{16,0},{32,16},{48,32},{1,49},{17,1},{33,17},{49,33},{2,50}... | collective-permute-start | bytes 1572872 | tf_op jit(solution)/shard_map/ppermute | solution.py:181
  80.9 14.1 %collective-permute-start.10 = (bf16[2,64,2048]{2,1,0:T(8,128)(2,1)S(1)}, bf16[2,64,2048]{2,1,0:T(8,128)(2,1)S(1)}, u32[]{:S(2)}, u32[]{:S(2)}) collective-permute-start(bf16[2,64,2048]{2,1,0:T(8,128)(2,1)S(1)} %pad_maximum_fusion.3.own_ref), channel_id=1, source_target_pairs={{0,16},{16,32},{32,48},{48,0},{1,17},{17,33},{33,49},{49,1},{2,18}... | collective-permute-start | bytes 1572872 | tf_op jit(solution)/shard_map/ppermute | solution.py:181
  83.7 11.1 %collective-permute-start.15 = (bf16[4,64,512]{2,1,0:T(8,128)(2,1)S(1)}, bf16[4,64,512]{2,1,0:T(8,128)(2,1)S(1)}, u32[]{:S(2)}, u32[]{:S(2)}) collective-permute-start(bf16[4,64,512]{2,1,0:T(8,128)(2,1)S(1)} %get-tuple-element.69), channel_id=1, source_target_pairs={{0,16},{17,33},{33,49},{48,0},{2,18},{19,35},{35,51},{50,2},{4,20}... | collective-permute-start | bytes 786440 | tf_op jit(solution)/shard_map/ppermute | solution.py:238
  95.0 12.9 %collective-permute-start.22 = (bf16[4,4,64,512]{3,2,1,0:T(8,128)(2,1)S(1)}, bf16[4,4,64,512]{3,2,1,0:T(8,128)(2,1)S(1)}, u32[]{:S(2)}, u32[]{:S(2)}) collective-permute-start(bf16[4,4,64,512]{3,2,1,0:T(8,128)(2,1)S(1)} %pad_maximum_fusion.1), channel_id=1, source_target_pairs={{64,2},{2,64},{80,18},{18,80},{97,35},{35,97},{113,51},{51,113},{6... | collective-permute-start | bytes 3145736 | tf_op jit(solution)/shard_map/ppermute | solution.py:248
  95.8 6.4 %collective-permute-start.21 = (bf16[64,2048]{1,0:T(8,128)(2,1)S(1)}, bf16[64,2048]{1,0:T(8,128)(2,1)S(1)}, u32[]{:S(2)}, u32[]{:S(2)}) collective-permute-start(bf16[64,2048]{1,0:T(8,128)(2,1)S(1)} %slice_bitcast_fusion.4), channel_id=1, source_target_pairs={{0,48},{16,0},{32,16},{48,32},{1,49},{17,1},{33,17},{49,33},{2,50}... | collective-permute-start | bytes 786440 | tf_op jit(solution)/shard_map/ppermute | solution.py:181
  95.9 7.7 %collective-permute-start.20 = (bf16[64,2048]{1,0:T(8,128)(2,1)S(1)}, bf16[64,2048]{1,0:T(8,128)(2,1)S(1)}, u32[]{:S(2)}, u32[]{:S(2)}) collective-permute-start(bf16[64,2048]{1,0:T(8,128)(2,1)S(1)} %slice_bitcast_fusion.5), channel_id=1, source_target_pairs={{0,16},{16,32},{32,48},{48,0},{1,17},{17,33},{33,49},{49,1},{2,18}... | collective-permute-start | bytes 786440 | tf_op jit(solution)/shard_map/ppermute | solution.py:181
  97.9 6.4 %collective-permute-start.19 = (bf16[64,2048]{1,0:T(8,128)(2,1)S(1)}, bf16[64,2048]{1,0:T(8,128)(2,1)S(1)}, u32[]{:S(2)}, u32[]{:S(2)}) collective-permute-start(bf16[64,2048]{1,0:T(8,128)(2,1)S(1)} %slice_bitcast_fusion.6), channel_id=1, source_target_pairs={{0,12},{4,0},{8,4},{12,8},{1,13},{5,1},{9,5},{13,9},{2,14},{6,2},{... | collective-permute-start | bytes 786440 | tf_op jit(solution)/shard_map/ppermute | solution.py:181
  100.3 7.6 %collective-permute-start.18 = (bf16[64,2048]{1,0:T(8,128)(2,1)S(1)}, bf16[64,2048]{1,0:T(8,128)(2,1)S(1)}, u32[]{:S(2)}, u32[]{:S(2)}) collective-permute-start(bf16[64,2048]{1,0:T(8,128)(2,1)S(1)} %slice_bitcast_fusion.7), channel_id=1, source_target_pairs={{0,4},{4,8},{8,12},{12,0},{1,5},{5,9},{9,13},{13,1},{2,6},{6,10},{... | collective-permute-start | bytes 786440 | tf_op jit(solution)/shard_map/ppermute | solution.py:181
  110.8 20.2 %collective-permute-start.25 = (bf16[4,4,64,512]{3,2,1,0:T(8,128)(2,1)S(1)}, bf16[4,4,64,512]{3,2,1,0:T(8,128)(2,1)S(1)}, u32[]{:S(2)}, u32[]{:S(2)}) collective-permute-start(bf16[4,4,64,512]{3,2,1,0:T(8,128)(2,1)S(1)} %pad_maximum_fusion.1), channel_id=1, source_target_pairs={{0,2},{64,0},{2,66},{66,64},{16,18},{80,16},{18,82},{82,80},{33,35... | collective-permute-start | bytes 3145736 | tf_op jit(solution)/shard_map/ppermute | solution.py:248
  118.7 38.9 %collective-permute-start.24 = (bf16[8,64,2048]{2,1,0:T(8,128)(2,1)}, bf16[8,64,2048]{2,1,0:T(8,128)(2,1)}, u32[]{:S(2)}, u32[]{:S(2)}) collective-permute-start(bf16[8,64,2048]{2,1,0:T(8,128)(2,1)} %shard_map.51.refs_0_), channel_id=1, source_target_pairs={{0,48},{16,0},{32,16},{48,32},{1,49},{17,1},{33,17},{49,33},{2,50}... | collective-permute-start | bytes 6291464 | tf_op jit(solution)/shard_map/ppermute | solution.py:181
  118.8 43.9 %collective-permute-start.23 = (bf16[8,64,2048]{2,1,0:T(8,128)(2,1)}, bf16[8,64,2048]{2,1,0:T(8,128)(2,1)}, u32[]{:S(2)}, u32[]{:S(2)}) collective-permute-start(bf16[8,64,2048]{2,1,0:T(8,128)(2,1)} %shard_map.51.refs_0_), channel_id=1, source_target_pairs={{0,16},{16,32},{32,48},{48,0},{1,17},{17,33},{33,49},{49,1},{2,18}... | collective-permute-start | bytes 6291464 | tf_op jit(solution)/shard_map/ppermute | solution.py:181
  120.8 43.4 %collective-permute-start.28 = (bf16[8,64,2048]{2,1,0:T(8,128)(2,1)}, bf16[8,64,2048]{2,1,0:T(8,128)(2,1)}, u32[]{:S(2)}, u32[]{:S(2)}) collective-permute-start(bf16[8,64,2048]{2,1,0:T(8,128)(2,1)} %shard_map.52.refs_0_), channel_id=1, source_target_pairs={{0,12},{4,0},{8,4},{12,8},{1,13},{5,1},{9,5},{13,9},{2,14},{6,2},{... | collective-permute-start | bytes 6291464 | tf_op jit(solution)/shard_map/ppermute | solution.py:181
  123.2 44.8 %collective-permute-start.27 = (bf16[8,64,2048]{2,1,0:T(8,128)(2,1)}, bf16[8,64,2048]{2,1,0:T(8,128)(2,1)}, u32[]{:S(2)}, u32[]{:S(2)}) collective-permute-start(bf16[8,64,2048]{2,1,0:T(8,128)(2,1)} %shard_map.52.refs_0_), channel_id=1, source_target_pairs={{0,4},{4,8},{8,12},{12,0},{1,5},{5,9},{9,13},{13,1},{2,6},{6,10},{... | collective-permute-start | bytes 6291464 | tf_op jit(solution)/shard_map/ppermute | solution.py:181
  131.2 38.3 %collective-permute-start.26 = (bf16[2,4,4,64,512]{4,3,2,1,0:T(8,128)(2,1)S(1)}, bf16[2,4,4,64,512]{4,3,2,1,0:T(8,128)(2,1)}, u32[]{:S(2)}, u32[]{:S(2)}) collective-permute-start(bf16[2,4,4,64,512]{4,3,2,1,0:T(8,128)(2,1)S(1)} %pad_maximum_fusion), channel_id=1, source_target_pairs={{0,1},{16,17},{33,32},{49,48},{2,3},{18,19},{35,34},{51,50},{4,5},... | collective-permute-start | bytes 6291464 | tf_op jit(solution)/shard_map/ppermute | solution.py:254
  159.0 31.2 %collective-permute-start.30 = (bf16[4,64,2048]{2,1,0:T(8,128)(2,1)S(1)}, bf16[4,64,2048]{2,1,0:T(8,128)(2,1)S(1)}, u32[]{:S(2)}, u32[]{:S(2)}) collective-permute-start(bf16[4,64,2048]{2,1,0:T(8,128)(2,1)S(1)} %slice.53), channel_id=1, source_target_pairs={{0,48},{16,0},{32,16},{48,32},{1,49},{17,1},{33,17},{49,33},{2,50}... | collective-permute-start | bytes 3145736 | tf_op jit(solution)/shard_map/ppermute | solution.py:181
  164.1 26.1 %collective-permute-start.29 = (bf16[4,64,2048]{2,1,0:T(8,128)(2,1)S(1)}, bf16[4,64,2048]{2,1,0:T(8,128)(2,1)S(1)}, u32[]{:S(2)}, u32[]{:S(2)}) collective-permute-start(bf16[4,64,2048]{2,1,0:T(8,128)(2,1)S(1)} %slice.52), channel_id=1, source_target_pairs={{0,16},{16,32},{32,48},{48,0},{1,17},{17,33},{33,49},{49,1},{2,18}... | collective-permute-start | bytes 3145736 | tf_op jit(solution)/shard_map/ppermute | solution.py:181
  165.5 24.7 %collective-permute-start.32 = (bf16[4,64,2048]{2,1,0:T(8,128)(2,1)S(1)}, bf16[4,64,2048]{2,1,0:T(8,128)(2,1)S(1)}, u32[]{:S(2)}, u32[]{:S(2)}) collective-permute-start(bf16[4,64,2048]{2,1,0:T(8,128)(2,1)S(1)} %slice.55), channel_id=1, source_target_pairs={{0,12},{4,0},{8,4},{12,8},{1,13},{5,1},{9,5},{13,9},{2,14},{6,2},{... | collective-permute-start | bytes 3145736 | tf_op jit(solution)/shard_map/ppermute | solution.py:181
  169.4 21.3 %collective-permute-start.31 = (bf16[4,64,2048]{2,1,0:T(8,128)(2,1)S(1)}, bf16[4,64,2048]{2,1,0:T(8,128)(2,1)S(1)}, u32[]{:S(2)}, u32[]{:S(2)}) collective-permute-start(bf16[4,64,2048]{2,1,0:T(8,128)(2,1)S(1)} %slice.54), channel_id=1, source_target_pairs={{0,4},{4,8},{8,12},{12,0},{1,5},{5,9},{9,13},{13,1},{2,6},{6,10},{... | collective-permute-start | bytes 3145736 | tf_op jit(solution)/shard_map/ppermute | solution.py:181
